TPU v7x, 128 devices: a whole 4x4x4 slice. The times are simulated.
128 devices in a mesh: rep: 2 (over y_lo), tx: 8 (over x, y_hi), ty: 8 (over z, core).
Axes of the slice: x: 4, y: 4 (y_hi: 2, y_lo: 2; y = y_hi * 2 + y_lo), z: 4, core: 2. Of those that a mesh axis runs over, the one named last changes fastest.
Arguments:
- density: bfloat16 [2, 256, 512, 128], P('rep', 'tx', 'ty'), may hold values from -6 to 6
- kernel_one: bfloat16 [16, 4, 3, 3, 3], replicated, may hold values from -0.625 to 0.625
- kernel_two: bfloat16 [16, 16, 3, 3, 3], replicated, may hold values from -0.3125 to 0.3125
- cotangent: bfloat16 [2, 128, 256, 256], P('rep', 'tx', 'ty'), may hold values from -30 to 30
Outputs:
- features: bfloat16 [2, 128, 256, 256], P('rep', 'tx', 'ty')
- grad_one: float32 [16, 4, 3, 3, 3], replicated
- grad_two: float32 [16, 16, 3, 3, 3], replicated
All inputs are finite; a program needn't handle non-finite values.
Results may differ from a plain program's by a relative error of at most 0.015.
Values may be sent and summed in bfloat16 or wider, within the bound.
No kernel may reach another device: no remote copies, remote signals or barrier semaphores. Data moves between devices by JAX's collectives and lax.ppermute only.
A program may use at most 320 MiB of HBM per device.

v0:
```python
import jax
import jax.numpy as jnp
from jax import lax
from jax.sharding import PartitionSpec as P

CIN = 4
CH = 16


leak_slope = 0.3


def extended(value, sides, width):
    for axis, dim in sides:
        peers, length = (lax.axis_size(axis), value.shape[dim])
        up = [(i, (i + 1) % peers) for i in range(peers)]
        down = [(j, i) for i, j in up]
        last = lax.slice_in_dim(value, length - width, length, axis=dim)
        initial = lax.slice_in_dim(value, 0, width, axis=dim)
        before = lax.ppermute(last, axis, up)
        after = lax.ppermute(initial, axis, down)
        value = jnp.concatenate([before, value, after], axis=dim)
    return value


def convolve(lhs, rhs, specs):
    return lax.conv_general_dilated(
        lhs, rhs, (1, 1, 1), "VALID", dimension_numbers=specs, preferred_element_type=jnp.float32
    )


def depth_pad(field):
    return jnp.pad(field, ((0, 0), (0, 0), (1, 1), (0, 0), (0, 0)))


def pooling(field):
    s, c, d, x, y = field.shape
    blocks = field.astype(jnp.float32).reshape(s, c, d // 2, 2, x // 2, 2, y // 2, 2)
    return jnp.mean(blocks, axis=(3, 5, 7))


def upsample(field):
    s, c, d, x, y = field.shape
    grown = jnp.broadcast_to(field[:, :, :, None, :, None, :, None], (s, c, d, 2, x, 2, y, 2))
    return grown.reshape(s, c, 2 * d, 2 * x, 2 * y)


def unpack(field, channels):
    s, x, y, merged = field.shape
    return jnp.transpose(field.reshape(s, x, y, channels, merged // channels), (0, 3, 4, 1, 2))


def packing(field):
    s, c, d, x, y = field.shape
    return jnp.transpose(field, (0, 3, 4, 1, 2)).reshape(s, x, y, c * d)


def on_device(density, kernel_one, kernel_two, cotangent):
    forward = ("NCDHW", "OIDHW", "NCDHW")
    weight_form = ("CNDHW", "IODHW", "CNDHW")
    backward = ("NCDHW", "IODHW", "NCDHW")
    fine_width = 1
    grads = unpack(cotangent, CH)
    wide = unpack(extended(density, (("tx", 1), ("ty", 2)), fine_width), CIN)
    grad_rim = unpack(extended(cotangent, (("tx", 1), ("ty", 2)), 1), CH)
    padded = depth_pad(wide)
    pre = convolve(padded, kernel_one, forward)
    act = jnp.where(pre > 0, pre, leak_slope * pre).astype(jnp.bfloat16)
    pooled = pooling(act).astype(jnp.bfloat16)
    pooled_rimmed = extended(packing(pooled), (("tx", 1), ("ty", 2)), 1)
    pooled_pad = depth_pad(unpack(pooled_rimmed, CH))
    features = packing(convolve(pooled_pad, kernel_two, forward).astype(jnp.bfloat16))
    slab_two = convolve(pooled_pad, grads, weight_form)
    grad_pad = depth_pad(grad_rim)
    flipped = kernel_two[:, :, ::-1, ::-1, ::-1]
    back_pooled = convolve(grad_pad, flipped, backward).astype(jnp.bfloat16)
    slope = jnp.where(pre > 0, 1.0, leak_slope).astype(jnp.float32)
    back_pre = (upsample(back_pooled.astype(jnp.float32)) * 0.125 * slope).astype(jnp.bfloat16)
    slab_one = convolve(padded, back_pre, weight_form)
    replicas = lax.axis_size("rep")
    tile_one, tile_two = lax.psum((slab_one, slab_two), ("tx", "ty"))
    total_one, total_two = (
        lax.psum(tile_one.astype(jnp.bfloat16), "rep").astype(jnp.float32),
        lax.psum(tile_two.astype(jnp.bfloat16), "rep").astype(jnp.float32),
    )
    return (features, total_one / replicas, total_two / replicas)


def solution(mesh):
    in_specs = (P("rep", "tx", "ty", None), P(), P(), P("rep", "tx", "ty", None))
    out_specs = (P("rep", "tx", "ty", None), P(), P())
    return jax.shard_map(
        on_device, mesh=mesh, in_specs=in_specs, out_specs=out_specs, check_vma=False
    )
```

profile of v0, /device:TPU:0, one launch (start us, length us, event | category | flops | bytes accessed | tf_op | source)
XLA Modules:
  0.0 1262.0 jit_solution(5296581193335295249)
XLA Ops:
  13.6 7.6 copy.227
  44.7 15.7 %copy.199 = bf16[34,1,8,11,4,32]{2,4,3,0,5,1:T(4,128)(2,1)} copy(bf16[34,1,8,11,4,32]{0,5,4,3,2,1:T(8,128)(2,1)S(1)} %fusion.23) | data formatting | bytes 1531904 | tf_op jit(solution)/shard_map/conv_general_dilated | solution.py:27
  60.4 79.3 %fusion.4 = f32[32,32,8,9,16]{4,2,3,1,0:T(8,128)} fusion(bf16[16,4,3,3,3]{0,1,4,3,2:T(4,128)(2,1)S(1)} %copy-done.13, bf16[34,1,8,11,4,32]{2,4,3,0,5,1:T(4,128)(2,1)} %copy.199), kind=kOutput, calls=%fused_computation.8 | convolution fusion | flops 249495552 | bytes 5488000 | tf_op jit(solution)/shard_map/conv_general_dilated | solution.py:27
  139.7 27.7 %copy.200 = f32[32,32,8,9,16]{1,4,3,2,0:T(8,128)} copy(f32[32,32,8,9,16]{4,2,3,1,0:T(8,128)} %fusion.4) | data formatting | bytes 9437184 | tf_op jit(solution)/shard_map/conv_general_dilated | solution.py:27
  167.4 17.8 %compare_select_fusion = (f32[32,32,8,9,16]{1,4,3,2,0:T(8,128)}, bf16[32,32,8,9,16]{1,4,3,2,0:T(8,128)(2,1)}) fusion(f32[32,32,8,9,16]{1,4,3,2,0:T(8,128)} %copy.200, pred[8,9]{1,0:T(8,128)(4,1)S(1)} %copy-done.12), kind=kLoop, calls=%fused_computation.5 | loop fusion | flops 7077888 | bytes 11796552 | tf_op jit(solution)/shard_map/jit(_where)/select_n | solution.py:77
  185.2 11.3 convert_bitcast_fusion
  196.5 30.0 %copy.201 = f32[1,16,32,32,64]{1,4,3,2,0:T(8,128)} copy(f32[1,16,32,32,64]{3,1,4,2,0:T(8,128)} %convert_bitcast_fusion) | data formatting | bytes 8388608 | tf_op jit(solution)/shard_map/reshape | solution.py:38
  226.5 25.2 %reduce_sum.9 = f32[16,16,16,32]{0,3,2,1:T(8,128)} reduce(f32[16,16,2,16,2,32,2]{0,6,5,4,3,2,1:T(2,128)} %bitcast.52, f32[]{:T(128)} %constant.5.clone.1), dimensions={2,4,6}, to_apply=%region_0.1 | reduce | flops 917504 | bytes 4718596 | tf_op jit(solution)/shard_map/reduce_sum | solution.py:39
  255.6 11.7 slice.71
  273.0 30.0 %copy.232 = f32[32,32,1,64,16]{4,3,1,0,2:T(8,128)} copy(f32[32,32,1,64,16]{1,4,3,0,2:T(8,128)} %slice.71) | data formatting | bytes 8388608
  302.9 65.3 %copy.223 = bf16[1,34,66,4,32]{3,0,2,1,4:T(2,128)(2,1)} copy(bf16[1,34,66,4,32]{2,4,3,1,0:T(8,128)(2,1)S(1)} %bitcast.67) | data formatting | bytes 1148928 | tf_op jit(solution)/shard_map/reshape | solution.py:50
  375.3 6.2 copy.234
  383.8 5.9 copy.219
  391.4 7.8 convert_multiply_fusion
  401.7 16.6 %broadcast_in_dim.12 = f32[16,16,2,16,2,32,2]{0,6,5,4,3,2,1:T(2,128)} broadcast(f32[16,16,16,32]{0,3,2,1:T(8,128)S(1)} %copy.221), dimensions={0,1,3,5} | broadcast | bytes 4718592 | tf_op jit(solution)/shard_map/broadcast_in_dim | solution.py:44
  418.3 27.8 %fusion = bf16[1,16,32,32,64]{1,4,3,2,0:T(8,128)(2,1)} fusion(f32[1,16,32,32,64]{1,4,3,2,0:T(8,128)} %bitcast.53, f32[32,32,1,64,16]{4,3,1,0,2:T(8,128)} %copy.232), kind=kLoop, calls=%fused_computation.1 | loop fusion | flops 2097152 | bytes 10485760 | tf_op jit(solution)/shard_map/convert_element_type | solution.py:78
  451.7 374.3 %fusion.1 = f32[16,4,3,3,3]{0,1,4,3,2:T(4,128)} fusion(bf16[1,34,66,4,32]{3,0,2,1,4:T(2,128)(2,1)} %copy.223, bf16[1,16,32,32,64]{1,4,3,2,0:T(8,128)(2,1)} %fusion), kind=kOutput, calls=%fused_computation.2 | convolution fusion | flops 221773824 | bytes 2678528 | tf_op jit(solution)/shard_map/conv_general_dilated | solution.py:27
  832.1 5.2 copy.207
  839.4 7.2 copy.209
  848.3 7.6 select_convert_fusion.1
  862.0 9.7 copy.226
  871.7 48.2 %fusion.43 = f32[16,16,3,3,3]{0,1,4,3,2:T(8,128)S(1)} fusion(bf16[1,18,34,16,16]{3,0,2,1,4:T(2,128)(2,1)} %copy.226, bf16[1,16,32,16,16]{3,0,2,1,4:T(2,128)(2,1)} %copy.227), kind=kOutput, calls=%fused_computation.59 | convolution fusion | flops 108527616 | bytes 603136 | tf_op jit(solution)/shard_map/conv_general_dilated | solution.py:27
  920.0 331.5 %all-reduce = (bf16[16,4,3,3,3]{0,1,4,3,2:T(4,128)(2,1)S(1)}, bf16[16,16,3,3,3]{0,1,4,3,2:T(8,128)(2,1)S(1)}) all-reduce(f32[16,4,3,3,3]{0,1,4,3,2:T(4,128)S(1)} %copy-done.11, f32[16,16,3,3,3]{0,1,4,3,2:T(8,128)S(1)} %fusion.43), channel_id=1, replica_groups=mesh['rep'=2,'tx'=8,'ty'=8] {'tx','ty'}, use_global_device_ids=true, to_apply=%region_1.2 | all-reduce | flops 8640 | bytes 51840 | tf_op jit(solution)/shard_map/psum | solution.py:81
  1251.5 8.8 all-reduce.1
  (105 shorter events, 82.3 us)
Async XLA Ops:
  0.6 390.7 %copy-start = (bf16[16,16,3,3,3]{1,0,4,3,2:T(8,128)(2,1)S(1)}, bf16[16,16,3,3,3]{1,0,4,3,2:T(8,128)(2,1)}, u32[]{:S(2)}) copy-start(bf16[16,16,3,3,3]{1,0,4,3,2:T(8,128)(2,1)} %param.6) | copy-start | bytes 41476
  2.2 19.0 %collective-permute-start = (bf16[1,1,64,128]{2,3,1,0:T(8,128)(2,1)S(1)}, bf16[1,1,64,128]{2,3,1,0:T(8,128)(2,1)S(1)}, u32[]{:S(2)}, u32[]{:S(2)}) collective-permute-start(bf16[1,1,64,128]{2,3,1,0:T(8,128)(2,1)S(1)} %get-tuple-element.36), channel_id=1, source_target_pairs={{0,8},{8,16},{16,24},{24,32},{32,40},{40,48},{48,56},{56,0},{1,9},... | collective-permute-start | bytes 49160 | tf_op jit(solution)/shard_map/ppermute | solution.py:20
  5.6 15.7 %collective-permute-start.1 = (bf16[1,1,64,128]{2,3,1,0:T(8,128)(2,1)S(1)}, bf16[1,1,64,128]{2,3,1,0:T(8,128)(2,1)S(1)}, u32[]{:S(2)}, u32[]{:S(2)}) collective-permute-start(bf16[1,1,64,128]{2,3,1,0:T(8,128)(2,1)S(1)} %get-tuple-element.37), channel_id=1, source_target_pairs={{8,0},{16,8},{24,16},{32,24},{40,32},{48,40},{56,48},{0,56},{9,1},... | collective-permute-start | bytes 49160 | tf_op jit(solution)/shard_map/ppermute | solution.py:21
  8.7 17.8 %collective-permute-start.9 = (bf16[1,1,32,256]{3,2,1,0:T(8,128)(2,1)S(1)}, bf16[1,1,32,256]{3,2,1,0:T(8,128)(2,1)S(1)}, u32[]{:S(2)}, u32[]{:S(2)}) collective-permute-start(bf16[1,1,32,256]{3,2,1,0:T(8,128)(2,1)S(1)} %get-tuple-element.40), channel_id=1, source_target_pairs={{8,0},{16,8},{24,16},{32,24},{40,32},{48,40},{56,48},{0,56},{9,1},... | collective-permute-start | bytes 49160 | tf_op jit(solution)/shard_map/ppermute | solution.py:21
  12.0 10.0 collective-permute-start.8
  23.9 11.3 collective-permute-start.3
  26.4 8.1 collective-permute-start.2
  31.6 338.1 %collective-permute-start.11 = (bf16[1,18,1,256]{3,1,2,0:T(8,128)(2,1)}, bf16[1,18,1,256]{3,1,2,0:T(8,128)(2,1)}, u32[]{:S(2)}, u32[]{:S(2)}) collective-permute-start(bf16[1,18,1,256]{3,1,2,0:T(8,128)(2,1)} %copy.231), channel_id=1, source_target_pairs={{1,0},{2,1},{3,2},{4,3},{5,4},{6,5},{7,6},{0,7},{9,8},{10,9},{11,1... | collective-permute-start | bytes 27656 | tf_op jit(solution)/shard_map/ppermute | solution.py:21
  34.5 333.7 %collective-permute-start.10 = (bf16[1,18,1,256]{3,1,2,0:T(8,128)(2,1)}, bf16[1,18,1,256]{3,1,2,0:T(8,128)(2,1)}, u32[]{:S(2)}, u32[]{:S(2)}) collective-permute-start(bf16[1,18,1,256]{3,1,2,0:T(8,128)(2,1)} %copy.230), channel_id=1, source_target_pairs={{0,1},{1,2},{2,3},{3,4},{4,5},{5,6},{6,7},{7,0},{8,9},{9,10},{10,1... | collective-permute-start | bytes 27656 | tf_op jit(solution)/shard_map/ppermute | solution.py:20
  39.0 4.8 copy-start.4
  44.7 15.7 %copy-start.13 = (bf16[16,4,3,3,3]{0,1,4,3,2:T(4,128)(2,1)S(1)}, bf16[16,4,3,3,3]{0,1,4,3,2:T(4,128)(2,1)}, u32[]{:S(2)}) copy-start(bf16[16,4,3,3,3]{0,1,4,3,2:T(4,128)(2,1)} %param.5) | copy-start | bytes 10372
  139.7 27.7 %copy-start.12 = (pred[8,9]{1,0:T(8,128)(4,1)S(1)}, pred[8,9]{1,0:T(8,128)(4,1)}, u32[]{:S(2)}) copy-start(pred[8,9]{1,0:T(8,128)(4,1)} %constant.34) | copy-start | bytes 220
  255.6 11.7 copy-start.1
  267.3 178.8 %collective-permute-start.4 = (bf16[1,1,32,256]{2,3,1,0:T(8,128)(2,1)S(1)}, bf16[1,1,32,256]{2,3,1,0:T(8,128)(2,1)S(1)}, u32[]{:S(2)}, u32[]{:S(2)}) collective-permute-start(bf16[1,1,32,256]{2,3,1,0:T(8,128)(2,1)S(1)} %get-tuple-element.34), channel_id=1, source_target_pairs={{0,8},{8,16},{16,24},{24,32},{32,40},{40,48},{48,56},{56,0},{1,9},... | collective-permute-start | bytes 49160 | tf_op jit(solution)/shard_map/ppermute | solution.py:20
  269.2 33.7 %copy-start.5 = (bf16[1,34,66,128]{2,3,1,0:T(8,128)(2,1)S(1)}, bf16[1,34,66,128]{2,3,1,0:T(8,128)(2,1)}, u32[]{:S(2)}) copy-start(bf16[1,34,66,128]{2,3,1,0:T(8,128)(2,1)} %copy-done.4) | copy-start | bytes 1723396
  269.2 176.9 %collective-permute-start.5 = (bf16[1,1,32,256]{2,3,1,0:T(8,128)(2,1)S(1)}, bf16[1,1,32,256]{2,3,1,0:T(8,128)(2,1)S(1)}, u32[]{:S(2)}, u32[]{:S(2)}) collective-permute-start(bf16[1,1,32,256]{2,3,1,0:T(8,128)(2,1)S(1)} %get-tuple-element.35), channel_id=1, source_target_pairs={{8,0},{16,8},{24,16},{32,24},{40,32},{48,40},{56,48},{0,56},{9,1},... | collective-permute-start | bytes 49160 | tf_op jit(solution)/shard_map/ppermute | solution.py:21
  368.2 3.6 copy-start.6
  383.8 7.6 copy-start.14
  418.3 27.8 %copy-start.2 = (bf16[1,16,32,16,16]{2,4,3,1,0:T(8,128)(2,1)S(1)}, bf16[1,16,32,16,16]{2,4,3,1,0:T(8,128)(2,1)}, u32[]{:S(2)}) copy-start(bf16[1,16,32,16,16]{2,4,3,1,0:T(8,128)(2,1)} %copy-done.1) | copy-start | bytes 786436
  449.3 378.2 %collective-permute-start.7 = (bf16[1,18,1,256]{3,1,2,0:T(8,128)(2,1)}, bf16[1,18,1,256]{3,1,2,0:T(8,128)(2,1)}, u32[]{:S(2)}, u32[]{:S(2)}) collective-permute-start(bf16[1,18,1,256]{3,1,2,0:T(8,128)(2,1)} %copy.204), channel_id=1, source_target_pairs={{1,0},{2,1},{3,2},{4,3},{5,4},{6,5},{7,6},{0,7},{9,8},{10,9},{11,1... | collective-permute-start | bytes 27656 | tf_op jit(solution)/shard_map/ppermute | solution.py:21
  451.7 374.3 %collective-permute-start.6 = (bf16[1,18,1,256]{3,1,2,0:T(8,128)(2,1)}, bf16[1,18,1,256]{3,1,2,0:T(8,128)(2,1)}, u32[]{:S(2)}, u32[]{:S(2)}) collective-permute-start(bf16[1,18,1,256]{3,1,2,0:T(8,128)(2,1)} %copy.203), channel_id=1, source_target_pairs={{0,1},{1,2},{2,3},{3,4},{4,5},{5,6},{6,7},{7,0},{8,9},{9,10},{10,1... | collective-permute-start | bytes 27656 | tf_op jit(solution)/shard_map/ppermute | solution.py:20
  826.0 3.7 copy-start.3
  839.4 8.9 copy-start.15
  871.7 48.2 %copy-start.11 = (f32[16,4,3,3,3]{0,1,4,3,2:T(4,128)S(1)}, f32[16,4,3,3,3]{0,1,4,3,2:T(4,128)}, u32[]{:S(2)}) copy-start(f32[16,4,3,3,3]{0,1,4,3,2:T(4,128)} %fusion.1) | copy-start | bytes 20740
  (4 other events, 3.3 us)
where the time goes:
time: 1270 us; the launch traced here: 1260 us
  matrix products  517 us (41%)
  blocking collectives  340 us (27%)
  local copies, waits for them, and re-layouts  285 us (22%)
  other arithmetic  95 us (7%)
  starting transfers between devices  22.8 us (2%)
    conv_general_dilated x5, matrix products, convolve(): lax.conv_general_dilated(lhs, rhs, (1, 1, 1), 'VALID', dimension_numbers=...  517 us
    psum x1, blocking collectives, on_device(): tile_one, tile_two = lax.psum((slab_one, slab_two), ('tx', 'ty'))  332 us
    reshape x7, local copies, waits for them, and re-layouts, unpack(): field.reshape(s, x, y, channels, merged // channels)  92.8 us
    conv_general_dilated x7, local copies, waits for them, and re-layouts, convolve(): lax.conv_general_dilated(lhs, rhs, (1, 1, 1), 'VALID', dimension_numbers=...  59.8 us
    unnamed x43, local copies, waits for them, and re-layouts  48.5 us
    reshape x1, local copies, waits for them, and re-layouts, pooling(): field.astype(jnp.float32).reshape(s, c, d // 2, 2, x // 2, 2, y // 2, 2)  30 us
    convert_element_type x1, other arithmetic, on_device(): (upsample(back_pooled.astype(jnp.float32)) * 0.125 * slope).astype(jnp.bf...  27.8 us
  transfers between devices with their start and end apart: 12, of which 0 were waited for; matrix products, arithmetic and copies ran while one was open for 63% of the time, Pallas kernels for 0%

commit v1 on v0

v1 whole, which is shorter than its diff:
```python
import functools

import jax
import jax.numpy as jnp
from jax import lax
from jax.experimental import pallas as pl
from jax.experimental.pallas import tpu as pltpu
from jax.sharding import PartitionSpec as P

CIN = 4
CH = 16
LEAK = 0.3
F32 = jnp.float32
BF16 = jnp.bfloat16
NXT = 32
NYT = 64
HX = NXT // 2
HY = NYT // 2
DROW = 80
CROW = 48
VMEM_LIMIT = 48 * 1024 * 1024


def dot_nt(lhs, rhs):
    return lax.dot_general(lhs, rhs, (((1,), (1,)), ((), ())), preferred_element_type=F32)


def dot_nn(lhs, rhs):
    return lax.dot_general(lhs, rhs, (((1,), (0,)), ((), ())), preferred_element_type=F32)


def iota(shape, dim):
    return lax.broadcasted_iota(jnp.int32, shape, dim)


def pack_y_kernel(d_ref, c_ref, up_ref, down_ref, ds, cs):
    for out, low, row, crow in ((down_ref, True, 0, 0), (up_ref, False, 13, 15)):
        at, cat = (0, 0) if low else (NYT - 16, HY - 16)
        ds[...] = d_ref[:, at : at + 16, :].astype(F32).reshape(NXT * 16, 128)
        for half in range(2):
            part = c_ref[:, cat : cat + 16, half * 128 : half * 128 + 128]
            cs[half] = part.astype(F32).reshape(HX * 16, 128)
        for k in range(3):
            out[k * 32 : k * 32 + 32, :] = ds[pl.ds(row + k, 32, stride=16), :].astype(BF16)
        for half in range(2):
            edge = cs[half, pl.ds(crow, 16, stride=16), :]
            out[96 + half * 16 : 112 + half * 16, :] = edge.astype(BF16)


def pack_x_kernel(d_ref, c_ref, lo_ref, hi_ref, up_ref, down_ref, ls, hs, ms):
    ls[...] = lo_ref[...].astype(F32)
    hs[...] = hi_ref[...].astype(F32)
    for out, x, cx in ((down_ref, 0, 0), (up_ref, NXT - 3, HX - 1)):
        out[0:192, :] = d_ref[x : x + 3, :, :].reshape(192, 128)
        out[192:224, :] = c_ref[cx, :, 0:128]
        out[224:256, :] = c_ref[cx, :, 128:256]
        for side, src in enumerate((ls, hs)):
            for k in range(3):
                ms[side * 9 + 3 * k : side * 9 + 3 * k + 3, :] = src[k * 32 + x : k * 32 + x + 3, :]
            for half in range(2):
                at = 18 + side * 2 + half
                ms[at : at + 1, :] = src[96 + half * 16 + cx : 97 + half * 16 + cx, :]
        ms[22:32, :] = jnp.zeros((10, 128), F32)
        out[256:288, :] = ms[...].astype(BF16)


def weights_kernel(k1_ref, k2_ref, w1_ref, wb_ref, w2_ref, s1, so, c1, c2):
    for t in range(27):
        s1[4 * t : 4 * t + 4, 0:CH] = k1_ref[t].astype(F32)
    s1[108:128, :] = jnp.zeros((20, 128), F32)
    k1t = s1[...].T[0:CH].astype(BF16)
    so[...] = jnp.zeros(so.shape, F32)
    for t in range(27):
        g, j = t // 8, t % 8
        so[g * 32 : g * 32 + 16, j * 16 : j * 16 + 16] = k2_ref[t].astype(F32)
    for g in range(4):
        for j in range(8):
            if g * 8 + j < 27:
                s1[j * 16 : j * 16 + 16, 0:CH] = k2_ref[g * 8 + j].astype(F32)
        so[g * 32 + 16 : g * 32 + 32, :] = s1[...].T[0:CH]
    rep1 = (iota((128, 27 * 128), 0) == iota((128, 27 * 128), 1) // 32).astype(BF16)
    c1[...] = dot_nn(k1t, rep1)
    rep2 = (iota((128, 2048), 0) == iota((128, 2048), 1) // 16).astype(BF16)
    c2[...] = dot_nn(so[...].astype(BF16), rep2)

    zero = jnp.zeros((), F32)
    for pd in range(2):
        gap = iota((1, 16, 128), 2) % 32 - 2 * iota((1, 16, 128), 1) - pd
        for kx in range(3):
            for ky in range(3):
                acc = jnp.zeros((16, 16, 128), F32)
                for kd in range(3):
                    t = kd * 9 + kx * 3 + ky
                    row = c1[:, t * 128 : t * 128 + 128][:, None, :]
                    acc = jnp.where(gap == kd - 1, row, acc)
                at = (kx * 3 + ky) * 128
                w1_ref[pd * 256 : pd * 256 + 256, at : at + 128] = acc.reshape(256, 128).astype(BF16)
    gap = iota((1, 16, 256), 2) % 16 - iota((1, 16, 256), 1)
    for kx in range(3):
        for ky in range(3):
            fwd = jnp.zeros((16, 16, 256), F32)
            bwd = jnp.zeros((16, 16, 256), F32)
            for kd in range(3):
                t = kd * 9 + kx * 3 + ky
                g, j = t // 8, t % 8
                row = c2[g * 32 : g * 32 + 16, j * 256 : j * 256 + 256][:, None, :]
                fwd = jnp.where(gap == kd - 1, row, fwd)
                row = c2[g * 32 + 16 : g * 32 + 32, j * 256 : j * 256 + 256][:, None, :]
                bwd = jnp.where(gap == 1 - kd, row, bwd)
            at = (kx * 3 + ky) * 256
            w2_ref[:, at : at + 256] = fwd.reshape(256, 256).astype(BF16)
            at = ((2 - kx) * 3 + 2 - ky) * 256
            wb_ref[:, at : at + 256] = bwd.reshape(256, 256).astype(BF16)


def fill_density(d_ref, lo_ref, hi_ref, xlo_ref, xhi_ref, corner, dp):
    for x in range(NXT):
        dp[(x + 4) * DROW + 8 : (x + 4) * DROW + 8 + NYT, :] = d_ref[x].astype(F32)
    for k in range(3):
        dp[pl.ds(4 * DROW + 5 + k, 32, stride=DROW), :] = lo_ref[k * 32 : k * 32 + 32, :].astype(F32)
        dp[pl.ds(4 * DROW + 8 + NYT + k, 32, stride=DROW), :] = hi_ref[k * 32 : k * 32 + 32, :].astype(F32)
    for base, src, at in ((1, xlo_ref, 0), (4 + NXT, xhi_ref, 32)):
        corner[at : at + 32, :] = src[256:288, :].astype(F32)
        for k in range(3):
            dp[(base + k) * DROW + 8 : (base + k) * DROW + 8 + NYT, :] = src[k * 64 : k * 64 + 64, :].astype(F32)
        for side, y in ((0, 5), (1, 8 + NYT)):
            for ky in range(3):
                for kx in range(3):
                    row = (base + kx) * DROW + y + ky
                    dp[row : row + 1, :] = corner[at + side * 9 + 3 * ky + kx : at + side * 9 + 3 * ky + kx + 1, :]


def fill_cotangent(c_ref, lo_ref, hi_ref, xlo_ref, xhi_ref, corner, cp):
    for half in range(2):
        for x in range(HX):
            at = (x + 1) * CROW + 8
            cp[half, at : at + HY, :] = c_ref[x, :, half * 128 : half * 128 + 128].astype(F32)
        rows = slice(96 + half * 16, 112 + half * 16)
        cp[half, pl.ds(CROW + 7, 16, stride=CROW), :] = lo_ref[rows, :].astype(F32)
        cp[half, pl.ds(CROW + 8 + HY, 16, stride=CROW), :] = hi_ref[rows, :].astype(F32)
        for base, src, at in ((0, xlo_ref, 0), (HX + 1, xhi_ref, 32)):
            cp[half, base * CROW + 8 : base * CROW + 8 + HY, :] = src[192 + half * 32 : 224 + half * 32, :].astype(F32)
            for side, y in ((0, 7), (1, 8 + HY)):
                row = at + 18 + side * 2 + half
                cp[half, base * CROW + y : base * CROW + y + 1, :] = corner[row : row + 1, :]


def fine_taps(dp, taps):
    for x in range(-3, NXT + 3):
        q = x % 2
        at = ((x - q) // 2 + 2) * HY
        for t in range(4):
            rows = dp[pl.ds((x + 4) * DROW + 7 + t, HY, stride=2), :]
            taps[q, at : at + HY, t * 128 : t * 128 + 128] = rows.astype(BF16)


def coarse_taps(padded, taps):
    for x in range(HX + 2):
        for k in range(3):
            for half in range(2):
                rows = padded[half, x * CROW + 7 + k : x * CROW + 7 + k + HY, :]
                lane = k * 256 + half * 128
                taps[x * HY : x * HY + HY, lane : lane + 128] = rows.astype(BF16)


def fine_patch(taps, first, count, px, py):
    parts = []
    for kx in range(3):
        s = px + kx - 1
        q = s % 2
        at = (first + (s - q) // 2 + 2) * HY
        parts.append(taps[q, at : at + count * HY, py * 128 : py * 128 + 384])
    return jnp.concatenate(parts, axis=1)


def coarse_patch(taps, first, count):
    parts = [taps[(first + k) * HY : (first + k + count) * HY, :] for k in range(3)]
    return jnp.concatenate(parts, axis=1)


def leaky_rounded(pre):
    return jnp.where(pre > 0, pre, LEAK * pre).astype(BF16).astype(F32)


def rim_patches(dp, taps, rim):
    for px in range(2):
        for py in range(2):
            at = (px * 2 + py) * 128
            rim[at : at + 32, :] = fine_patch(taps, -1, 1, px, py)
            rim[at + 32 : at + 64, :] = fine_patch(taps, HX, 1, px, py)
            for side, y in ((0, -3), (1, NYT - 1)):
                for kx in range(3):
                    for ky in range(3):
                        start = (1 + px + kx) * DROW + 8 + y + py + ky
                        rows = dp[pl.ds(start, 18, stride=2 * DROW), :]
                        rows = jnp.concatenate([rows, jnp.zeros((14, 128), F32)], axis=0)
                        lane = (kx * 3 + ky) * 128
                        rim[at + 64 + side * 32 : at + 96 + side * 32, lane : lane + 128] = rows.astype(BF16)


def split_dot(select, values):
    high = values.astype(BF16)
    low = (values - high.astype(F32)).astype(BF16)
    return dot_nt(select, high) + dot_nt(select, low)


def extract(g1, g2, out_ref, a1, a2):
    for kd in range(3):
        for m in range(9):
            acc = jnp.zeros((16, 16, 128), F32)
            for pd in range(2):
                gap = iota((1, 16, 128), 2) % 32 - 2 * iota((1, 16, 128), 1) - pd
                part = g1[pd * 256 : pd * 256 + 256, m * 128 : m * 128 + 128].reshape(16, 16, 128)
                acc = acc + jnp.where(gap == kd - 1, part, 0.0)
            a1[(m * 3 + kd) * 16 : (m * 3 + kd) * 16 + 16, :] = jnp.sum(acc, axis=1)
            gap = iota((1, 16, 256), 2) % 16 - iota((1, 16, 256), 1)
            part = g2[:, m * 256 : m * 256 + 256].reshape(16, 16, 256)
            a2[(m * 3 + kd) * 16 : (m * 3 + kd) * 16 + 16, :] = jnp.sum(jnp.where(gap == 1 - kd, part, 0.0), axis=1)
    a1[432:512, :] = jnp.zeros((80, 128), F32)
    a2[432:512, :] = jnp.zeros((80, 256), F32)
    pick2 = (iota((16, 256), 1) // 16 == iota((16, 256), 0)).astype(BF16)
    pick1 = (iota((16, 128), 1) // 32 == iota((16, 128), 0)).astype(BF16)
    out_ref[0:16, :] = split_dot(pick2, a2[...])
    out_ref[16:24, :] = split_dot(pick1, a1[...])[0:8]


def main_kernel(
    d_ref, c_ref, lo_ref, hi_ref, xlo_ref, xhi_ref, w1_ref, wb_ref, w2_ref, feat_ref, grad_ref,
    dp, cp, pp, corner, ft, ct, pt, rim, bpre, g1, g2, a1, a2,
):
    fill_density(d_ref, lo_ref, hi_ref, xlo_ref, xhi_ref, corner, dp)
    fill_cotangent(c_ref, lo_ref, hi_ref, xlo_ref, xhi_ref, corner, cp)
    fine_taps(dp, ft)
    coarse_taps(cp, ct)
    rim_patches(dp, ft, rim)

    total = jnp.zeros((256, 128), F32)
    for c in range(4):
        act = leaky_rounded(dot_nt(w1_ref[...], rim[c * 128 : c * 128 + 128, :]))
        total = total + act[0:256] + act[256:512]
    edge = (total * 0.125).T.astype(BF16).astype(F32)
    for half in range(2):
        lanes = slice(half * 128, half * 128 + 128)
        pp[half, 8:40, :] = edge[0:32, lanes]
        pp[half, (HX + 1) * CROW + 8 : (HX + 1) * CROW + 40, :] = edge[32:64, lanes]
        pp[half, pl.ds(7, 18, stride=CROW), :] = edge[64:82, lanes]
        pp[half, pl.ds(8 + HY, 18, stride=CROW), :] = edge[96:114, lanes]

    pooled = []
    for h in range(2):
        back = dot_nt(wb_ref[...], coarse_patch(ct, h * 8, 8)).astype(BF16).astype(F32) * 0.125
        total = jnp.zeros((256, 256), F32)
        for px in range(2):
            for py in range(2):
                pre = dot_nt(w1_ref[...], fine_patch(ft, h * 8, 8, px, py))
                act = leaky_rounded(pre)
                total = total + act[0:256] + act[256:512]
                both = jnp.concatenate([back, back], axis=0)
                bpre[px * 2 + py, :, h * 256 : h * 256 + 256] = jnp.where(pre > 0, both, LEAK * both).astype(BF16)
        mean = total * 0.125
        pooled.append(mean.astype(BF16))
        cells = mean.T.astype(BF16).astype(F32)
        for x in range(8):
            at = (h * 8 + x + 1) * CROW + 8
            for half in range(2):
                pp[half, at : at + HY, :] = cells[x * HY : x * HY + HY, half * 128 : half * 128 + 128]

    total = None
    for px in range(2):
        for py in range(2):
            part = dot_nn(bpre[px * 2 + py], fine_patch(ft, 0, HX, px, py))
            total = part if total is None else total + part
    g1[...] = total
    g2[...] = dot_nn(jnp.concatenate(pooled, axis=1), coarse_patch(ct, 0, HX))
    extract(g1, g2, grad_ref, a1, a2)

    coarse_taps(pp, pt)
    feat = dot_nt(coarse_patch(pt, 0, HX), w2_ref[...])
    feat_ref[...] = feat.astype(BF16).reshape(HX, HY, 256)


def final_kernel(scale, a_ref, b_ref, g1_ref, g2_ref):
    total = (a_ref[...] + b_ref[...]) * scale
    for kd in range(3):
        for kx in range(3):
            for ky in range(3):
                t = kd * 9 + kx * 3 + ky
                at = ((kx * 3 + ky) * 3 + kd) * 16
                g1_ref[t] = total[16:20, at : at + 16]
                at = (((2 - kx) * 3 + 2 - ky) * 3 + kd) * 16
                g2_ref[t] = total[0:16, at : at + 16]


def call(kernel, outs, scratch=()):
    return pl.pallas_call(
        kernel,
        out_shape=outs,
        scratch_shapes=list(scratch),
        compiler_params=pltpu.CompilerParams(vmem_limit_bytes=VMEM_LIMIT),
    )


def struct(shape, kind):
    return jax.ShapeDtypeStruct(shape, kind)


def swap(value, axis, step):
    n = lax.axis_size(axis)
    return lax.ppermute(value, axis, [(i, (i + step) % n) for i in range(n)])


def on_device(density, kernel_one, kernel_two, cotangent):
    d, c = density[0], cotangent[0]
    k1 = jnp.transpose(kernel_one, (2, 3, 4, 1, 0)).reshape(27, CIN, CH)
    k2 = jnp.transpose(kernel_two, (2, 3, 4, 0, 1)).reshape(27, CH, CH)

    message = struct((128, 128), BF16)
    up, down = call(
        pack_y_kernel, (message, message), (pltpu.VMEM((NXT * 16, 128), F32), pltpu.VMEM((2, HX * 16, 128), F32))
    )(d, c)
    lo, hi = swap(up, "ty", 1), swap(down, "ty", -1)
    w1, wb, w2 = call(
        weights_kernel,
        (struct((512, 1152), BF16), struct((256, 2304), BF16), struct((256, 2304), BF16)),
        (
            pltpu.VMEM((128, 128), F32),
            pltpu.VMEM((128, 128), F32),
            pltpu.VMEM((16, 27 * 128), F32),
            pltpu.VMEM((128, 2048), F32),
        ),
    )(k1, k2)
    message = struct((288, 128), BF16)
    up, down = call(
        pack_x_kernel,
        (message, message),
        (pltpu.VMEM((128, 128), F32), pltpu.VMEM((128, 128), F32), pltpu.VMEM((32, 128), F32)),
    )(d, c, lo, hi)
    xlo, xhi = swap(up, "tx", 1), swap(down, "tx", -1)

    feat, grads = call(
        main_kernel,
        (struct((HX, HY, 256), BF16), struct((24, 512), F32)),
        (
            pltpu.VMEM((40 * DROW, 128), F32),
            pltpu.VMEM((2, (HX + 2) * CROW, 128), F32),
            pltpu.VMEM((2, (HX + 2) * CROW, 128), F32),
            pltpu.VMEM((64, 128), F32),
            pltpu.VMEM((2, 20 * HY, 512), BF16),
            pltpu.VMEM(((HX + 2) * HY, 768), BF16),
            pltpu.VMEM(((HX + 2) * HY, 768), BF16),
            pltpu.VMEM((512, 1152), BF16),
            pltpu.VMEM((4, 512, 512), BF16),
            pltpu.VMEM((512, 1152), F32),
            pltpu.VMEM((256, 2304), F32),
            pltpu.VMEM((512, 128), F32),
            pltpu.VMEM((512, 256), F32),
        ),
    )(d, c, lo, hi, xlo, xhi, w1, wb, w2)

    steps = [(axis, k) for axis in ("ty", "tx", "rep") for k in (1, 2, 4) if k < lax.axis_size(axis)]
    other = jnp.zeros_like(grads)
    for at, (axis, k) in enumerate(steps):
        other = lax.ppermute(grads, axis, [(i, i ^ k) for i in range(lax.axis_size(axis))])
        if at < len(steps) - 1:
            grads = grads + other
    g1, g2 = call(
        functools.partial(final_kernel, 1.0 / lax.axis_size("rep")),
        (struct((27, CIN, CH), F32), struct((27, CH, CH), F32)),
    )(grads, other)
    g1 = jnp.transpose(g1.reshape(3, 3, 3, CIN, CH), (4, 3, 0, 1, 2))
    g2 = jnp.transpose(g2.reshape(3, 3, 3, CH, CH), (3, 4, 0, 1, 2))
    return feat[None], g1, g2


def solution(mesh):
    in_specs = (P("rep", "tx", "ty", None), P(), P(), P("rep", "tx", "ty", None))
    out_specs = (P("rep", "tx", "ty", None), P(), P())
    return jax.shard_map(on_device, mesh=mesh, in_specs=in_specs, out_specs=out_specs, check_vma=False)
```

time: 1270 us -> 61.9 us (0.05)
  matrix products: 517 us -> 0 us
  blocking collectives: 340 us -> 0 us
  local copies, waits for them, and re-layouts: 285 us -> 2 us
  other arithmetic: 95 us -> 0.05 us
  waiting for transfers between devices: 0.03 us -> 25.2 us
  Pallas kernels: 0 us -> 14.7 us
    conv_general_dilated x5 -> x0, matrix products: 517 us -> none  [convolve(): lax.conv_general_dilated(lhs, rhs, (1, 1, 1), 'VALID', dimension_numbers=...]
    psum x2 -> x0, blocking collectives: 340 us -> none  [the longest x1 332 us: on_device(): tile_one, tile_two = lax.psum((slab_one, slab_two), ('tx', 'ty'))]
    reshape x8 -> x0, local copies, waits for them, and re-layouts: 123 us -> none  [the longest x7 92.8 us: unpack(): field.reshape(s, x, y, channels, merged // channels)]
    conv_general_dilated x7 -> x0, local copies, waits for them, and re-layouts: 59.8 us -> none  [convolve(): lax.conv_general_dilated(lhs, rhs, (1, 1, 1), 'VALID', dimension_numbers=...]
    unnamed x43 -> x12, local copies, waits for them, and re-layouts: 48.5 us -> 2 us
    convert_element_type x1 -> x0, other arithmetic: 27.8 us -> none  [on_device(): (upsample(back_pooled.astype(jnp.float32)) * 0.125 * slope).astype(jnp.bf...]
    reduce_sum x1 -> x0, other arithmetic: 25.2 us -> none  [pooling(): return jnp.mean(blocks, axis=(3, 5, 7))]
    ppermute x12 -> x11, waiting for transfers between devices: 0.03 us -> 25.2 us  [the longest x7 21.5 us: on_device(): lax.ppermute(grads, axis, [(i, i ^ k) for i in range(lax.axis_size(axis))])]
  transfers between devices with their start and end apart: 12 -> 11, of which waited for: 0 -> 10; matrix products, arithmetic and copies ran while one was open for 63% -> 0% of each run, Pallas kernels for 0% -> 3%
where the time goes in v1:
time: 61.9 us; the launch traced here: 61.7 us
  waiting for transfers between devices  25.2 us (41%)
  starting transfers between devices  19 us (31%)
  Pallas kernels  14.7 us (24%)
  local copies, waits for them, and re-layouts  2 us (3%)
  between operations  0.7 us (1%)
    ppermute x7, waiting for transfers between devices, on_device(): lax.ppermute(grads, axis, [(i, i ^ k) for i in range(lax.axis_size(axis))])  21.5 us
    pallas_call x1, Pallas kernels, on_device(): call(main_kernel, (struct((HX, HY, 256), BF16), struct((24, 512), F32)),...  11.8 us
    ppermute x7, starting transfers between devices, on_device(): lax.ppermute(grads, axis, [(i, i ^ k) for i in range(lax.axis_size(axis))])  9.75 us
    ppermute x4, starting transfers between devices, swap(): return lax.ppermute(value, axis, [(i, (i + step) % n) for i in range(n)])  9.3 us
    ppermute x4, waiting for transfers between devices, swap(): return lax.ppermute(value, axis, [(i, (i + step) % n) for i in range(n)])  3.67 us
    unnamed x12, local copies, waits for them, and re-layouts  2 us
    pallas_call x1, Pallas kernels, on_device(): call(weights_kernel, (struct((512, 1152), BF16), struct((256, 2304), BF16...  1.94 us
  transfers between devices with their start and end apart: 11, of which 10 were waited for; matrix products, arithmetic and copies ran while one was open for 0% of the time, Pallas kernels for 3%

profile of v1, /device:TPU:0, one launch (start us, length us, event | category | flops | bytes accessed | tf_op | source)
XLA Modules:
  0.0 61.7 jit_solution(6042268797994337046)
XLA Ops:
  0.6 1.0 %copy-done = bf16[1,32,64,128]{3,2,1,0:T(8,128)(2,1)S(1)} copy-done((bf16[1,32,64,128]{3,2,1,0:T(8,128)(2,1)S(1)}, bf16[1,32,64,128]{3,2,1,0:T(8,128)(2,1)}, u32[]{:S(2)}) %copy-start) | copy-done | bytes 524312
  1.7 0.9 %copy-done.2 = bf16[1,16,32,256]{3,2,1,0:T(8,128)(2,1)S(1)} copy-done((bf16[1,16,32,256]{3,2,1,0:T(8,128)(2,1)S(1)}, bf16[1,16,32,256]{3,2,1,0:T(8,128)(2,1)}, u32[]{:S(2)}) %copy-start.2) | copy-done | bytes 262168
  2.8 3.6 %collective-permute-start.1 = (bf16[128,128]{1,0:T(8,128)(2,1)S(1)}, bf16[128,128]{1,0:T(8,128)(2,1)S(1)}, u32[]{:S(2)}, u32[]{:S(2)}) collective-permute-start(bf16[128,128]{1,0:T(8,128)(2,1)S(1)} %get-tuple-element.15), channel_id=1, source_target_pairs={{0,7},{1,0},{2,1},{3,2},{4,3},{5,4},{6,5},{7,6},{8,15},{9,8},{10,9... | collective-permute-start | bytes 98312 | tf_op jit(solution)/shard_map/ppermute | solution.py:309
  6.3 1.6 %collective-permute-done.lo_ref = bf16[128,128]{1,0:T(8,128)(2,1)S(1)} collective-permute-done((bf16[128,128]{1,0:T(8,128)(2,1)S(1)}, bf16[128,128]{1,0:T(8,128)(2,1)S(1)}, u32[]{:S(2)}, u32[]{:S(2)}) %collective-permute-start) | collective-permute-done | bytes 32800 | tf_op jit(solution)/shard_map/ppermute | solution.py:309
  8.0 3.3 %collective-permute-start.2 = (bf16[288,128]{1,0:T(8,128)(2,1)S(1)}, bf16[288,128]{1,0:T(8,128)(2,1)S(1)}, u32[]{:S(2)}, u32[]{:S(2)}) collective-permute-start(bf16[288,128]{1,0:T(8,128)(2,1)S(1)} %get-tuple-element.16), channel_id=1, source_target_pairs={{0,8},{8,16},{16,24},{24,32},{32,40},{40,48},{48,56},{56,0},{1,9},... | collective-permute-start | bytes 221192 | tf_op jit(solution)/shard_map/ppermute | solution.py:309
  11.2 2.4 %collective-permute-start.3 = (bf16[288,128]{1,0:T(8,128)(2,1)S(1)}, bf16[288,128]{1,0:T(8,128)(2,1)S(1)}, u32[]{:S(2)}, u32[]{:S(2)}) collective-permute-start(bf16[288,128]{1,0:T(8,128)(2,1)S(1)} %get-tuple-element.17), channel_id=1, source_target_pairs={{0,56},{8,0},{16,8},{24,16},{32,24},{40,32},{48,40},{56,48},{1,57}... | collective-permute-start | bytes 221192 | tf_op jit(solution)/shard_map/ppermute | solution.py:309
  13.7 1.9 %shard_map.69 = (bf16[512,1152]{1,0:T(8,128)(2,1)S(1)}, bf16[256,2304]{1,0:T(8,128)(2,1)S(1)}, bf16[256,2304]{1,0:T(8,128)(2,1)S(1)}) custom-call(bf16[27,4,16]{2,1,0:T(4,128)(2,1)S(1)} %bitcast.22, bf16[27,16,16]{2,1,0:T(8,128)(2,1)S(1)} %bitcast.21), custom_call_target="tpu_custom_call" | custom-call | tf_op jit(solution)/shard_map/pallas_call | solution.py:322
  15.6 0.6 collective-permute-done.2.xlo_ref
  16.2 1.5 %collective-permute-done.3.xhi_ref = bf16[288,128]{1,0:T(8,128)(2,1)S(1)} collective-permute-done((bf16[288,128]{1,0:T(8,128)(2,1)S(1)}, bf16[288,128]{1,0:T(8,128)(2,1)S(1)}, u32[]{:S(2)}, u32[]{:S(2)}) %collective-permute-start.3) | collective-permute-done | bytes 73760 | tf_op jit(solution)/shard_map/ppermute | solution.py:309
  17.7 11.8 %shard_map.70 = (bf16[16,32,256]{2,1,0:T(8,128)(2,1)}, f32[24,512]{1,0:T(8,128)S(1)}) custom-call(bf16[32,64,128]{2,1,0:T(8,128)(2,1)S(1)} %bitcast.17, bf16[16,32,256]{2,1,0:T(8,128)(2,1)S(1)} %bitcast.20, bf16[128,128]{1,0:T(8,128)(2,1)S(1)} %collective-permute-done.lo_ref, bf16[128,128]{1,0:T(8,128)(2,1)S(1)} %collective-permute-done.1.hi_ref, ...), custom_call_target="tpu_custom_call" | custom-call | tf_op jit(solution)/shard_map/pallas_call | solution.py:340
  29.5 1.2 %collective-permute-done.4 = f32[24,512]{1,0:T(8,128)S(1)} collective-permute-done((f32[24,512]{1,0:T(8,128)S(1)}, f32[24,512]{1,0:T(8,128)S(1)}, u32[]{:S(2)}, u32[]{:S(2)}) %collective-permute-start.4) | collective-permute-done | bytes 49184 | tf_op jit(solution)/shard_map/ppermute | solution.py:363
  30.8 1.1 %collective-permute-start.5 = (f32[24,512]{1,0:T(8,128)S(1)}, f32[24,512]{1,0:T(8,128)S(1)}, u32[]{:S(2)}, u32[]{:S(2)}) collective-permute-start(f32[24,512]{1,0:T(8,128)S(1)} %add.18), channel_id=1, source_target_pairs={{0,2},{1,3},{2,0},{3,1},{4,6},{5,7},{6,4},{7,5},{8,10},{9,11},{10,... | collective-permute-start | bytes 147464 | tf_op jit(solution)/shard_map/ppermute | solution.py:363
  31.9 3.1 %collective-permute-done.5 = f32[24,512]{1,0:T(8,128)S(1)} collective-permute-done((f32[24,512]{1,0:T(8,128)S(1)}, f32[24,512]{1,0:T(8,128)S(1)}, u32[]{:S(2)}, u32[]{:S(2)}) %collective-permute-start.5) | collective-permute-done | bytes 49184 | tf_op jit(solution)/shard_map/ppermute | solution.py:363
  34.9 2.8 %collective-permute-start.6 = (f32[24,512]{1,0:T(8,128)S(1)}, f32[24,512]{1,0:T(8,128)S(1)}, u32[]{:S(2)}, u32[]{:S(2)}) collective-permute-start(f32[24,512]{1,0:T(8,128)S(1)} %add.19), channel_id=1, source_target_pairs={{0,4},{1,5},{2,6},{3,7},{4,0},{5,1},{6,2},{7,3},{8,12},{9,13},{10,... | collective-permute-start | bytes 147464 | tf_op jit(solution)/shard_map/ppermute | solution.py:363
  37.8 2.8 %collective-permute-done.6 = f32[24,512]{1,0:T(8,128)S(1)} collective-permute-done((f32[24,512]{1,0:T(8,128)S(1)}, f32[24,512]{1,0:T(8,128)S(1)}, u32[]{:S(2)}, u32[]{:S(2)}) %collective-permute-start.6) | collective-permute-done | bytes 49184 | tf_op jit(solution)/shard_map/ppermute | solution.py:363
  40.6 1.6 %collective-permute-start.7 = (f32[24,512]{1,0:T(8,128)S(1)}, f32[24,512]{1,0:T(8,128)S(1)}, u32[]{:S(2)}, u32[]{:S(2)}) collective-permute-start(f32[24,512]{1,0:T(8,128)S(1)} %add.20), channel_id=1, source_target_pairs={{0,8},{8,0},{16,24},{24,16},{32,40},{40,32},{48,56},{56,48},{1,9},... | collective-permute-start | bytes 147464 | tf_op jit(solution)/shard_map/ppermute | solution.py:363
  42.3 4.0 %collective-permute-done.7 = f32[24,512]{1,0:T(8,128)S(1)} collective-permute-done((f32[24,512]{1,0:T(8,128)S(1)}, f32[24,512]{1,0:T(8,128)S(1)}, u32[]{:S(2)}, u32[]{:S(2)}) %collective-permute-start.7) | collective-permute-done | bytes 49184 | tf_op jit(solution)/shard_map/ppermute | solution.py:363
  46.3 1.0 %collective-permute-start.8 = (f32[24,512]{1,0:T(8,128)S(1)}, f32[24,512]{1,0:T(8,128)S(1)}, u32[]{:S(2)}, u32[]{:S(2)}) collective-permute-start(f32[24,512]{1,0:T(8,128)S(1)} %add.21), channel_id=1, source_target_pairs={{0,16},{8,24},{16,0},{24,8},{32,48},{40,56},{48,32},{56,40},{1,17}... | collective-permute-start | bytes 147464 | tf_op jit(solution)/shard_map/ppermute | solution.py:363
  47.3 3.7 %collective-permute-done.8 = f32[24,512]{1,0:T(8,128)S(1)} collective-permute-done((f32[24,512]{1,0:T(8,128)S(1)}, f32[24,512]{1,0:T(8,128)S(1)}, u32[]{:S(2)}, u32[]{:S(2)}) %collective-permute-start.8) | collective-permute-done | bytes 49184 | tf_op jit(solution)/shard_map/ppermute | solution.py:363
  51.0 2.2 %collective-permute-start.9 = (f32[24,512]{1,0:T(8,128)S(1)}, f32[24,512]{1,0:T(8,128)S(1)}, u32[]{:S(2)}, u32[]{:S(2)}) collective-permute-start(f32[24,512]{1,0:T(8,128)S(1)} %add.22), channel_id=1, source_target_pairs={{0,32},{8,40},{16,48},{24,56},{32,0},{40,8},{48,16},{56,24},{1,33}... | collective-permute-start | bytes 147464 | tf_op jit(solution)/shard_map/ppermute | solution.py:363
  53.1 3.5 %collective-permute-done.9 = f32[24,512]{1,0:T(8,128)S(1)} collective-permute-done((f32[24,512]{1,0:T(8,128)S(1)}, f32[24,512]{1,0:T(8,128)S(1)}, u32[]{:S(2)}, u32[]{:S(2)}) %collective-permute-start.9) | collective-permute-done | bytes 49184 | tf_op jit(solution)/shard_map/ppermute | solution.py:363
  56.7 1.1 %collective-permute-start.10 = (f32[24,512]{1,0:T(8,128)S(1)}, f32[24,512]{1,0:T(8,128)S(1)}, u32[]{:S(2)}, u32[]{:S(2)}) collective-permute-start(f32[24,512]{1,0:T(8,128)S(1)} %add.23.a_ref), channel_id=1, source_target_pairs={{0,64},{64,0},{1,65},{65,1},{2,66},{66,2},{3,67},{67,3},{4,68},{68... | collective-permute-start | bytes 147464 | tf_op jit(solution)/shard_map/ppermute | solution.py:363
  57.8 3.1 %collective-permute-done.10.b_ref = f32[24,512]{1,0:T(8,128)S(1)} collective-permute-done((f32[24,512]{1,0:T(8,128)S(1)}, f32[24,512]{1,0:T(8,128)S(1)}, u32[]{:S(2)}, u32[]{:S(2)}) %collective-permute-start.10) | collective-permute-done | bytes 49184 | tf_op jit(solution)/shard_map/ppermute | solution.py:363
  60.8 0.8 %shard_map.71 = (f32[27,4,16]{2,1,0:T(4,128)}, f32[27,16,16]{2,1,0:T(8,128)}) custom-call(f32[24,512]{1,0:T(8,128)S(1)} %add.23.a_ref, f32[24,512]{1,0:T(8,128)S(1)} %collective-permute-done.10.b_ref), custom_call_target="tpu_custom_call" | custom-call | tf_op jit(solution)/shard_map/pallas_call | solution.py:366
  (21 shorter events, 0.3 us)
Async XLA Ops:
  0.6 1.0 %copy-start = (bf16[1,32,64,128]{3,2,1,0:T(8,128)(2,1)S(1)}, bf16[1,32,64,128]{3,2,1,0:T(8,128)(2,1)}, u32[]{:S(2)}) copy-start(bf16[1,32,64,128]{3,2,1,0:T(8,128)(2,1)} %param.4) | copy-start | bytes 1572868
  1.7 0.9 %copy-start.2 = (bf16[1,16,32,256]{3,2,1,0:T(8,128)(2,1)S(1)}, bf16[1,16,32,256]{3,2,1,0:T(8,128)(2,1)}, u32[]{:S(2)}) copy-start(bf16[1,16,32,256]{3,2,1,0:T(8,128)(2,1)} %param.7) | copy-start | bytes 786436
  2.6 11.1 %copy-start.4 = (bf16[16,16,3,3,3]{1,0,4,3,2:T(8,128)(2,1)S(1)}, bf16[16,16,3,3,3]{1,0,4,3,2:T(8,128)(2,1)}, u32[]{:S(2)}) copy-start(bf16[16,16,3,3,3]{1,0,4,3,2:T(8,128)(2,1)} %param.6) | copy-start | bytes 41476
  2.6 11.1 %copy-start.5 = (bf16[16,4,3,3,3]{0,1,4,3,2:T(4,128)(2,1)S(1)}, bf16[16,4,3,3,3]{0,1,4,3,2:T(4,128)(2,1)}, u32[]{:S(2)}) copy-start(bf16[16,4,3,3,3]{0,1,4,3,2:T(4,128)(2,1)} %param.5) | copy-start | bytes 10372
  2.6 15.1 %copy-start.1 = (bf16[1,32,64,128]{3,2,1,0:T(8,128)(2,1)S(1)}, bf16[1,32,64,128]{3,2,1,0:T(8,128)(2,1)}, u32[]{:S(2)}) copy-start(bf16[1,32,64,128]{3,2,1,0:T(8,128)(2,1)} %param.4) | copy-start | bytes 1572868
  2.6 15.1 %copy-start.3 = (bf16[1,16,32,256]{3,2,1,0:T(8,128)(2,1)S(1)}, bf16[1,16,32,256]{3,2,1,0:T(8,128)(2,1)}, u32[]{:S(2)}) copy-start(bf16[1,16,32,256]{3,2,1,0:T(8,128)(2,1)} %param.7) | copy-start | bytes 786436
  2.7 5.2 %collective-permute-start = (bf16[128,128]{1,0:T(8,128)(2,1)S(1)}, bf16[128,128]{1,0:T(8,128)(2,1)S(1)}, u32[]{:S(2)}, u32[]{:S(2)}) collective-permute-start(bf16[128,128]{1,0:T(8,128)(2,1)S(1)} %get-tuple-element.14), channel_id=1, source_target_pairs={{0,1},{1,2},{2,3},{3,4},{4,5},{5,6},{6,7},{7,0},{8,9},{9,10},{10,1... | collective-permute-start | bytes 98312 | tf_op jit(solution)/shard_map/ppermute | solution.py:309
  2.8 5.2 %collective-permute-start.1 = (bf16[128,128]{1,0:T(8,128)(2,1)S(1)}, bf16[128,128]{1,0:T(8,128)(2,1)S(1)}, u32[]{:S(2)}, u32[]{:S(2)}) collective-permute-start(bf16[128,128]{1,0:T(8,128)(2,1)S(1)} %get-tuple-element.15), channel_id=1, source_target_pairs={{0,7},{1,0},{2,1},{3,2},{4,3},{5,4},{6,5},{7,6},{8,15},{9,8},{10,9... | collective-permute-start | bytes 98312 | tf_op jit(solution)/shard_map/ppermute | solution.py:309
  8.0 8.2 %collective-permute-start.2 = (bf16[288,128]{1,0:T(8,128)(2,1)S(1)}, bf16[288,128]{1,0:T(8,128)(2,1)S(1)}, u32[]{:S(2)}, u32[]{:S(2)}) collective-permute-start(bf16[288,128]{1,0:T(8,128)(2,1)S(1)} %get-tuple-element.16), channel_id=1, source_target_pairs={{0,8},{8,16},{16,24},{24,32},{32,40},{40,48},{48,56},{56,0},{1,9},... | collective-permute-start | bytes 221192 | tf_op jit(solution)/shard_map/ppermute | solution.py:309
  11.2 6.5 %collective-permute-start.3 = (bf16[288,128]{1,0:T(8,128)(2,1)S(1)}, bf16[288,128]{1,0:T(8,128)(2,1)S(1)}, u32[]{:S(2)}, u32[]{:S(2)}) collective-permute-start(bf16[288,128]{1,0:T(8,128)(2,1)S(1)} %get-tuple-element.17), channel_id=1, source_target_pairs={{0,56},{8,0},{16,8},{24,16},{32,24},{40,32},{48,40},{56,48},{1,57}... | collective-permute-start | bytes 221192 | tf_op jit(solution)/shard_map/ppermute | solution.py:309
  29.5 1.2 %collective-permute-start.4 = (f32[24,512]{1,0:T(8,128)S(1)}, f32[24,512]{1,0:T(8,128)S(1)}, u32[]{:S(2)}, u32[]{:S(2)}) collective-permute-start(f32[24,512]{1,0:T(8,128)S(1)} %get-tuple-element.22), channel_id=1, source_target_pairs={{0,1},{1,0},{2,3},{3,2},{4,5},{5,4},{6,7},{7,6},{8,9},{9,8},{10,11... | collective-permute-start | bytes 147464 | tf_op jit(solution)/shard_map/ppermute | solution.py:363
  30.8 4.2 %collective-permute-start.5 = (f32[24,512]{1,0:T(8,128)S(1)}, f32[24,512]{1,0:T(8,128)S(1)}, u32[]{:S(2)}, u32[]{:S(2)}) collective-permute-start(f32[24,512]{1,0:T(8,128)S(1)} %add.18), channel_id=1, source_target_pairs={{0,2},{1,3},{2,0},{3,1},{4,6},{5,7},{6,4},{7,5},{8,10},{9,11},{10,... | collective-permute-start | bytes 147464 | tf_op jit(solution)/shard_map/ppermute | solution.py:363
  34.9 5.7 %collective-permute-start.6 = (f32[24,512]{1,0:T(8,128)S(1)}, f32[24,512]{1,0:T(8,128)S(1)}, u32[]{:S(2)}, u32[]{:S(2)}) collective-permute-start(f32[24,512]{1,0:T(8,128)S(1)} %add.19), channel_id=1, source_target_pairs={{0,4},{1,5},{2,6},{3,7},{4,0},{5,1},{6,2},{7,3},{8,12},{9,13},{10,... | collective-permute-start | bytes 147464 | tf_op jit(solution)/shard_map/ppermute | solution.py:363
  40.6 5.7 %collective-permute-start.7 = (f32[24,512]{1,0:T(8,128)S(1)}, f32[24,512]{1,0:T(8,128)S(1)}, u32[]{:S(2)}, u32[]{:S(2)}) collective-permute-start(f32[24,512]{1,0:T(8,128)S(1)} %add.20), channel_id=1, source_target_pairs={{0,8},{8,0},{16,24},{24,16},{32,40},{40,32},{48,56},{56,48},{1,9},... | collective-permute-start | bytes 147464 | tf_op jit(solution)/shard_map/ppermute | solution.py:363
  46.3 4.7 %collective-permute-start.8 = (f32[24,512]{1,0:T(8,128)S(1)}, f32[24,512]{1,0:T(8,128)S(1)}, u32[]{:S(2)}, u32[]{:S(2)}) collective-permute-start(f32[24,512]{1,0:T(8,128)S(1)} %add.21), channel_id=1, source_target_pairs={{0,16},{8,24},{16,0},{24,8},{32,48},{40,56},{48,32},{56,40},{1,17}... | collective-permute-start | bytes 147464 | tf_op jit(solution)/shard_map/ppermute | solution.py:363
  51.0 5.7 %collective-permute-start.9 = (f32[24,512]{1,0:T(8,128)S(1)}, f32[24,512]{1,0:T(8,128)S(1)}, u32[]{:S(2)}, u32[]{:S(2)}) collective-permute-start(f32[24,512]{1,0:T(8,128)S(1)} %add.22), channel_id=1, source_target_pairs={{0,32},{8,40},{16,48},{24,56},{32,0},{40,8},{48,16},{56,24},{1,33}... | collective-permute-start | bytes 147464 | tf_op jit(solution)/shard_map/ppermute | solution.py:363
  56.7 4.2 %collective-permute-start.10 = (f32[24,512]{1,0:T(8,128)S(1)}, f32[24,512]{1,0:T(8,128)S(1)}, u32[]{:S(2)}, u32[]{:S(2)}) collective-permute-start(f32[24,512]{1,0:T(8,128)S(1)} %add.23.a_ref), channel_id=1, source_target_pairs={{0,64},{64,0},{1,65},{65,1},{2,66},{66,2},{3,67},{67,3},{4,68},{68... | collective-permute-start | bytes 147464 | tf_op jit(solution)/shard_map/ppermute | solution.py:363

commit v2 on v0

v2 whole, which is shorter than its diff:
```python
import jax
import jax.numpy as jnp
from jax import lax
from jax.experimental import pallas as pl
from jax.experimental.pallas import tpu as pltpu
from jax.sharding import Mesh
from jax.sharding import PartitionSpec as P

CIN = 4
CH = 16
LEAK = 0.3
F32 = jnp.float32
BF16 = jnp.bfloat16
NXT = 32
NYT = 64
HX = NXT // 2
HY = NYT // 2
DROW = 80
CROW = 48
ZONE = 10
VMEM_LIMIT = 32 * 1024 * 1024
FLOPS = 5_000_000_000
VMEM_ALL = 60 * 1024 * 1024


def dot_nt(lhs, rhs):
    return lax.dot_general(lhs, rhs, (((1,), (1,)), ((), ())), preferred_element_type=F32)


def dot_nn(lhs, rhs):
    return lax.dot_general(lhs, rhs, (((1,), (0,)), ((), ())), preferred_element_type=F32)


def iota(shape, dim):
    return lax.broadcasted_iota(jnp.int32, shape, dim)


def pack_y_kernel(d_hbm, c_hbm, up_ref, down_ref, db, cb, ds, cs, sem):
    copies = []
    for low in range(2):
        at, cat = (NYT - 16, HY - 16) if low == 0 else (0, 0)
        copies.append(pltpu.make_async_copy(d_hbm.at[:, pl.ds(at, 16), :], db.at[low], sem.at[2 * low]))
        copies.append(pltpu.make_async_copy(c_hbm.at[:, pl.ds(cat, 16), :], cb.at[low], sem.at[2 * low + 1]))
    for copy in copies:
        copy.start()
    for copy in copies:
        copy.wait()
    for low, out, row, crow in ((0, up_ref, 13, 15), (1, down_ref, 0, 0)):
        ds[...] = db[low].astype(F32).reshape(NXT * 16, 128)
        for half in range(2):
            cs[half] = cb[low, :, :, half * 128 : half * 128 + 128].astype(F32).reshape(HX * 16, 128)
        for k in range(3):
            out[k * 32 : k * 32 + 32, :] = ds[pl.ds(row + k, 32, stride=16), :].astype(BF16)
        for half in range(2):
            edge = cs[half, pl.ds(crow, 16, stride=16), :]
            out[96 + half * 16 : 112 + half * 16, :] = edge.astype(BF16)


def pack_x_kernel(d_ref, c_ref, lo_ref, hi_ref, after_ref, up_ref, down_ref, ls, hs, ms):
    ls[...] = lo_ref[...].astype(F32)
    hs[...] = hi_ref[...].astype(F32)
    for out, x, cx in ((down_ref, 0, 0), (up_ref, NXT - 3, HX - 1)):
        out[0:192, :] = d_ref[x : x + 3, :, :].reshape(192, 128)
        out[192:224, :] = c_ref[cx, :, 0:128]
        out[224:256, :] = c_ref[cx, :, 128:256]
        for side, src in enumerate((ls, hs)):
            for k in range(3):
                ms[side * 9 + 3 * k : side * 9 + 3 * k + 3, :] = src[k * 32 + x : k * 32 + x + 3, :]
            for half in range(2):
                at = 18 + side * 2 + half
                ms[at : at + 1, :] = src[96 + half * 16 + cx : 97 + half * 16 + cx, :]
        ms[22:32, :] = jnp.zeros((10, 128), F32)
        out[256:288, :] = ms[...].astype(BF16)


def weights_kernel(k1_ref, k2_ref, w1_ref, wb_ref, w2_ref, s1, so, c1, cf, cb):
    for t in range(27):
        s1[4 * t : 4 * t + 4, 0:CH] = k1_ref[t].astype(F32)
    s1[108:128, :] = jnp.zeros((20, 128), F32)
    k1t = s1[...].T[0:CH].astype(BF16)
    so[...] = jnp.zeros(so.shape, F32)
    for t in range(27):
        g, j = t // 8, t % 8
        so[g * 16 : g * 16 + 16, j * 16 : j * 16 + 16] = k2_ref[t].astype(F32)
    for g in range(4):
        for j in range(8):
            if g * 8 + j < 27:
                s1[j * 16 : j * 16 + 16, 0:CH] = k2_ref[g * 8 + j].astype(F32)
        so[64 + g * 16 : 80 + g * 16, :] = s1[...].T[0:CH]
    rep1 = (iota((128, 27 * 128), 0) == iota((128, 27 * 128), 1) // 32).astype(BF16)
    c1[...] = dot_nn(k1t, rep1)
    row, lane = iota((128, 2048), 0), iota((128, 2048), 1)
    rep2 = ((row // 16 == lane // 256) & (row % 16 == lane % 16)).astype(BF16)
    cf[...] = dot_nn(so[0:64, :].astype(BF16), rep2)
    rep2 = (row == lane // 16).astype(BF16)
    cb[...] = dot_nn(so[64:128, :].astype(BF16), rep2)

    depth1 = iota((16, 128), 1) % 32
    depth2 = iota((16, 256), 1) % 16
    gap = iota((1, 16, 256), 2) // 16 - iota((1, 16, 256), 1)
    for kx in range(3):
        for ky in range(3):
            ts = [kd * 9 + kx * 3 + ky for kd in range(3)]
            at = (kx * 3 + ky) * 128
            ones = [c1[:, t * 128 : t * 128 + 128] for t in ts]
            for d in range(32):
                acc = jnp.zeros((16, 128), F32)
                for kd in range(3):
                    acc = jnp.where(depth1 == d + kd - 1, ones[kd], acc)
                row = (d % 2) * 256 + (d // 2) * 16
                w1_ref[row : row + 16, at : at + 128] = acc.astype(BF16)
            at = ((2 - kx) * 3 + 2 - ky) * 256
            backs = [cb[t // 8 * 16 : t // 8 * 16 + 16, t % 8 * 256 : t % 8 * 256 + 256] for t in ts]
            for d in range(16):
                acc = jnp.zeros((16, 256), F32)
                for kd in range(3):
                    acc = jnp.where(depth2 == d + 1 - kd, backs[kd], acc)
                wb_ref[d * 16 : d * 16 + 16, at : at + 256] = acc.astype(BF16)
            at = (kx * 3 + ky) * 256
            acc = jnp.zeros((16, 16, 256), F32)
            for kd, t in enumerate(ts):
                part = cf[t // 8 * 16 : t // 8 * 16 + 16, t % 8 * 256 : t % 8 * 256 + 256]
                acc = jnp.where(gap == kd - 1, part[:, None, :], acc)
            w2_ref[:, at : at + 256] = acc.reshape(256, 256).astype(BF16)


def fine_taps(dp, taps, layers):
    for row, q, at in layers:
        for t in range(4):
            rows = dp[pl.ds(row + 7 + t, HY, stride=2), :]
            taps[q, at : at + HY, t * 128 : t * 128 + 128] = rows.astype(BF16)


def coarse_taps(padded, taps, count):
    for x in range(count):
        for k in range(3):
            for half in range(2):
                rows = padded[half, x * CROW + 7 + k : x * CROW + 7 + k + HY, :]
                lane = k * 256 + half * 128
                taps[x * HY : x * HY + HY, lane : lane + 128] = rows.astype(BF16)


def fine_patch(taps, first, count, px, py):
    parts = []
    for kx in range(3):
        s = px + kx - 1
        q = s % 2
        at = (first + (s - q) // 2) * HY
        parts.append(taps[q, at : at + count * HY, py * 128 : py * 128 + 384])
    return jnp.concatenate(parts, axis=1)


def coarse_patch(taps, first, count):
    parts = [taps[(first + k - 1) * HY : (first + k - 1 + count) * HY, :] for k in range(3)]
    return jnp.concatenate(parts, axis=1)


def pooled_sum(pre):
    total = jnp.zeros((256, 128), F32)
    for c in range(4):
        part = pre[:, c * 128 : c * 128 + 128]
        act = jnp.where(part > 0, part, LEAK * part).astype(BF16).astype(F32)
        total = total + act[0:256] + act[256:512]
    return total * 0.125


def back_through(pre, back):
    both = jnp.concatenate([back, back], axis=0)
    low = LEAK * both
    return [jnp.where(pre[:, c * 128 : c * 128 + 128] > 0, both, low).astype(BF16) for c in range(4)]


def inner_kernel(d_ref, c_ref, lo_ref, hi_ref, w1_ref, wb_ref, pool_ref, ct_ref, g1_ref, dp, cp, ft, bpre):
    for x in range(3, 29):
        at = (x - 3) * DROW + 8
        dp[at : at + NYT, :] = d_ref[x].astype(F32)
    for k in range(3):
        lo = lo_ref[k * 32 : k * 32 + 32, :].astype(F32)
        hi = hi_ref[k * 32 : k * 32 + 32, :].astype(F32)
        dp[pl.ds(5 + k, 26, stride=DROW), :] = lo[3:29]
        dp[pl.ds(8 + NYT + k, 26, stride=DROW), :] = hi[3:29]
    for half in range(2):
        for x in range(1, 15):
            at = (x - 1) * CROW + 8
            cp[half, at : at + HY, :] = c_ref[x, :, half * 128 : half * 128 + 128].astype(F32)
        rows = slice(96 + half * 16, 112 + half * 16)
        cp[half, pl.ds(7, 14, stride=CROW), :] = lo_ref[rows, :].astype(F32)[1:15]
        cp[half, pl.ds(8 + HY, 14, stride=CROW), :] = hi_ref[rows, :].astype(F32)[1:15]
    fine_taps(dp, ft, [((x - 3) * DROW, x % 2, (x // 2 - 1) * HY) for x in range(3, 29)])
    coarse_taps(cp, ct_ref, 14)
    back = dot_nt(wb_ref[...], coarse_patch(ct_ref, 1, 12)).astype(BF16).astype(F32) * 0.125
    patches = []
    for g in range(3):
        group = [fine_patch(ft, 1 + 4 * g, 4, px, py) for px in range(2) for py in range(2)]
        pre = dot_nt(w1_ref[...], jnp.concatenate(group, axis=0))
        pool_ref[:, g * 128 : g * 128 + 128] = pooled_sum(pre).astype(BF16)
        for c, part in enumerate(back_through(pre, back[:, g * 128 : g * 128 + 128])):
            bpre[:, (g * 4 + c) * 128 : (g * 4 + c) * 128 + 128] = part
        patches += group
    g1_ref[...] = dot_nn(bpre[...], jnp.concatenate(patches, axis=0))


def split_dot(select, values):
    high = values.astype(BF16)
    low = (values - high.astype(F32)).astype(BF16)
    return dot_nt(select, high) + dot_nt(select, low)


def extract(g1, g2, out_ref, a1, a2):
    depth1 = iota((16, 128), 1) % 32
    depth2 = iota((16, 256), 1) % 16
    for m in range(9):
        acc = [jnp.zeros((16, 128), F32)] * 3
        for d in range(32):
            row = (d % 2) * 256 + (d // 2) * 16
            part = g1[row : row + 16, m * 128 : m * 128 + 128]
            acc = [jnp.where(depth1 == d + kd - 1, part, acc[kd]) for kd in range(3)]
        for kd in range(3):
            a1[(m * 3 + kd) * 16 : (m * 3 + kd) * 16 + 16, :] = acc[kd]
        acc = [jnp.zeros((16, 256), F32)] * 3
        for d in range(16):
            part = g2[d * 16 : d * 16 + 16, m * 256 : m * 256 + 256]
            acc = [jnp.where(depth2 == d + 1 - kd, part, acc[kd]) for kd in range(3)]
        for kd in range(3):
            a2[(m * 3 + kd) * 16 : (m * 3 + kd) * 16 + 16, :] = acc[kd]
    a1[432:512, :] = jnp.zeros((80, 128), F32)
    a2[432:512, :] = jnp.zeros((80, 256), F32)
    pick2 = (iota((16, 256), 1) // 16 == iota((16, 256), 0)).astype(BF16)
    pick1 = (iota((16, 128), 1) // 32 == iota((16, 128), 0)).astype(BF16)
    two = split_dot(pick2, a2[...])
    one = split_dot(pick1, a1[...])
    out_ref[...] = jnp.concatenate([two, one], axis=0).astype(BF16)


def edge_kernel(
    d_ref, c_ref, lo_ref, hi_ref, xlo_ref, xhi_ref, w1_ref, wb_ref, pool_ref, ct_ref, g1_ref,
    grad_ref, rim_ref, ft, dp, cp, corner, ct, g1, g2, a1, a2,
):
    for zone, (src, base, first, own, x0) in enumerate(((xlo_ref, 1, 4, 0, -4), (xhi_ref, 6, 0, 26, 26))):
        top = zone * ZONE
        corner[zone * 32 : zone * 32 + 32, :] = src[256:288, :].astype(F32)
        for n in range(6):
            at = (top + first + n) * DROW + 8
            dp[at : at + NYT, :] = d_ref[own + n].astype(F32)
        for k in range(3):
            lo = lo_ref[k * 32 : k * 32 + 32, :].astype(F32)
            hi = hi_ref[k * 32 : k * 32 + 32, :].astype(F32)
            dp[pl.ds((top + first) * DROW + 5 + k, 6, stride=DROW), :] = lo[own : own + 6]
            dp[pl.ds((top + first) * DROW + 8 + NYT + k, 6, stride=DROW), :] = hi[own : own + 6]
            at = (top + base + k) * DROW + 8
            dp[at : at + NYT, :] = src[k * 64 : k * 64 + 64, :].astype(F32)
        for side, y in ((0, 5), (1, 8 + NYT)):
            for ky in range(3):
                for kx in range(3):
                    row = (top + base + kx) * DROW + y + ky
                    at = zone * 32 + side * 9 + 3 * ky + kx
                    dp[row : row + 1, :] = corner[at : at + 1, :]
        ctop, cbase, cfirst, cown = zone * 4, zone * 3, 1 - zone, zone * 13
        for half in range(2):
            lanes = slice(half * 128, half * 128 + 128)
            for n in range(3):
                at = (ctop + cfirst + n) * CROW + 8
                cp[half, at : at + HY, :] = c_ref[cown + n, :, lanes].astype(F32)
            rows = slice(96 + half * 16, 112 + half * 16)
            for side, y in ((0, 7), (1, 8 + HY)):
                part = (lo_ref, hi_ref)[side][rows, :].astype(F32)[cown : cown + 3]
                cp[half, pl.ds((ctop + cfirst) * CROW + y, 3, stride=CROW), :] = part
                row = (ctop + cbase) * CROW + y
                at = zone * 32 + 18 + side * 2 + half
                cp[half, row : row + 1, :] = corner[at : at + 1, :]
            at = (ctop + cbase) * CROW + 8
            cp[half, at : at + HY, :] = src[192 + half * 32 : 224 + half * 32, :].astype(F32)
    layers = []
    for n in range(2 * ZONE):
        if n not in (0, 2 * ZONE - 1):
            layers.append((n * DROW, n % 2, n // 2 * HY))
    fine_taps(dp, ft, layers)
    coarse_taps(cp, ct, 8)
    cpatch = jnp.concatenate([coarse_patch(ct, 1, 2), coarse_patch(ct, 5, 2)], axis=0)
    back = dot_nt(wb_ref[...], cpatch).astype(BF16).astype(F32) * 0.125
    group = []
    for px in range(2):
        for py in range(2):
            group += [fine_patch(ft, 2, 2, px, py), fine_patch(ft, 6, 2, px, py)]
    group = jnp.concatenate(group, axis=0)
    pre = dot_nt(w1_ref[...], group)
    mean = pooled_sum(pre).astype(BF16)
    rim_ref[...] = mean
    g1[...] = g1_ref[...] + dot_nn(jnp.concatenate(back_through(pre, back), axis=1), group)
    pooled = jnp.concatenate([pool_ref[...], mean], axis=1)
    g2[...] = dot_nn(pooled, jnp.concatenate([coarse_patch(ct_ref, 1, 12), cpatch], axis=0))
    extract(g1, g2, grad_ref, a1, a2)


def feature_kernel(
    after_ref, up_ref, down_ref, lo_ref, hi_ref, xlo_ref, xhi_ref, ft_ref, pool_ref, rim_ref, w1_ref, w2_ref,
    feat_ref, token_ref, col, corner, rim, pp, pt,
):
    for k in range(3):
        col[k, 8:40, :] = lo_ref[k * 32 : k * 32 + 32, :].astype(F32)
        col[5 + k, 8:40, :] = hi_ref[k * 32 : k * 32 + 32, :].astype(F32)
    col[3, 8:40, :] = down_ref[0:32, :].astype(F32)
    col[4, 8:40, :] = up_ref[64:96, :].astype(F32)
    for src, row in ((xlo_ref, 5), (xhi_ref, 40)):
        corner[...] = src[...].astype(F32)
        for kx in range(3):
            for ky in range(3):
                col[ky, row + kx : row + kx + 1, :] = corner[256 + 3 * ky + kx : 257 + 3 * ky + kx, :]
                col[5 + ky, row + kx : row + kx + 1, :] = corner[265 + 3 * ky + kx : 266 + 3 * ky + kx, :]
            col[3, row + kx : row + kx + 1, :] = corner[kx * 64 : kx * 64 + 1, :]
            col[4, row + kx : row + kx + 1, :] = corner[kx * 64 + 63 : kx * 64 + 64, :]
    for px in range(2):
        for py in range(2):
            at = (px * 2 + py) * 128
            rim[at : at + 32, :] = fine_patch(ft_ref, 1, 1, px, py)
            rim[at + 32 : at + 64, :] = fine_patch(ft_ref, 8, 1, px, py)
            for side in range(2):
                for kx in range(3):
                    for ky in range(3):
                        rows = col[side * 4 + py + ky, pl.ds(5 + px + kx, 18, stride=2), :]
                        rows = jnp.concatenate([rows, jnp.zeros((14, 128), F32)], axis=0)
                        lane = (kx * 3 + ky) * 128
                        rim[at + 64 + side * 32 : at + 96 + side * 32, lane : lane + 128] = rows.astype(BF16)
    edge = pooled_sum(dot_nt(w1_ref[...], rim[...])).T.astype(BF16).astype(F32)
    inner = pool_ref[...].astype(F32).T
    outer = rim_ref[...].astype(F32).T
    for half in range(2):
        lanes = slice(half * 128, half * 128 + 128)
        pp[half, 8:40, :] = edge[0:32, lanes]
        pp[half, (HX + 1) * CROW + 8 : (HX + 1) * CROW + 40, :] = edge[32:64, lanes]
        for n, x in enumerate((0, 1, 14, 15)):
            pp[half, (x + 1) * CROW + 8 : (x + 1) * CROW + 40, :] = outer[n * 32 : n * 32 + 32, lanes]
        for n in range(12):
            pp[half, (n + 3) * CROW + 8 : (n + 3) * CROW + 40, :] = inner[n * 32 : n * 32 + 32, lanes]
        pp[half, pl.ds(7, 18, stride=CROW), :] = edge[64:82, lanes]
        pp[half, pl.ds(8 + HY, 18, stride=CROW), :] = edge[96:114, lanes]
    coarse_taps(pp, pt, HX + 2)
    feat = dot_nt(coarse_patch(pt, 1, HX), w2_ref[...])
    feat_ref[...] = feat.astype(BF16).reshape(HX, HY, 256)
    token_ref[...] = feat[0:8, 0:128]


def add_two_kernel(a_ref, b_ref, out_ref):
    out_ref[...] = (a_ref[...].astype(F32) + b_ref[...].astype(F32)).astype(BF16)


def add_four(refs):
    a, b, c, d = (ref[...].astype(F32) for ref in refs)
    return (a + b) + (c + d)


def add_four_kernel(a_ref, b_ref, c_ref, d_ref, after_ref, out_ref):
    out_ref[...] = add_four((a_ref, b_ref, c_ref, d_ref)).astype(BF16)


def final_kernel(a_ref, b_ref, c_ref, d_ref, g1_ref, g2_ref):
    total = add_four((a_ref, b_ref, c_ref, d_ref)) * 0.5
    for kd in range(3):
        for kx in range(3):
            for ky in range(3):
                t = kd * 9 + kx * 3 + ky
                at = ((kx * 3 + ky) * 3 + kd) * 16
                g1_ref[t] = total[16:20, at : at + 16]
                at = (((2 - kx) * 3 + 2 - ky) * 3 + kd) * 16
                g2_ref[t] = total[0:16, at : at + 16]


ANY = pl.BlockSpec(memory_space=pl.ANY)
VM = pl.BlockSpec(memory_space=pltpu.VMEM)


def call(kernel, ins, outs, scratch=(), limit=VMEM_LIMIT, flops=None):
    cost = None if flops is None else pl.CostEstimate(flops=flops, bytes_accessed=1_000_000, transcendentals=0)
    return pl.pallas_call(
        kernel,
        out_shape=outs,
        in_specs=ins,
        scratch_shapes=list(scratch),
        cost_estimate=cost,
        compiler_params=pltpu.CompilerParams(vmem_limit_bytes=limit),
    )


def struct(shape, kind):
    return jax.ShapeDtypeStruct(shape, kind)


def buffer(*shape):
    return pltpu.VMEM(shape, F32)


def buffer16(*shape):
    return pltpu.VMEM(shape, BF16)


def shift(value, axes, step):
    n = lax.axis_size(axes)
    return lax.ppermute(value, axes, [(i, (i + step) % n) for i in range(n)])


def partner(value, axes, bits):
    n = lax.axis_size(axes)
    return lax.ppermute(value, axes, [(i, i ^ bits) for i in range(n)])


TX = ("x", "yh")
TY = ("z", "core")


def on_device(density, kernel_one, kernel_two, cotangent):
    d, c = density[0], cotangent[0]
    k1 = jnp.transpose(kernel_one, (2, 3, 4, 1, 0)).reshape(27, CIN, CH)
    k2 = jnp.transpose(kernel_two, (2, 3, 4, 0, 1)).reshape(27, CH, CH)

    message = struct((128, 128), BF16)
    yup, ydown = call(
        pack_y_kernel,
        [ANY] * 2,
        (message, message),
        (
            buffer16(2, NXT, 16, 128), buffer16(2, HX, 16, 256),
            buffer(NXT * 16, 128), buffer(2, HX * 16, 128), pltpu.SemaphoreType.DMA((4,)),
        ),
        limit=VMEM_ALL,
        flops=FLOPS,
    )(d, c)
    lo, hi = shift(yup, TY, 1), shift(ydown, TY, -1)
    w1, wb, w2 = call(
        weights_kernel,
        [VM] * 2,
        (struct((512, 1152), BF16), struct((256, 2304), BF16), struct((256, 2304), BF16)),
        (buffer(128, 128), buffer(128, 128), buffer(16, 27 * 128), buffer(64, 2048), buffer(64, 2048)),
    )(k1, k2)
    message = struct((288, 128), BF16)
    up, down = call(
        pack_x_kernel,
        [VM] * 4 + [ANY],
        (message, message),
        (buffer(128, 128), buffer(128, 128), buffer(32, 128)),
    )(d, c, lo, hi, w1)
    xlo, xhi = shift(up, TX, 1), shift(down, TX, -1)

    pool, ct, g1 = call(
        inner_kernel,
        [VM] * 6,
        (struct((256, 384), BF16), struct((14 * HY, 768), BF16), struct((512, 1152), F32)),
        (buffer(26 * DROW, 128), buffer(2, 14 * CROW, 128), buffer16(2, 14 * HY, 512), buffer16(512, 1536)),
    )(d, c, lo, hi, w1, wb)
    grads, rim, ft = call(
        edge_kernel,
        [VM] * 11,
        (struct((32, 512), BF16), struct((256, 128), BF16), struct((2, 10 * HY, 512), BF16)),
        (
            buffer(2 * ZONE * DROW, 128), buffer(2, 8 * CROW, 128), buffer(64, 128), buffer16(8 * HY, 768),
            buffer(512, 1152), buffer(256, 2304), buffer(512, 128), buffer(512, 256),
        ),
    )(d, c, lo, hi, xlo, xhi, w1, wb, pool, ct, g1)

    grads = call(add_two_kernel, [VM] * 2, struct((32, 512), BF16))(grads, partner(grads, "core", 1))
    feat, token = call(
        feature_kernel,
        [ANY] + [VM] * 11,
        (struct((HX, HY, 256), BF16), struct((8, 128), F32)),
        (
            buffer(8, 48, 128), buffer(288, 128), buffer16(512, 1152),
            buffer(2, (HX + 2) * CROW, 128), buffer16((HX + 2) * HY, 768),
        ),
    )(grads, yup, ydown, lo, hi, xlo, xhi, ft, pool, rim, w1, w2)
    after = w1
    for axes in ("z", "x"):
        others = [partner(grads, axes, bits) for bits in (1, 2, 3)]
        grads = call(add_four_kernel, [VM] * 4 + [ANY], struct((32, 512), BF16))(grads, *others, after)
        after = token
    near = partner(grads, "rep", 1)
    far, across = partner(grads, "yh", 1), partner(grads, ("rep", "yh"), 3)
    g1, g2 = call(final_kernel, [VM] * 4, (struct((27, CIN, CH), F32), struct((27, CH, CH), F32)))(
        grads, near, far, across
    )
    g1 = jnp.transpose(g1.reshape(3, 3, 3, CIN, CH), (4, 3, 0, 1, 2))
    g2 = jnp.transpose(g2.reshape(3, 3, 3, CH, CH), (3, 4, 0, 1, 2))
    return feat[None], g1, g2


def solution(mesh):
    fine = Mesh(mesh.devices.reshape(2, 4, 2, 4, 2), ("rep", "x", "yh", "z", "core"))
    tiles = P("rep", TX, TY, None)
    return jax.shard_map(
        on_device, mesh=fine, in_specs=(tiles, P(), P(), tiles), out_specs=(tiles, P(), P()), check_vma=False
    )
```

time: 1270 us -> 48.5 us (0.04)
  matrix products: 517 us -> 0 us
  blocking collectives: 340 us -> 0 us
  local copies, waits for them, and re-layouts: 285 us -> 0.02 us
  other arithmetic: 95 us -> 0 us
  Pallas kernels: 0 us -> 16.8 us
    conv_general_dilated x5 -> x0, matrix products: 517 us -> none  [convolve(): lax.conv_general_dilated(lhs, rhs, (1, 1, 1), 'VALID', dimension_numbers=...]
    psum x2 -> x0, blocking collectives: 340 us -> none  [the longest x1 332 us: on_device(): tile_one, tile_two = lax.psum((slab_one, slab_two), ('tx', 'ty'))]
    reshape x8 -> x0, local copies, waits for them, and re-layouts: 123 us -> none  [the longest x7 92.8 us: unpack(): field.reshape(s, x, y, channels, merged // channels)]
    conv_general_dilated x7 -> x0, local copies, waits for them, and re-layouts: 59.8 us -> none  [convolve(): lax.conv_general_dilated(lhs, rhs, (1, 1, 1), 'VALID', dimension_numbers=...]
    unnamed x43 -> x12, local copies, waits for them, and re-layouts: 48.5 us -> 0.02 us
    convert_element_type x1 -> x0, other arithmetic: 27.8 us -> none  [on_device(): (upsample(back_pooled.astype(jnp.float32)) * 0.125 * slope).astype(jnp.bf...]
    reduce_sum x1 -> x0, other arithmetic: 25.2 us -> none  [pooling(): return jnp.mean(blocks, axis=(3, 5, 7))]
    select_n x1 -> x0, other arithmetic: 17.8 us -> none  [on_device(): slope = jnp.where(pre > 0, 1.0, leak_slope).astype(jnp.float32)]
  transfers between devices with their start and end apart: 12 -> 14, of which waited for: 0 -> 8; matrix products, arithmetic and copies ran while one was open for 63% -> 0% of each run, Pallas kernels for 0% -> 22%
where the time goes in v2:
time: 48.5 us; the launch traced here: 48.3 us
  starting transfers between devices  21.9 us (45%)
  Pallas kernels  16.8 us (35%)
  waiting for transfers between devices  8.86 us (18%)
  between operations  0.74 us (2%)
    ppermute x10, starting transfers between devices, partner(): return lax.ppermute(value, axes, [(i, i ^ bits) for i in range(n)])  12.6 us
    ppermute x4, starting transfers between devices, shift(): return lax.ppermute(value, axes, [(i, (i + step) % n) for i in range(n)])  9.3 us
    ppermute x10, waiting for transfers between devices, partner(): return lax.ppermute(value, axes, [(i, i ^ bits) for i in range(n)])  8.57 us
    pallas_call x1, Pallas kernels, on_device(): call(inner_kernel, [VM] * 6, (struct((256, 384), BF16), struct((14 * HY,...  5.23 us
    pallas_call x1, Pallas kernels, on_device(): call(feature_kernel, [ANY] + [VM] * 11, (struct((HX, HY, 256), BF16), str...  3.62 us
    pallas_call x1, Pallas kernels, on_device(): call(edge_kernel, [VM] * 11, (struct((32, 512), BF16), struct((256, 128),...  3.52 us
    pallas_call x1, Pallas kernels, on_device(): call(pack_y_kernel, [ANY] * 2, (message, message), (buffer16(2, NXT, 16,...  1.91 us
    pallas_call x1, Pallas kernels, on_device(): call(weights_kernel, [VM] * 2, (struct((512, 1152), BF16), struct((256, 2...  1.61 us
  transfers between devices with their start and end apart: 14, of which 8 were waited for; matrix products, arithmetic and copies ran while one was open for 0% of the time, Pallas kernels for 22%

profile of v2, /device:TPU:0, one launch (start us, length us, event | category | flops | bytes accessed | tf_op | source)
XLA Modules:
  0.0 48.3 jit_solution(13935979313185899789)
XLA Ops:
  0.7 1.9 %shard_map.67 = (bf16[128,128]{1,0:T(8,128)(2,1)}, bf16[128,128]{1,0:T(8,128)(2,1)}) custom-call(bf16[32,64,128]{2,1,0:T(8,128)(2,1)} %bitcast.15, bf16[16,32,256]{2,1,0:T(8,128)(2,1)} %bitcast.19), custom_call_target="tpu_custom_call" | custom-call | flops 5000000000 | bytes 1000000 | tf_op jit(solution)/shard_map/pallas_call | solution.py:416
  2.6 3.6 %collective-permute-start.1 = (bf16[128,128]{1,0:T(8,128)(2,1)}, bf16[128,128]{1,0:T(8,128)(2,1)S(1)}, u32[]{:S(2)}, u32[]{:S(2)}) collective-permute-start(bf16[128,128]{1,0:T(8,128)(2,1)} %get-tuple-element.21.down_ref), channel_id=1, source_target_pairs={{0,7},{1,0},{2,1},{3,2},{4,3},{5,4},{6,5},{7,6},{8,15},{9,8},{10,9... | collective-permute-start | bytes 98312 | tf_op jit(solution)/shard_map/ppermute | solution.py:398
  6.2 1.6 %shard_map.68 = (bf16[512,1152]{1,0:T(8,128)(2,1)S(1)}, bf16[256,2304]{1,0:T(8,128)(2,1)S(1)}, bf16[256,2304]{1,0:T(8,128)(2,1)S(1)}) custom-call(bf16[27,4,16]{2,1,0:T(4,128)(2,1)S(1)} %bitcast.24, bf16[27,16,16]{2,1,0:T(8,128)(2,1)S(1)} %bitcast.23), custom_call_target="tpu_custom_call" | custom-call | tf_op jit(solution)/shard_map/pallas_call | solution.py:428
  8.1 3.3 %collective-permute-start.2 = (bf16[288,128]{1,0:T(8,128)(2,1)S(1)}, bf16[288,128]{1,0:T(8,128)(2,1)S(1)}, u32[]{:S(2)}, u32[]{:S(2)}) collective-permute-start(bf16[288,128]{1,0:T(8,128)(2,1)S(1)} %get-tuple-element.23), channel_id=1, source_target_pairs={{0,8},{8,16},{16,24},{24,32},{32,40},{40,48},{48,56},{56,0},{1,9},... | collective-permute-start | bytes 221192 | tf_op jit(solution)/shard_map/ppermute | solution.py:398
  11.4 2.4 %collective-permute-start.3 = (bf16[288,128]{1,0:T(8,128)(2,1)S(1)}, bf16[288,128]{1,0:T(8,128)(2,1)S(1)}, u32[]{:S(2)}, u32[]{:S(2)}) collective-permute-start(bf16[288,128]{1,0:T(8,128)(2,1)S(1)} %get-tuple-element.24), channel_id=1, source_target_pairs={{0,56},{8,0},{16,8},{24,16},{32,24},{40,32},{48,40},{56,48},{1,57}... | collective-permute-start | bytes 221192 | tf_op jit(solution)/shard_map/ppermute | solution.py:398
  13.9 5.2 %shard_map.70 = (bf16[256,384]{1,0:T(8,128)(2,1)S(1)}, bf16[448,768]{1,0:T(8,128)(2,1)S(1)}, f32[512,1152]{1,0:T(8,128)S(1)}) custom-call(bf16[32,64,128]{2,1,0:T(8,128)(2,1)S(1)} %bitcast.17, bf16[16,32,256]{2,1,0:T(8,128)(2,1)S(1)} %bitcast.21, bf16[128,128]{1,0:T(8,128)(2,1)S(1)} %collective-permute-done.lo_ref, ...), custom_call_target="tpu_custom_call" | custom-call | tf_op jit(solution)/shard_map/pallas_call | solution.py:443
  19.1 3.5 %shard_map.71 = (bf16[32,512]{1,0:T(8,128)(2,1)S(1)}, bf16[256,128]{1,0:T(8,128)(2,1)S(1)}, bf16[2,320,512]{2,1,0:T(8,128)(2,1)S(1)}) custom-call(bf16[32,64,128]{2,1,0:T(8,128)(2,1)S(1)} %bitcast.18, bf16[16,32,256]{2,1,0:T(8,128)(2,1)S(1)} %bitcast.22, bf16[128,128]{1,0:T(8,128)(2,1)S(1)} %collective-permute-done.lo_ref, ...), custom_call_target="tpu_custom_call" | custom-call | tf_op jit(solution)/shard_map/pallas_call | solution.py:449
  22.7 1.2 %collective-permute-done.4.b_ref = bf16[32,512]{1,0:T(8,128)(2,1)S(1)} collective-permute-done((bf16[32,512]{1,0:T(8,128)(2,1)S(1)}, bf16[32,512]{1,0:T(8,128)(2,1)S(1)}, u32[]{:S(2)}, u32[]{:S(2)}) %collective-permute-start.4) | collective-permute-done | bytes 32800 | tf_op jit(solution)/shard_map/ppermute | solution.py:403
  23.9 2.5 %collective-permute-start.7 = (bf16[32,512]{1,0:T(8,128)(2,1)S(1)}, bf16[32,512]{1,0:T(8,128)(2,1)S(1)}, u32[]{:S(2)}, u32[]{:S(2)}) collective-permute-start(bf16[32,512]{1,0:T(8,128)(2,1)S(1)} %shard_map.72.after_ref.a_ref), channel_id=1, source_target_pairs={{0,6},{2,4},{4,2},{6,0},{1,7},{3,5},{5,3},{7,1},{8,14},{10,12},{12... | collective-permute-start | bytes 98312 | tf_op jit(solution)/shard_map/ppermute | solution.py:403
  26.4 0.9 %collective-permute-start.6 = (bf16[32,512]{1,0:T(8,128)(2,1)S(1)}, bf16[32,512]{1,0:T(8,128)(2,1)S(1)}, u32[]{:S(2)}, u32[]{:S(2)}) collective-permute-start(bf16[32,512]{1,0:T(8,128)(2,1)S(1)} %shard_map.72.after_ref.a_ref), channel_id=1, source_target_pairs={{0,4},{2,6},{4,0},{6,2},{1,5},{3,7},{5,1},{7,3},{8,12},{10,14},{12... | collective-permute-start | bytes 98312 | tf_op jit(solution)/shard_map/ppermute | solution.py:403
  27.4 0.7 %collective-permute-start.5 = (bf16[32,512]{1,0:T(8,128)(2,1)S(1)}, bf16[32,512]{1,0:T(8,128)(2,1)S(1)}, u32[]{:S(2)}, u32[]{:S(2)}) collective-permute-start(bf16[32,512]{1,0:T(8,128)(2,1)S(1)} %shard_map.72.after_ref.a_ref), channel_id=1, source_target_pairs={{0,2},{2,0},{4,6},{6,4},{1,3},{3,1},{5,7},{7,5},{8,10},{10,8},{12,... | collective-permute-start | bytes 98312 | tf_op jit(solution)/shard_map/ppermute | solution.py:403
  28.1 1.0 %collective-permute-done.7.d_ref = bf16[32,512]{1,0:T(8,128)(2,1)S(1)} collective-permute-done((bf16[32,512]{1,0:T(8,128)(2,1)S(1)}, bf16[32,512]{1,0:T(8,128)(2,1)S(1)}, u32[]{:S(2)}, u32[]{:S(2)}) %collective-permute-start.7) | collective-permute-done | bytes 32800 | tf_op jit(solution)/shard_map/ppermute | solution.py:403
  29.1 3.0 %collective-permute-done.6.c_ref = bf16[32,512]{1,0:T(8,128)(2,1)S(1)} collective-permute-done((bf16[32,512]{1,0:T(8,128)(2,1)S(1)}, bf16[32,512]{1,0:T(8,128)(2,1)S(1)}, u32[]{:S(2)}, u32[]{:S(2)}) %collective-permute-start.6) | collective-permute-done | bytes 32800 | tf_op jit(solution)/shard_map/ppermute | solution.py:403
  32.1 1.5 %collective-permute-start.10 = (bf16[32,512]{1,0:T(8,128)(2,1)S(1)}, bf16[32,512]{1,0:T(8,128)(2,1)S(1)}, u32[]{:S(2)}, u32[]{:S(2)}) collective-permute-start(bf16[32,512]{1,0:T(8,128)(2,1)S(1)} %shard_map.74.a_ref), channel_id=1, source_target_pairs={{0,48},{16,32},{32,16},{48,0},{1,49},{17,33},{33,17},{49,1},{2,50}... | collective-permute-start | bytes 98312 | tf_op jit(solution)/shard_map/ppermute | solution.py:403
  33.7 0.8 %collective-permute-start.9 = (bf16[32,512]{1,0:T(8,128)(2,1)S(1)}, bf16[32,512]{1,0:T(8,128)(2,1)S(1)}, u32[]{:S(2)}, u32[]{:S(2)}) collective-permute-start(bf16[32,512]{1,0:T(8,128)(2,1)S(1)} %shard_map.74.a_ref), channel_id=1, source_target_pairs={{0,32},{16,48},{32,0},{48,16},{1,33},{17,49},{33,1},{49,17},{2,34}... | collective-permute-start | bytes 98312 | tf_op jit(solution)/shard_map/ppermute | solution.py:403
  34.4 1.9 %collective-permute-start.8 = (bf16[32,512]{1,0:T(8,128)(2,1)S(1)}, bf16[32,512]{1,0:T(8,128)(2,1)S(1)}, u32[]{:S(2)}, u32[]{:S(2)}) collective-permute-start(bf16[32,512]{1,0:T(8,128)(2,1)S(1)} %shard_map.74.a_ref), channel_id=1, source_target_pairs={{0,16},{16,0},{32,48},{48,32},{1,17},{17,1},{33,49},{49,33},{2,18}... | collective-permute-start | bytes 98312 | tf_op jit(solution)/shard_map/ppermute | solution.py:403
  36.3 3.6 %shard_map.73 = (bf16[16,32,256]{2,1,0:T(8,128)(2,1)}, f32[8,128]{1,0:T(8,128)S(1)}) custom-call(bf16[32,512]{1,0:T(8,128)(2,1)S(1)} %shard_map.72.after_ref.a_ref, bf16[128,128]{1,0:T(8,128)(2,1)S(1)} %copy-done.3, bf16[128,128]{1,0:T(8,128)(2,1)S(1)} %copy-done.4, bf16[128,128]{1,0:T(8,128)(2,1)S(1)} %collective-permute-done.lo_ref, ...), custom_call_target="tpu_custom_call" | custom-call | tf_op jit(solution)/shard_map/pallas_call | solution.py:460
  40.0 1.9 %collective-permute-start.13 = (bf16[32,512]{1,0:T(8,128)(2,1)S(1)}, bf16[32,512]{1,0:T(8,128)(2,1)S(1)}, u32[]{:S(2)}, u32[]{:S(2)}) collective-permute-start(bf16[32,512]{1,0:T(8,128)(2,1)S(1)} %shard_map.75.a_ref), channel_id=1, source_target_pairs={{0,72},{8,64},{64,8},{72,0},{1,73},{9,65},{65,9},{73,1},{2,74},{10... | collective-permute-start | bytes 98312 | tf_op jit(solution)/shard_map/ppermute | solution.py:403
  41.8 1.8 %collective-permute-start.12 = (bf16[32,512]{1,0:T(8,128)(2,1)S(1)}, bf16[32,512]{1,0:T(8,128)(2,1)S(1)}, u32[]{:S(2)}, u32[]{:S(2)}) collective-permute-start(bf16[32,512]{1,0:T(8,128)(2,1)S(1)} %shard_map.75.a_ref), channel_id=1, source_target_pairs={{0,8},{8,0},{1,9},{9,1},{2,10},{10,2},{3,11},{11,3},{4,12},{12,4},... | collective-permute-start | bytes 98312 | tf_op jit(solution)/shard_map/ppermute | solution.py:403
  43.6 0.6 %collective-permute-start.11 = (bf16[32,512]{1,0:T(8,128)(2,1)S(1)}, bf16[32,512]{1,0:T(8,128)(2,1)S(1)}, u32[]{:S(2)}, u32[]{:S(2)}) collective-permute-start(bf16[32,512]{1,0:T(8,128)(2,1)S(1)} %shard_map.75.a_ref), channel_id=1, source_target_pairs={{0,64},{64,0},{1,65},{65,1},{2,66},{66,2},{3,67},{67,3},{4,68},{68... | collective-permute-start | bytes 98312 | tf_op jit(solution)/shard_map/ppermute | solution.py:403
  44.1 1.0 %collective-permute-done.13.d_ref = bf16[32,512]{1,0:T(8,128)(2,1)S(1)} collective-permute-done((bf16[32,512]{1,0:T(8,128)(2,1)S(1)}, bf16[32,512]{1,0:T(8,128)(2,1)S(1)}, u32[]{:S(2)}, u32[]{:S(2)}) %collective-permute-start.13) | collective-permute-done | bytes 32800 | tf_op jit(solution)/shard_map/ppermute | solution.py:403
  45.2 2.1 %collective-permute-done.12.c_ref = bf16[32,512]{1,0:T(8,128)(2,1)S(1)} collective-permute-done((bf16[32,512]{1,0:T(8,128)(2,1)S(1)}, bf16[32,512]{1,0:T(8,128)(2,1)S(1)}, u32[]{:S(2)}, u32[]{:S(2)}) %collective-permute-start.12) | collective-permute-done | bytes 32800 | tf_op jit(solution)/shard_map/ppermute | solution.py:403
  47.2 0.3 collective-permute-done.11.b_ref
  47.5 0.8 %shard_map.76 = (f32[27,4,16]{2,1,0:T(4,128)}, f32[27,16,16]{2,1,0:T(8,128)}) custom-call(bf16[32,512]{1,0:T(8,128)(2,1)S(1)} %shard_map.75.a_ref, bf16[32,512]{1,0:T(8,128)(2,1)S(1)} %collective-permute-done.11.b_ref, bf16[32,512]{1,0:T(8,128)(2,1)S(1)} %collective-permute-done.12.c_ref, bf16[32,512]{1,0:T(8,128)(2,1)S(1)} %collective-permute-done.13.d_ref), custom_call_target="tpu_custom_call" | custom-call | tf_op jit(solution)/shard_map/pallas_call | solution.py:476
  (26 shorter events, 0.5 us)
Async XLA Ops:
  0.6 5.6 %copy-start.2 = (bf16[16,16,3,3,3]{1,0,4,3,2:T(8,128)(2,1)S(1)}, bf16[16,16,3,3,3]{1,0,4,3,2:T(8,128)(2,1)}, u32[]{:S(2)}) copy-start(bf16[16,16,3,3,3]{1,0,4,3,2:T(8,128)(2,1)} %param.6) | copy-start | bytes 41476
  0.6 5.6 %copy-start.5 = (bf16[16,4,3,3,3]{0,1,4,3,2:T(4,128)(2,1)S(1)}, bf16[16,4,3,3,3]{0,1,4,3,2:T(4,128)(2,1)}, u32[]{:S(2)}) copy-start(bf16[16,4,3,3,3]{0,1,4,3,2:T(4,128)(2,1)} %param.5) | copy-start | bytes 10372
  0.7 7.5 %copy-start = (bf16[1,32,64,128]{3,2,1,0:T(8,128)(2,1)S(1)}, bf16[1,32,64,128]{3,2,1,0:T(8,128)(2,1)}, u32[]{:S(2)}) copy-start(bf16[1,32,64,128]{3,2,1,0:T(8,128)(2,1)} %param.4) | copy-start | bytes 1572868
  0.7 7.4 %copy-start.1 = (bf16[1,16,32,256]{3,2,1,0:T(8,128)(2,1)S(1)}, bf16[1,16,32,256]{3,2,1,0:T(8,128)(2,1)}, u32[]{:S(2)}) copy-start(bf16[1,16,32,256]{3,2,1,0:T(8,128)(2,1)} %param.7) | copy-start | bytes 786436
  2.6 5.4 %collective-permute-start = (bf16[128,128]{1,0:T(8,128)(2,1)}, bf16[128,128]{1,0:T(8,128)(2,1)S(1)}, u32[]{:S(2)}, u32[]{:S(2)}) collective-permute-start(bf16[128,128]{1,0:T(8,128)(2,1)} %get-tuple-element.20.up_ref), channel_id=1, source_target_pairs={{0,1},{1,2},{2,3},{3,4},{4,5},{5,6},{6,7},{7,0},{8,9},{9,10},{10,1... | collective-permute-start | bytes 98312 | tf_op jit(solution)/shard_map/ppermute | solution.py:398
  2.6 5.5 %collective-permute-start.1 = (bf16[128,128]{1,0:T(8,128)(2,1)}, bf16[128,128]{1,0:T(8,128)(2,1)S(1)}, u32[]{:S(2)}, u32[]{:S(2)}) collective-permute-start(bf16[128,128]{1,0:T(8,128)(2,1)} %get-tuple-element.21.down_ref), channel_id=1, source_target_pairs={{0,7},{1,0},{2,1},{3,2},{4,3},{5,4},{6,5},{7,6},{8,15},{9,8},{10,9... | collective-permute-start | bytes 98312 | tf_op jit(solution)/shard_map/ppermute | solution.py:398
  8.1 10.9 %collective-permute-start.2 = (bf16[288,128]{1,0:T(8,128)(2,1)S(1)}, bf16[288,128]{1,0:T(8,128)(2,1)S(1)}, u32[]{:S(2)}, u32[]{:S(2)}) collective-permute-start(bf16[288,128]{1,0:T(8,128)(2,1)S(1)} %get-tuple-element.23), channel_id=1, source_target_pairs={{0,8},{8,16},{16,24},{24,32},{32,40},{40,48},{48,56},{56,0},{1,9},... | collective-permute-start | bytes 221192 | tf_op jit(solution)/shard_map/ppermute | solution.py:398
  11.4 7.7 %collective-permute-start.3 = (bf16[288,128]{1,0:T(8,128)(2,1)S(1)}, bf16[288,128]{1,0:T(8,128)(2,1)S(1)}, u32[]{:S(2)}, u32[]{:S(2)}) collective-permute-start(bf16[288,128]{1,0:T(8,128)(2,1)S(1)} %get-tuple-element.24), channel_id=1, source_target_pairs={{0,56},{8,0},{16,8},{24,16},{32,24},{40,32},{48,40},{56,48},{1,57}... | collective-permute-start | bytes 221192 | tf_op jit(solution)/shard_map/ppermute | solution.py:398
  22.6 13.7 %copy-start.3 = (bf16[128,128]{1,0:T(8,128)(2,1)S(1)}, bf16[128,128]{1,0:T(8,128)(2,1)}, u32[]{:S(2)}) copy-start(bf16[128,128]{1,0:T(8,128)(2,1)} %get-tuple-element.20.up_ref) | copy-start | bytes 98308
  22.6 13.7 %copy-start.4 = (bf16[128,128]{1,0:T(8,128)(2,1)S(1)}, bf16[128,128]{1,0:T(8,128)(2,1)}, u32[]{:S(2)}) copy-start(bf16[128,128]{1,0:T(8,128)(2,1)} %get-tuple-element.21.down_ref) | copy-start | bytes 98308
  22.6 1.3 %collective-permute-start.4 = (bf16[32,512]{1,0:T(8,128)(2,1)S(1)}, bf16[32,512]{1,0:T(8,128)(2,1)S(1)}, u32[]{:S(2)}, u32[]{:S(2)}) collective-permute-start(bf16[32,512]{1,0:T(8,128)(2,1)S(1)} %get-tuple-element.29.a_ref), channel_id=1, source_target_pairs={{0,1},{1,0},{2,3},{3,2},{4,5},{5,4},{6,7},{7,6},{8,9},{9,8},{10,11... | collective-permute-start | bytes 98312 | tf_op jit(solution)/shard_map/ppermute | solution.py:403
  23.9 5.2 %collective-permute-start.7 = (bf16[32,512]{1,0:T(8,128)(2,1)S(1)}, bf16[32,512]{1,0:T(8,128)(2,1)S(1)}, u32[]{:S(2)}, u32[]{:S(2)}) collective-permute-start(bf16[32,512]{1,0:T(8,128)(2,1)S(1)} %shard_map.72.after_ref.a_ref), channel_id=1, source_target_pairs={{0,6},{2,4},{4,2},{6,0},{1,7},{3,5},{5,3},{7,1},{8,14},{10,12},{12... | collective-permute-start | bytes 98312 | tf_op jit(solution)/shard_map/ppermute | solution.py:403
  26.4 5.7 %collective-permute-start.6 = (bf16[32,512]{1,0:T(8,128)(2,1)S(1)}, bf16[32,512]{1,0:T(8,128)(2,1)S(1)}, u32[]{:S(2)}, u32[]{:S(2)}) collective-permute-start(bf16[32,512]{1,0:T(8,128)(2,1)S(1)} %shard_map.72.after_ref.a_ref), channel_id=1, source_target_pairs={{0,4},{2,6},{4,0},{6,2},{1,5},{3,7},{5,1},{7,3},{8,12},{10,14},{12... | collective-permute-start | bytes 98312 | tf_op jit(solution)/shard_map/ppermute | solution.py:403
  27.4 4.8 %collective-permute-start.5 = (bf16[32,512]{1,0:T(8,128)(2,1)S(1)}, bf16[32,512]{1,0:T(8,128)(2,1)S(1)}, u32[]{:S(2)}, u32[]{:S(2)}) collective-permute-start(bf16[32,512]{1,0:T(8,128)(2,1)S(1)} %shard_map.72.after_ref.a_ref), channel_id=1, source_target_pairs={{0,2},{2,0},{4,6},{6,4},{1,3},{3,1},{5,7},{7,5},{8,10},{10,8},{12,... | collective-permute-start | bytes 98312 | tf_op jit(solution)/shard_map/ppermute | solution.py:403
  32.1 7.8 %collective-permute-start.10 = (bf16[32,512]{1,0:T(8,128)(2,1)S(1)}, bf16[32,512]{1,0:T(8,128)(2,1)S(1)}, u32[]{:S(2)}, u32[]{:S(2)}) collective-permute-start(bf16[32,512]{1,0:T(8,128)(2,1)S(1)} %shard_map.74.a_ref), channel_id=1, source_target_pairs={{0,48},{16,32},{32,16},{48,0},{1,49},{17,33},{33,17},{49,1},{2,50}... | collective-permute-start | bytes 98312 | tf_op jit(solution)/shard_map/ppermute | solution.py:403
  33.7 6.3 %collective-permute-start.9 = (bf16[32,512]{1,0:T(8,128)(2,1)S(1)}, bf16[32,512]{1,0:T(8,128)(2,1)S(1)}, u32[]{:S(2)}, u32[]{:S(2)}) collective-permute-start(bf16[32,512]{1,0:T(8,128)(2,1)S(1)} %shard_map.74.a_ref), channel_id=1, source_target_pairs={{0,32},{16,48},{32,0},{48,16},{1,33},{17,49},{33,1},{49,17},{2,34}... | collective-permute-start | bytes 98312 | tf_op jit(solution)/shard_map/ppermute | solution.py:403
  34.4 5.5 %collective-permute-start.8 = (bf16[32,512]{1,0:T(8,128)(2,1)S(1)}, bf16[32,512]{1,0:T(8,128)(2,1)S(1)}, u32[]{:S(2)}, u32[]{:S(2)}) collective-permute-start(bf16[32,512]{1,0:T(8,128)(2,1)S(1)} %shard_map.74.a_ref), channel_id=1, source_target_pairs={{0,16},{16,0},{32,48},{48,32},{1,17},{17,1},{33,49},{49,33},{2,18}... | collective-permute-start | bytes 98312 | tf_op jit(solution)/shard_map/ppermute | solution.py:403
  40.0 5.2 %collective-permute-start.13 = (bf16[32,512]{1,0:T(8,128)(2,1)S(1)}, bf16[32,512]{1,0:T(8,128)(2,1)S(1)}, u32[]{:S(2)}, u32[]{:S(2)}) collective-permute-start(bf16[32,512]{1,0:T(8,128)(2,1)S(1)} %shard_map.75.a_ref), channel_id=1, source_target_pairs={{0,72},{8,64},{64,8},{72,0},{1,73},{9,65},{65,9},{73,1},{2,74},{10... | collective-permute-start | bytes 98312 | tf_op jit(solution)/shard_map/ppermute | solution.py:403
  41.8 5.4 %collective-permute-start.12 = (bf16[32,512]{1,0:T(8,128)(2,1)S(1)}, bf16[32,512]{1,0:T(8,128)(2,1)S(1)}, u32[]{:S(2)}, u32[]{:S(2)}) collective-permute-start(bf16[32,512]{1,0:T(8,128)(2,1)S(1)} %shard_map.75.a_ref), channel_id=1, source_target_pairs={{0,8},{8,0},{1,9},{9,1},{2,10},{10,2},{3,11},{11,3},{4,12},{12,4},... | collective-permute-start | bytes 98312 | tf_op jit(solution)/shard_map/ppermute | solution.py:403
  43.6 3.9 %collective-permute-start.11 = (bf16[32,512]{1,0:T(8,128)(2,1)S(1)}, bf16[32,512]{1,0:T(8,128)(2,1)S(1)}, u32[]{:S(2)}, u32[]{:S(2)}) collective-permute-start(bf16[32,512]{1,0:T(8,128)(2,1)S(1)} %shard_map.75.a_ref), channel_id=1, source_target_pairs={{0,64},{64,0},{1,65},{65,1},{2,66},{66,2},{3,67},{67,3},{4,68},{68... | collective-permute-start | bytes 98312 | tf_op jit(solution)/shard_map/ppermute | solution.py:403

commit v3 on v2

v3 whole, which is shorter than its diff:
```python
import jax
import jax.numpy as jnp
from jax import lax
from jax.experimental import pallas as pl
from jax.experimental.pallas import tpu as pltpu
from jax.sharding import Mesh
from jax.sharding import PartitionSpec as P

CIN = 4
CH = 16
LEAK = 0.3
F32 = jnp.float32
BF16 = jnp.bfloat16
NXT = 32
NYT = 64
HX = NXT // 2
HY = NYT // 2
DROW = 80
CROW = 48
INNER = tuple(range(2, HX - 2))
OUTER = (0, 1, HX - 2, HX - 1)
VMEM_LIMIT = 32 * 1024 * 1024
FLOPS = 5_000_000_000
VMEM_ALL = 60 * 1024 * 1024


def dot_nt(lhs, rhs):
    return lax.dot_general(lhs, rhs, (((1,), (1,)), ((), ())), preferred_element_type=F32)


def dot_nn(lhs, rhs):
    return lax.dot_general(lhs, rhs, (((1,), (0,)), ((), ())), preferred_element_type=F32)


def iota(shape, dim):
    return lax.broadcasted_iota(jnp.int32, shape, dim)


def pack_y_kernel(d_hbm, c_hbm, up_ref, down_ref, db, cb, ds, cs, sem):
    copies = []
    for low in range(2):
        at, cat = (NYT - 16, HY - 16) if low == 0 else (0, 0)
        copies.append(pltpu.make_async_copy(d_hbm.at[:, pl.ds(at, 16), :], db.at[low], sem.at[2 * low]))
        copies.append(pltpu.make_async_copy(c_hbm.at[:, pl.ds(cat, 16), :], cb.at[low], sem.at[2 * low + 1]))
    for copy in copies:
        copy.start()
    for copy in copies:
        copy.wait()
    for low, out, row, crow in ((0, up_ref, 13, 15), (1, down_ref, 0, 0)):
        ds[...] = db[low].astype(F32).reshape(NXT * 16, 128)
        for half in range(2):
            cs[half] = cb[low, :, :, half * 128 : half * 128 + 128].astype(F32).reshape(HX * 16, 128)
        for k in range(3):
            out[k * 32 : k * 32 + 32, :] = ds[pl.ds(row + k, 32, stride=16), :].astype(BF16)
        for half in range(2):
            edge = cs[half, pl.ds(crow, 16, stride=16), :]
            out[96 + half * 16 : 112 + half * 16, :] = edge.astype(BF16)


def pack_x_kernel(d_ref, c_ref, lo_ref, hi_ref, after_ref, also_ref, up_ref, down_ref, ls, hs, ms):
    ls[...] = lo_ref[...].astype(F32)
    hs[...] = hi_ref[...].astype(F32)
    for out, x, cx in ((down_ref, 0, 0), (up_ref, NXT - 3, HX - 1)):
        out[0:192, :] = d_ref[x : x + 3, :, :].reshape(192, 128)
        out[192:224, :] = c_ref[cx, :, 0:128]
        out[224:256, :] = c_ref[cx, :, 128:256]
        for side, src in enumerate((ls, hs)):
            for k in range(3):
                ms[side * 9 + 3 * k : side * 9 + 3 * k + 3, :] = src[k * 32 + x : k * 32 + x + 3, :]
            for half in range(2):
                at = 18 + side * 2 + half
                ms[at : at + 1, :] = src[96 + half * 16 + cx : 97 + half * 16 + cx, :]
        ms[22:32, :] = jnp.zeros((10, 128), F32)
        out[256:288, :] = ms[...].astype(BF16)


def weights_kernel(k1_ref, k2_ref, w1_ref, wb_ref, s1, c1, cb):
    for t in range(27):
        s1[4 * t : 4 * t + 4, 0:CH] = k1_ref[t].astype(F32)
    s1[108:128, :] = jnp.zeros((20, 128), F32)
    k1t = s1[...].T[0:CH].astype(BF16)
    rep1 = (iota((128, 27 * 128), 0) == iota((128, 27 * 128), 1) // 32).astype(BF16)
    c1[...] = dot_nn(k1t, rep1)
    groups = []
    for g in range(4):
        for j in range(8):
            if g * 8 + j < 27:
                s1[j * 16 : j * 16 + 16, 0:CH] = k2_ref[g * 8 + j].astype(F32)
        groups.append(s1[...].T[0:CH])
    rep2 = (iota((128, 2048), 0) == iota((128, 2048), 1) // 16).astype(BF16)
    cb[...] = dot_nn(jnp.concatenate(groups, axis=0).astype(BF16), rep2)

    depth1 = iota((16, 128), 1) % 32
    depth2 = iota((16, 256), 1) % 16
    for kx in range(3):
        for ky in range(3):
            ts = [kd * 9 + kx * 3 + ky for kd in range(3)]
            at = (kx * 3 + ky) * 128
            ones = [c1[:, t * 128 : t * 128 + 128] for t in ts]
            for d in range(32):
                acc = jnp.zeros((16, 128), F32)
                for kd in range(3):
                    acc = jnp.where(depth1 == d + kd - 1, ones[kd], acc)
                row = (d % 2) * 256 + (d // 2) * 16
                w1_ref[row : row + 16, at : at + 128] = acc.astype(BF16)
            at = ((2 - kx) * 3 + 2 - ky) * 256
            backs = [cb[t // 8 * 16 : t // 8 * 16 + 16, t % 8 * 256 : t % 8 * 256 + 256] for t in ts]
            for d in range(16):
                acc = jnp.zeros((16, 256), F32)
                for kd in range(3):
                    acc = jnp.where(depth2 == d + 1 - kd, backs[kd], acc)
                wb_ref[d * 16 : d * 16 + 16, at : at + 256] = acc.astype(BF16)


def feature_weights_kernel(k2_ref, after_ref, w2_ref, so, cf):
    so[...] = jnp.zeros(so.shape, F32)
    for t in range(27):
        g, j = t // 8, t % 8
        so[g * 16 : g * 16 + 16, j * 16 : j * 16 + 16] = k2_ref[t].astype(F32)
    row, lane = iota((128, 2048), 0), iota((128, 2048), 1)
    rep2 = ((row // 16 == lane // 256) & (row % 16 == lane % 16)).astype(BF16)
    cf[...] = dot_nn(so[...].astype(BF16), rep2)
    gap = iota((1, 16, 256), 2) // 16 - iota((1, 16, 256), 1)
    for m in range(9):
        acc = jnp.zeros((16, 16, 256), F32)
        for kd in range(3):
            t = kd * 9 + m
            part = cf[t // 8 * 16 : t // 8 * 16 + 16, t % 8 * 256 : t % 8 * 256 + 256]
            acc = jnp.where(gap == kd - 1, part[:, None, :], acc)
        w2_ref[:, m * 256 : m * 256 + 256] = acc.reshape(256, 256).astype(BF16)


def fine_taps(dp, taps, layers):
    for n in range(layers):
        for t in range(4):
            rows = dp[pl.ds(n * DROW + 7 + t, HY, stride=2), :]
            taps[n * HY : n * HY + HY, t * 128 : t * 128 + 128] = rows.astype(BF16)


def coarse_taps(padded, taps, layers):
    for n in range(layers):
        for k in range(3):
            for half in range(2):
                rows = padded[half, n * CROW + 7 + k : n * CROW + 7 + k + HY, :]
                lane = k * 256 + half * 128
                taps[n * HY : n * HY + HY, lane : lane + 128] = rows.astype(BF16)


def fine_layer(taps, rims, x, py):
    if 0 <= x < NXT:
        return taps[x * HY : x * HY + HY, py * 128 : py * 128 + 384]
    n = x + 3 if x < 0 else x - NXT + 3
    return rims[n * HY : n * HY + HY, py * 128 : py * 128 + 384]


def fine_patch(taps, rims, cells, px, py):
    rows = []
    for cell in cells:
        rows.append(jnp.concatenate([fine_layer(taps, rims, 2 * cell + px + kx - 1, py) for kx in range(3)], axis=1))
    return jnp.concatenate(rows, axis=0)


def coarse_patch(taps, rims, cells):
    rows = []
    for cell in cells:
        parts = []
        for x in (cell - 1, cell, cell + 1):
            ref, n = (taps, x) if 0 <= x < HX else (rims, 0 if x < 0 else 1)
            parts.append(ref[n * HY : n * HY + HY, :])
        rows.append(jnp.concatenate(parts, axis=1))
    return jnp.concatenate(rows, axis=0)


def pooled_sum(pre):
    total = jnp.zeros((256, 128), F32)
    for c in range(4):
        part = pre[:, c * 128 : c * 128 + 128]
        act = jnp.where(part > 0, part, LEAK * part).astype(BF16).astype(F32)
        total = total + act[0:256] + act[256:512]
    return total * 0.125


def back_through(pre, back):
    both = jnp.concatenate([back, back], axis=0)
    low = LEAK * both
    return [jnp.where(pre[:, c * 128 : c * 128 + 128] > 0, both, low).astype(BF16) for c in range(4)]


def tap_kernel(d_ref, c_ref, ft_ref, ct_ref, dp, cp):
    for x in range(NXT):
        dp[x * DROW + 8 : x * DROW + 8 + NYT, :] = d_ref[x].astype(F32)
    for half in range(2):
        for x in range(HX):
            at = x * CROW + 8
            cp[half, at : at + HY, :] = c_ref[x, :, half * 128 : half * 128 + 128].astype(F32)
    fine_taps(dp, ft_ref, NXT)
    coarse_taps(cp, ct_ref, HX)


def set_row(ref, block, lanes, row, value):
    old = ref[block : block + 16, lanes].astype(F32)
    ref[block : block + 16, lanes] = jnp.where(iota((16, 128), 0) == row, value, old).astype(BF16)


def inner_kernel(ft_in, ct_in, lo_ref, hi_ref, w1_ref, wb_ref, ft, ct, pool_ref, g1_ref, ls, hs, bpre):
    ls[...] = lo_ref[...].astype(F32)
    hs[...] = hi_ref[...].astype(F32)
    for x in range(NXT):
        set_row(ft, x * HY, slice(0, 128), 0, ls[64 + x : 65 + x, :])
        set_row(ft, x * HY + 16, slice(384, 512), 15, hs[x : x + 1, :])
    for x in range(HX):
        for half in range(2):
            at = 96 + half * 16 + x
            set_row(ct, x * HY, slice(half * 128, half * 128 + 128), 0, ls[at : at + 1, :])
            set_row(ct, x * HY + 16, slice(512 + half * 128, 640 + half * 128), 15, hs[at : at + 1, :])
    back = dot_nt(wb_ref[...], coarse_patch(ct, None, INNER)).astype(BF16).astype(F32) * 0.125
    patches = []
    for g in range(3):
        cells = INNER[4 * g : 4 * g + 4]
        group = [fine_patch(ft, None, cells, px, py) for px in range(2) for py in range(2)]
        pre = dot_nt(w1_ref[...], jnp.concatenate(group, axis=0))
        pool_ref[:, g * 128 : g * 128 + 128] = pooled_sum(pre).astype(BF16)
        for c, part in enumerate(back_through(pre, back[:, g * 128 : g * 128 + 128])):
            bpre[:, (g * 4 + c) * 128 : (g * 4 + c) * 128 + 128] = part
        patches += group
    g1_ref[...] = dot_nn(bpre[...], jnp.concatenate(patches, axis=0))


def split_dot(select, values):
    high = values.astype(BF16)
    low = (values - high.astype(F32)).astype(BF16)
    return dot_nt(select, high) + dot_nt(select, low)


def extract(g1, g2, out_ref, a1, a2):
    depth1 = iota((16, 128), 1) % 32
    depth2 = iota((16, 256), 1) % 16
    for m in range(9):
        acc = [jnp.zeros((16, 128), F32)] * 3
        for d in range(32):
            row = (d % 2) * 256 + (d // 2) * 16
            part = g1[row : row + 16, m * 128 : m * 128 + 128]
            acc = [jnp.where(depth1 == d + kd - 1, part, acc[kd]) for kd in range(3)]
        for kd in range(3):
            a1[(m * 3 + kd) * 16 : (m * 3 + kd) * 16 + 16, :] = acc[kd]
        acc = [jnp.zeros((16, 256), F32)] * 3
        for d in range(16):
            part = g2[d * 16 : d * 16 + 16, m * 256 : m * 256 + 256]
            acc = [jnp.where(depth2 == d + 1 - kd, part, acc[kd]) for kd in range(3)]
        for kd in range(3):
            a2[(m * 3 + kd) * 16 : (m * 3 + kd) * 16 + 16, :] = acc[kd]
    a1[432:512, :] = jnp.zeros((80, 128), F32)
    a2[432:512, :] = jnp.zeros((80, 256), F32)
    pick2 = (iota((16, 256), 1) // 16 == iota((16, 256), 0)).astype(BF16)
    pick1 = (iota((16, 128), 1) // 32 == iota((16, 128), 0)).astype(BF16)
    two = split_dot(pick2, a2[...])
    one = split_dot(pick1, a1[...])[0:8]
    out_ref[...] = jnp.concatenate([two, one], axis=0).astype(BF16)


def edge_kernel(
    ft, ct, xlo_ref, xhi_ref, w1_ref, wb_ref, pool_ref, g1_ref,
    grad_ref, outer_ref, rims, dp, cp, corner, crims, g1, g2, a1, a2,
):
    for zone, src in enumerate((xlo_ref, xhi_ref)):
        corner[zone * 32 : zone * 32 + 32, :] = src[256:288, :].astype(F32)
        for k in range(3):
            at = (zone * 3 + k) * DROW + 8
            dp[at : at + NYT, :] = src[k * 64 : k * 64 + 64, :].astype(F32)
        for side, y in ((0, 5), (1, 8 + NYT)):
            for ky in range(3):
                for kx in range(3):
                    row = (zone * 3 + kx) * DROW + y + ky
                    at = zone * 32 + side * 9 + 3 * ky + kx
                    dp[row : row + 1, :] = corner[at : at + 1, :]
        for half in range(2):
            at = zone * CROW + 8
            cp[half, at : at + HY, :] = src[192 + half * 32 : 224 + half * 32, :].astype(F32)
            for side, y in ((0, 7), (1, 8 + HY)):
                at = zone * 32 + 18 + side * 2 + half
                cp[half, zone * CROW + y : zone * CROW + y + 1, :] = corner[at : at + 1, :]
    fine_taps(dp, rims, 6)
    coarse_taps(cp, crims, 2)
    cpatch = coarse_patch(ct, crims, OUTER)
    back = dot_nt(wb_ref[...], cpatch).astype(BF16).astype(F32) * 0.125
    group = [fine_patch(ft, rims, OUTER, px, py) for px in range(2) for py in range(2)]
    group = jnp.concatenate(group, axis=0)
    pre = dot_nt(w1_ref[...], group)
    mean = pooled_sum(pre).astype(BF16)
    outer_ref[...] = mean
    g1[...] = g1_ref[...] + dot_nn(jnp.concatenate(back_through(pre, back), axis=1), group)
    pooled = jnp.concatenate([pool_ref[...], mean], axis=1)
    g2[...] = dot_nn(pooled, jnp.concatenate([coarse_patch(ct, None, INNER), cpatch], axis=0))
    extract(g1, g2, grad_ref, a1, a2)


def rim_kernel(
    after_ref, up_ref, down_ref, lo_ref, hi_ref, xlo_ref, xhi_ref, ft_ref, rims_ref, w1_ref, edge_ref, col, corner, rim
):
    for k in range(3):
        col[k, 8:40, :] = lo_ref[k * 32 : k * 32 + 32, :].astype(F32)
        col[5 + k, 8:40, :] = hi_ref[k * 32 : k * 32 + 32, :].astype(F32)
    col[3, 8:40, :] = down_ref[0:32, :].astype(F32)
    col[4, 8:40, :] = up_ref[64:96, :].astype(F32)
    for src, row in ((xlo_ref, 5), (xhi_ref, 40)):
        corner[...] = src[...].astype(F32)
        for kx in range(3):
            for ky in range(3):
                col[ky, row + kx : row + kx + 1, :] = corner[256 + 3 * ky + kx : 257 + 3 * ky + kx, :]
                col[5 + ky, row + kx : row + kx + 1, :] = corner[265 + 3 * ky + kx : 266 + 3 * ky + kx, :]
            col[3, row + kx : row + kx + 1, :] = corner[kx * 64 : kx * 64 + 1, :]
            col[4, row + kx : row + kx + 1, :] = corner[kx * 64 + 63 : kx * 64 + 64, :]
    for px in range(2):
        for py in range(2):
            at = (px * 2 + py) * 128
            rim[at : at + 64, :] = fine_patch(ft_ref, rims_ref, (-1, HX), px, py)
            for side in range(2):
                for kx in range(3):
                    for ky in range(3):
                        rows = col[side * 4 + py + ky, pl.ds(5 + px + kx, 18, stride=2), :]
                        rows = jnp.concatenate([rows, jnp.zeros((14, 128), F32)], axis=0)
                        lane = (kx * 3 + ky) * 128
                        rim[at + 64 + side * 32 : at + 96 + side * 32, lane : lane + 128] = rows.astype(BF16)
    edge_ref[...] = pooled_sum(dot_nt(w1_ref[...], rim[...])).T.astype(BF16)


def feature_kernel(after_ref, edge_ref, pool_ref, outer_ref, w2_ref, feat_ref, token_ref, pp, pt):
    edge = edge_ref[...].astype(F32)
    inner = pool_ref[...].astype(F32).T
    outer = outer_ref[...].astype(F32).T
    for half in range(2):
        lanes = slice(half * 128, half * 128 + 128)
        pp[half, 8:40, :] = edge[0:32, lanes]
        pp[half, (HX + 1) * CROW + 8 : (HX + 1) * CROW + 40, :] = edge[32:64, lanes]
        for cells, part in ((INNER, inner), (OUTER, outer)):
            for n, x in enumerate(cells):
                pp[half, (x + 1) * CROW + 8 : (x + 1) * CROW + 40, :] = part[n * 32 : n * 32 + 32, lanes]
        pp[half, pl.ds(7, 18, stride=CROW), :] = edge[64:82, lanes]
        pp[half, pl.ds(8 + HY, 18, stride=CROW), :] = edge[96:114, lanes]
    coarse_taps(pp, pt, HX + 2)
    patch = [pt[k * HY : (k + HX) * HY, :] for k in range(3)]
    feat = dot_nt(jnp.concatenate(patch, axis=1), w2_ref[...])
    feat_ref[...] = feat.astype(BF16).reshape(HX, HY, 256)
    token_ref[...] = feat[0:8, 0:128]


def add_two_kernel(a_ref, b_ref, out_ref):
    out_ref[...] = (a_ref[...].astype(F32) + b_ref[...].astype(F32)).astype(BF16)


def add_four(refs):
    a, b, c, d = (ref[...].astype(F32) for ref in refs)
    return (a + b) + (c + d)


def add_four_kernel(a_ref, b_ref, c_ref, d_ref, after_ref, also_ref, out_ref):
    out_ref[...] = add_four((a_ref, b_ref, c_ref, d_ref)).astype(BF16)


def final_kernel(a_ref, b_ref, c_ref, d_ref, g1_ref, g2_ref):
    total = add_four((a_ref, b_ref, c_ref, d_ref)) * 0.5
    for kd in range(3):
        for kx in range(3):
            for ky in range(3):
                t = kd * 9 + kx * 3 + ky
                at = ((kx * 3 + ky) * 3 + kd) * 16
                g1_ref[t] = total[16:20, at : at + 16]
                at = (((2 - kx) * 3 + 2 - ky) * 3 + kd) * 16
                g2_ref[t] = total[0:16, at : at + 16]


ANY = pl.BlockSpec(memory_space=pl.ANY)
VM = pl.BlockSpec(memory_space=pltpu.VMEM)


def call(kernel, ins, outs, scratch=(), limit=VMEM_LIMIT, flops=None, aliases=None):
    cost = None if flops is None else pl.CostEstimate(flops=flops, bytes_accessed=1_000_000, transcendentals=0)
    return pl.pallas_call(
        kernel,
        out_shape=outs,
        in_specs=ins,
        scratch_shapes=list(scratch),
        cost_estimate=cost,
        input_output_aliases=aliases or {},
        compiler_params=pltpu.CompilerParams(vmem_limit_bytes=limit),
    )


def struct(shape, kind):
    return jax.ShapeDtypeStruct(shape, kind)


def buffer(*shape):
    return pltpu.VMEM(shape, F32)


def buffer16(*shape):
    return pltpu.VMEM(shape, BF16)


def shift(value, axes, step):
    n = lax.axis_size(axes)
    return lax.ppermute(value, axes, [(i, (i + step) % n) for i in range(n)])


def partner(value, axes, bits):
    n = lax.axis_size(axes)
    return lax.ppermute(value, axes, [(i, i ^ bits) for i in range(n)])


TX = ("x", "yh")
TY = ("z", "core")


def on_device(density, kernel_one, kernel_two, cotangent):
    d, c = density[0], cotangent[0]
    k1 = jnp.transpose(kernel_one, (2, 3, 4, 1, 0)).reshape(27, CIN, CH)
    k2 = jnp.transpose(kernel_two, (2, 3, 4, 0, 1)).reshape(27, CH, CH)

    message = struct((128, 128), BF16)
    yup, ydown = call(
        pack_y_kernel,
        [ANY] * 2,
        (message, message),
        (
            buffer16(2, NXT, 16, 128), buffer16(2, HX, 16, 256),
            buffer(NXT * 16, 128), buffer(2, HX * 16, 128), pltpu.SemaphoreType.DMA((4,)),
        ),
        limit=VMEM_ALL,
        flops=FLOPS,
    )(d, c)
    lo, hi = shift(yup, TY, 1), shift(ydown, TY, -1)
    w1, wb = call(
        weights_kernel,
        [VM] * 2,
        (struct((512, 1152), BF16), struct((256, 2304), BF16)),
        (buffer(128, 128), buffer(16, 27 * 128), buffer(64, 2048)),
    )(k1, k2)
    ft, ct = call(
        tap_kernel,
        [VM] * 2,
        (struct((NXT * HY, 512), BF16), struct((HX * HY, 768), BF16)),
        (buffer(NXT * DROW, 128), buffer(2, HX * CROW, 128)),
    )(d, c)
    message = struct((288, 128), BF16)
    up, down = call(
        pack_x_kernel,
        [VM] * 4 + [ANY] * 2,
        (message, message),
        (buffer(128, 128), buffer(128, 128), buffer(32, 128)),
    )(d, c, lo, hi, w1, ct)
    xlo, xhi = shift(up, TX, 1), shift(down, TX, -1)

    ft, ct, pool, g1 = call(
        inner_kernel,
        [VM] * 6,
        (struct(ft.shape, BF16), struct(ct.shape, BF16), struct((256, 384), BF16), struct((512, 1152), F32)),
        (buffer(128, 128), buffer(128, 128), buffer16(512, 1536)),
        aliases={0: 0, 1: 1},
    )(ft, ct, lo, hi, w1, wb)
    gradient = struct((24, 512), BF16)
    grads, outer, rims = call(
        edge_kernel,
        [VM] * 8,
        (gradient, struct((256, 128), BF16), struct((6 * HY, 512), BF16)),
        (
            buffer(6 * DROW, 128), buffer(2, 2 * CROW, 128), buffer(64, 128), buffer16(2 * HY, 768),
            buffer(512, 1152), buffer(256, 2304), buffer(512, 128), buffer(512, 256),
        ),
    )(ft, ct, xlo, xhi, w1, wb, pool, g1)

    grads = call(add_two_kernel, [VM] * 2, gradient)(grads, partner(grads, "core", 1))
    w2 = call(
        feature_weights_kernel,
        [VM, ANY],
        struct((256, 2304), BF16),
        (buffer(64, 128), buffer(64, 2048)),
    )(k2, grads)
    edge = call(
        rim_kernel,
        [ANY] + [VM] * 9,
        struct((128, 256), BF16),
        (buffer(8, 48, 128), buffer(288, 128), buffer16(512, 1152)),
    )(grads, yup, ydown, lo, hi, xlo, xhi, ft, rims, w1)
    others = [partner(grads, "z", bits) for bits in (1, 3, 2)]
    grads = call(add_four_kernel, [VM] * 4 + [ANY] * 2, gradient)(grads, *others, edge, w2)
    feat, token = call(
        feature_kernel,
        [ANY] + [VM] * 4,
        (struct((HX, HY, 256), BF16), struct((8, 128), F32)),
        (buffer(2, (HX + 2) * CROW, 128), buffer16((HX + 2) * HY, 768)),
    )(grads, edge, pool, outer, w2)
    others = [partner(grads, "x", bits) for bits in (1, 3, 2)]
    grads = call(add_four_kernel, [VM] * 4 + [ANY] * 2, gradient)(grads, *others, token, token)
    near = partner(grads, "rep", 1)
    across = partner(grads, ("rep", "yh"), 3)
    far = partner(grads, "yh", 1)
    g1, g2 = call(final_kernel, [VM] * 4, (struct((27, CIN, CH), F32), struct((27, CH, CH), F32)))(
        grads, near, across, far
    )
    g1 = jnp.transpose(g1.reshape(3, 3, 3, CIN, CH), (4, 3, 0, 1, 2))
    g2 = jnp.transpose(g2.reshape(3, 3, 3, CH, CH), (3, 4, 0, 1, 2))
    return feat[None], g1, g2


def solution(mesh):
    fine = Mesh(mesh.devices.reshape(2, 4, 2, 4, 2), ("rep", "x", "yh", "z", "core"))
    tiles = P("rep", TX, TY, None)
    return jax.shard_map(
        on_device, mesh=fine, in_specs=(tiles, P(), P(), tiles), out_specs=(tiles, P(), P()), check_vma=False
    )
```

time: 48.5 us -> 47.8 us (0.986)
  Pallas kernels: 16.8 us -> 16.2 us
  starting transfers between devices: 21.9 us -> 21.3 us
    pallas_call x1, Pallas kernels: 1.61 us -> 1.02 us  [on_device(): call(weights_kernel, [VM] * 2, (struct((512, 1152), BF16), struct((256, 2...]
    ppermute x10, starting transfers between devices: 12.6 us -> 12 us  [partner(): return lax.ppermute(value, axes, [(i, i ^ bits) for i in range(n)])]
    pallas_call x7 -> x10, Pallas kernels: 12.5 us -> 12.5 us  [the longest x1 5.1 us: on_device(): call(inner_kernel, [VM] * 6, (struct(ft.shape, BF16), struct(ct.shape, BF...]
  transfers between devices with their start and end apart: 14 -> 14, of which waited for: 8 -> 9; matrix products, arithmetic and copies ran while one was open for 0% -> 0% of each run, Pallas kernels for 22% -> 21%
where the time goes in v3:
time: 47.8 us; the launch traced here: 47.7 us
  starting transfers between devices  21.3 us (45%)
  Pallas kernels  16.2 us (34%)
  waiting for transfers between devices  9.3 us (19%)
  between operations  0.79 us (2%)
    ppermute x10, starting transfers between devices, partner(): return lax.ppermute(value, axes, [(i, i ^ bits) for i in range(n)])  12 us
    ppermute x4, starting transfers between devices, shift(): return lax.ppermute(value, axes, [(i, (i + step) % n) for i in range(n)])  9.3 us
    ppermute x10, waiting for transfers between devices, partner(): return lax.ppermute(value, axes, [(i, i ^ bits) for i in range(n)])  8.81 us
    pallas_call x1, Pallas kernels, on_device(): call(inner_kernel, [VM] * 6, (struct(ft.shape, BF16), struct(ct.shape, BF...  5.1 us
    pallas_call x1, Pallas kernels, on_device(): call(edge_kernel, [VM] * 8, (gradient, struct((256, 128), BF16), struct((...  3.47 us
    pallas_call x1, Pallas kernels, on_device(): call(pack_y_kernel, [ANY] * 2, (message, message), (buffer16(2, NXT, 16,...  1.91 us
    pallas_call x1, Pallas kernels, on_device(): call(feature_kernel, [ANY] + [VM] * 4, (struct((HX, HY, 256), BF16), stru...  1.6 us
    pallas_call x1, Pallas kernels, on_device(): call(rim_kernel, [ANY] + [VM] * 9, struct((128, 256), BF16), (buffer(8, 4...  1.11 us
  transfers between devices with their start and end apart: 14, of which 9 were waited for; matrix products, arithmetic and copies ran while one was open for 0% of the time, Pallas kernels for 21%

profile of v3, /device:TPU:0, one launch (start us, length us, event | category | flops | bytes accessed | tf_op | source)
XLA Modules:
  0.0 47.7 jit_solution(438857813652939066)
XLA Ops:
  0.7 1.9 %shard_map.68 = (bf16[128,128]{1,0:T(8,128)(2,1)}, bf16[128,128]{1,0:T(8,128)(2,1)}) custom-call(bf16[32,64,128]{2,1,0:T(8,128)(2,1)} %bitcast.15, bf16[16,32,256]{2,1,0:T(8,128)(2,1)} %bitcast.18), custom_call_target="tpu_custom_call" | custom-call | flops 5000000000 | bytes 1000000 | tf_op jit(solution)/shard_map/pallas_call | solution.py:421
  2.6 3.6 %collective-permute-start.1 = (bf16[128,128]{1,0:T(8,128)(2,1)}, bf16[128,128]{1,0:T(8,128)(2,1)S(1)}, u32[]{:S(2)}, u32[]{:S(2)}) collective-permute-start(bf16[128,128]{1,0:T(8,128)(2,1)} %get-tuple-element.25.down_ref), channel_id=1, source_target_pairs={{0,7},{1,0},{2,1},{3,2},{4,3},{5,4},{6,5},{7,6},{8,15},{9,8},{10,9... | collective-permute-start | bytes 98312 | tf_op jit(solution)/shard_map/ppermute | solution.py:403
  6.6 1.0 %shard_map.69 = (bf16[512,1152]{1,0:T(8,128)(2,1)S(1)}, bf16[256,2304]{1,0:T(8,128)(2,1)S(1)}) custom-call(bf16[27,4,16]{2,1,0:T(4,128)(2,1)S(1)} %bitcast.23, bf16[27,16,16]{2,1,0:T(8,128)(2,1)S(1)} %bitcast.21), custom_call_target="tpu_custom_call" | custom-call | tf_op jit(solution)/shard_map/pallas_call | solution.py:433
  8.1 3.3 %collective-permute-start.2 = (bf16[288,128]{1,0:T(8,128)(2,1)S(1)}, bf16[288,128]{1,0:T(8,128)(2,1)S(1)}, u32[]{:S(2)}, u32[]{:S(2)}) collective-permute-start(bf16[288,128]{1,0:T(8,128)(2,1)S(1)} %get-tuple-element.30), channel_id=1, source_target_pairs={{0,8},{8,16},{16,24},{24,32},{32,40},{40,48},{48,56},{56,0},{1,9},... | collective-permute-start | bytes 221192 | tf_op jit(solution)/shard_map/ppermute | solution.py:403
  11.4 2.4 %collective-permute-start.3 = (bf16[288,128]{1,0:T(8,128)(2,1)S(1)}, bf16[288,128]{1,0:T(8,128)(2,1)S(1)}, u32[]{:S(2)}, u32[]{:S(2)}) collective-permute-start(bf16[288,128]{1,0:T(8,128)(2,1)S(1)} %get-tuple-element.31), channel_id=1, source_target_pairs={{0,56},{8,0},{16,8},{24,16},{32,24},{40,32},{48,40},{56,48},{1,57}... | collective-permute-start | bytes 221192 | tf_op jit(solution)/shard_map/ppermute | solution.py:403
  13.8 5.1 %shard_map.70 = (bf16[1024,512]{1,0:T(8,128)(2,1)S(1)}, bf16[512,768]{1,0:T(8,128)(2,1)S(1)}, bf16[256,384]{1,0:T(8,128)(2,1)S(1)}, f32[512,1152]{1,0:T(8,128)S(1)}) custom-call(bf16[1024,512]{1,0:T(8,128)(2,1)S(1)} %get-tuple-element.22.ft_in, bf16[512,768]{1,0:T(8,128)(2,1)S(1)} %get-tuple-element.23.ct_in.also_ref, ...), custom_call_target="tpu_custom_call", output_to_operand_aliasing={{0}: (0, {}), {1}: (1, {})} | custom-call | tf_op jit(solution)/shard_map/pallas_call | solution.py:454
  19.0 3.5 %shard_map.72 = (bf16[24,512]{1,0:T(8,128)(2,1)S(1)}, bf16[256,128]{1,0:T(8,128)(2,1)S(1)}, bf16[192,512]{1,0:T(8,128)(2,1)S(1)}) custom-call(bf16[1024,512]{1,0:T(8,128)(2,1)S(1)} %get-tuple-element.28.ft.ft_ref, bf16[512,768]{1,0:T(8,128)(2,1)S(1)} %get-tuple-element.29.ct, bf16[288,128]{1,0:T(8,128)(2,1)S(1)} %collective-permute-done.2.xlo_ref, ...), custom_call_target="tpu_custom_call" | custom-call | tf_op jit(solution)/shard_map/pallas_call | solution.py:462
  22.5 1.2 %collective-permute-done.4.b_ref = bf16[24,512]{1,0:T(8,128)(2,1)S(1)} collective-permute-done((bf16[24,512]{1,0:T(8,128)(2,1)S(1)}, bf16[24,512]{1,0:T(8,128)(2,1)S(1)}, u32[]{:S(2)}, u32[]{:S(2)}) %collective-permute-start.4) | collective-permute-done | bytes 24608 | tf_op jit(solution)/shard_map/ppermute | solution.py:408
  23.7 3.0 %collective-permute-start.7 = (bf16[24,512]{1,0:T(8,128)(2,1)S(1)}, bf16[24,512]{1,0:T(8,128)(2,1)S(1)}, u32[]{:S(2)}, u32[]{:S(2)}) collective-permute-start(bf16[24,512]{1,0:T(8,128)(2,1)S(1)} %shard_map.73.after_ref.a_ref), channel_id=1, source_target_pairs={{0,4},{2,6},{4,0},{6,2},{1,5},{3,7},{5,1},{7,3},{8,12},{10,14},{12... | collective-permute-start | bytes 73736 | tf_op jit(solution)/shard_map/ppermute | solution.py:408
  26.8 1.0 %collective-permute-start.6 = (bf16[24,512]{1,0:T(8,128)(2,1)S(1)}, bf16[24,512]{1,0:T(8,128)(2,1)S(1)}, u32[]{:S(2)}, u32[]{:S(2)}) collective-permute-start(bf16[24,512]{1,0:T(8,128)(2,1)S(1)} %shard_map.73.after_ref.a_ref), channel_id=1, source_target_pairs={{0,6},{2,4},{4,2},{6,0},{1,7},{3,5},{5,3},{7,1},{8,14},{10,12},{12... | collective-permute-start | bytes 73736 | tf_op jit(solution)/shard_map/ppermute | solution.py:408
  27.8 0.7 %shard_map.75.also_ref.w2_ref = bf16[256,2304]{1,0:T(8,128)(2,1)S(1)} custom-call(bf16[27,16,16]{2,1,0:T(8,128)(2,1)S(1)} %bitcast.22, bf16[24,512]{1,0:T(8,128)(2,1)S(1)} %shard_map.73.after_ref.a_ref), custom_call_target="tpu_custom_call" | custom-call | tf_op jit(solution)/shard_map/pallas_call | solution.py:473
  28.5 1.1 %shard_map.74.after_ref.edge_ref = bf16[128,256]{1,0:T(8,128)(2,1)S(1)} custom-call(bf16[24,512]{1,0:T(8,128)(2,1)S(1)} %shard_map.73.after_ref.a_ref, bf16[128,128]{1,0:T(8,128)(2,1)S(1)} %copy-done.3, bf16[128,128]{1,0:T(8,128)(2,1)S(1)} %copy-done.4, bf16[128,128]{1,0:T(8,128)(2,1)S(1)} %collective-permute-done.lo_ref, ...), custom_call_target="tpu_custom_call" | custom-call | tf_op jit(solution)/shard_map/pallas_call | solution.py:479
  29.6 2.2 %collective-permute-done.6.c_ref = bf16[24,512]{1,0:T(8,128)(2,1)S(1)} collective-permute-done((bf16[24,512]{1,0:T(8,128)(2,1)S(1)}, bf16[24,512]{1,0:T(8,128)(2,1)S(1)}, u32[]{:S(2)}, u32[]{:S(2)}) %collective-permute-start.6) | collective-permute-done | bytes 24608 | tf_op jit(solution)/shard_map/ppermute | solution.py:408
  31.8 1.8 %collective-permute-start.10 = (bf16[24,512]{1,0:T(8,128)(2,1)S(1)}, bf16[24,512]{1,0:T(8,128)(2,1)S(1)}, u32[]{:S(2)}, u32[]{:S(2)}) collective-permute-start(bf16[24,512]{1,0:T(8,128)(2,1)S(1)} %shard_map.76.after_ref.a_ref), channel_id=1, source_target_pairs={{0,32},{16,48},{32,0},{48,16},{1,33},{17,49},{33,1},{49,17},{2,34}... | collective-permute-start | bytes 73736 | tf_op jit(solution)/shard_map/ppermute | solution.py:408
  33.6 1.1 %collective-permute-start.9 = (bf16[24,512]{1,0:T(8,128)(2,1)S(1)}, bf16[24,512]{1,0:T(8,128)(2,1)S(1)}, u32[]{:S(2)}, u32[]{:S(2)}) collective-permute-start(bf16[24,512]{1,0:T(8,128)(2,1)S(1)} %shard_map.76.after_ref.a_ref), channel_id=1, source_target_pairs={{0,48},{16,32},{32,16},{48,0},{1,49},{17,33},{33,17},{49,1},{2,50}... | collective-permute-start | bytes 73736 | tf_op jit(solution)/shard_map/ppermute | solution.py:408
  34.7 0.6 %collective-permute-start.8 = (bf16[24,512]{1,0:T(8,128)(2,1)S(1)}, bf16[24,512]{1,0:T(8,128)(2,1)S(1)}, u32[]{:S(2)}, u32[]{:S(2)}) collective-permute-start(bf16[24,512]{1,0:T(8,128)(2,1)S(1)} %shard_map.76.after_ref.a_ref), channel_id=1, source_target_pairs={{0,16},{16,0},{32,48},{48,32},{1,17},{17,1},{33,49},{49,33},{2,18}... | collective-permute-start | bytes 73736 | tf_op jit(solution)/shard_map/ppermute | solution.py:408
  35.4 1.6 %shard_map.77 = (bf16[16,32,256]{2,1,0:T(8,128)(2,1)}, f32[8,128]{1,0:T(8,128)S(1)}) custom-call(bf16[24,512]{1,0:T(8,128)(2,1)S(1)} %shard_map.76.after_ref.a_ref, bf16[128,256]{1,0:T(8,128)(2,1)S(1)} %shard_map.74.after_ref.edge_ref, bf16[256,384]{1,0:T(8,128)(2,1)S(1)} %get-tuple-element.32.pool_ref, bf16[256,128]{1,0:T(8,128)(2,1)S(1)} %get-tuple-element.36.outer_ref, ...), custom_call_target="tpu_custom_call" | custom-call | tf_op jit(solution)/shard_map/pallas_call | solution.py:487
  37.2 1.4 %collective-permute-done.9.c_ref = bf16[24,512]{1,0:T(8,128)(2,1)S(1)} collective-permute-done((bf16[24,512]{1,0:T(8,128)(2,1)S(1)}, bf16[24,512]{1,0:T(8,128)(2,1)S(1)}, u32[]{:S(2)}, u32[]{:S(2)}) %collective-permute-start.9) | collective-permute-done | bytes 24608 | tf_op jit(solution)/shard_map/ppermute | solution.py:408
  38.7 2.4 %collective-permute-start.13 = (bf16[24,512]{1,0:T(8,128)(2,1)S(1)}, bf16[24,512]{1,0:T(8,128)(2,1)S(1)}, u32[]{:S(2)}, u32[]{:S(2)}) collective-permute-start(bf16[24,512]{1,0:T(8,128)(2,1)S(1)} %shard_map.78.a_ref), channel_id=1, source_target_pairs={{0,8},{8,0},{1,9},{9,1},{2,10},{10,2},{3,11},{11,3},{4,12},{12,4},... | collective-permute-start | bytes 73736 | tf_op jit(solution)/shard_map/ppermute | solution.py:408
  41.0 2.0 %collective-permute-start.12 = (bf16[24,512]{1,0:T(8,128)(2,1)S(1)}, bf16[24,512]{1,0:T(8,128)(2,1)S(1)}, u32[]{:S(2)}, u32[]{:S(2)}) collective-permute-start(bf16[24,512]{1,0:T(8,128)(2,1)S(1)} %shard_map.78.a_ref), channel_id=1, source_target_pairs={{0,72},{8,64},{64,8},{72,0},{1,73},{9,65},{65,9},{73,1},{2,74},{10... | collective-permute-start | bytes 73736 | tf_op jit(solution)/shard_map/ppermute | solution.py:408
  43.0 1.1 %collective-permute-done.13.d_ref = bf16[24,512]{1,0:T(8,128)(2,1)S(1)} collective-permute-done((bf16[24,512]{1,0:T(8,128)(2,1)S(1)}, bf16[24,512]{1,0:T(8,128)(2,1)S(1)}, u32[]{:S(2)}, u32[]{:S(2)}) %collective-permute-start.13) | collective-permute-done | bytes 24608 | tf_op jit(solution)/shard_map/ppermute | solution.py:408
  44.1 2.0 %collective-permute-done.12.c_ref = bf16[24,512]{1,0:T(8,128)(2,1)S(1)} collective-permute-done((bf16[24,512]{1,0:T(8,128)(2,1)S(1)}, bf16[24,512]{1,0:T(8,128)(2,1)S(1)}, u32[]{:S(2)}, u32[]{:S(2)}) %collective-permute-start.12) | collective-permute-done | bytes 24608 | tf_op jit(solution)/shard_map/ppermute | solution.py:408
  46.1 0.7 %collective-permute-done.11.b_ref = bf16[24,512]{1,0:T(8,128)(2,1)S(1)} collective-permute-done((bf16[24,512]{1,0:T(8,128)(2,1)S(1)}, bf16[24,512]{1,0:T(8,128)(2,1)S(1)}, u32[]{:S(2)}, u32[]{:S(2)}) %collective-permute-start.11) | collective-permute-done | bytes 24608 | tf_op jit(solution)/shard_map/ppermute | solution.py:408
  46.8 0.8 %shard_map.79 = (f32[27,4,16]{2,1,0:T(4,128)}, f32[27,16,16]{2,1,0:T(8,128)}) custom-call(bf16[24,512]{1,0:T(8,128)(2,1)S(1)} %shard_map.78.a_ref, bf16[24,512]{1,0:T(8,128)(2,1)S(1)} %collective-permute-done.11.b_ref, bf16[24,512]{1,0:T(8,128)(2,1)S(1)} %collective-permute-done.12.c_ref, bf16[24,512]{1,0:T(8,128)(2,1)S(1)} %collective-permute-done.13.d_ref), custom_call_target="tpu_custom_call" | custom-call | tf_op jit(solution)/shard_map/pallas_call | solution.py:498
  (29 shorter events, 1.3 us)
Async XLA Ops:
  0.6 5.6 %copy-start = (bf16[1,32,64,128]{3,2,1,0:T(8,128)(2,1)S(1)}, bf16[1,32,64,128]{3,2,1,0:T(8,128)(2,1)}, u32[]{:S(2)}) copy-start(bf16[1,32,64,128]{3,2,1,0:T(8,128)(2,1)} %param.4) | copy-start | bytes 1572868
  0.6 5.6 %copy-start.1 = (bf16[1,16,32,256]{3,2,1,0:T(8,128)(2,1)S(1)}, bf16[1,16,32,256]{3,2,1,0:T(8,128)(2,1)}, u32[]{:S(2)}) copy-start(bf16[1,16,32,256]{3,2,1,0:T(8,128)(2,1)} %param.7) | copy-start | bytes 786436
  0.7 5.9 %copy-start.2 = (bf16[16,16,3,3,3]{1,0,4,3,2:T(8,128)(2,1)S(1)}, bf16[16,16,3,3,3]{1,0,4,3,2:T(8,128)(2,1)}, u32[]{:S(2)}) copy-start(bf16[16,16,3,3,3]{1,0,4,3,2:T(8,128)(2,1)} %param.6) | copy-start | bytes 41476
  0.7 5.9 %copy-start.5 = (bf16[16,4,3,3,3]{0,1,4,3,2:T(4,128)(2,1)S(1)}, bf16[16,4,3,3,3]{0,1,4,3,2:T(4,128)(2,1)}, u32[]{:S(2)}) copy-start(bf16[16,4,3,3,3]{0,1,4,3,2:T(4,128)(2,1)} %param.5) | copy-start | bytes 10372
  2.6 5.4 %collective-permute-start = (bf16[128,128]{1,0:T(8,128)(2,1)}, bf16[128,128]{1,0:T(8,128)(2,1)S(1)}, u32[]{:S(2)}, u32[]{:S(2)}) collective-permute-start(bf16[128,128]{1,0:T(8,128)(2,1)} %get-tuple-element.24.up_ref), channel_id=1, source_target_pairs={{0,1},{1,2},{2,3},{3,4},{4,5},{5,6},{6,7},{7,0},{8,9},{9,10},{10,1... | collective-permute-start | bytes 98312 | tf_op jit(solution)/shard_map/ppermute | solution.py:403
  2.6 5.5 %collective-permute-start.1 = (bf16[128,128]{1,0:T(8,128)(2,1)}, bf16[128,128]{1,0:T(8,128)(2,1)S(1)}, u32[]{:S(2)}, u32[]{:S(2)}) collective-permute-start(bf16[128,128]{1,0:T(8,128)(2,1)} %get-tuple-element.25.down_ref), channel_id=1, source_target_pairs={{0,7},{1,0},{2,1},{3,2},{4,3},{5,4},{6,5},{7,6},{8,15},{9,8},{10,9... | collective-permute-start | bytes 98312 | tf_op jit(solution)/shard_map/ppermute | solution.py:403
  8.1 10.8 %collective-permute-start.2 = (bf16[288,128]{1,0:T(8,128)(2,1)S(1)}, bf16[288,128]{1,0:T(8,128)(2,1)S(1)}, u32[]{:S(2)}, u32[]{:S(2)}) collective-permute-start(bf16[288,128]{1,0:T(8,128)(2,1)S(1)} %get-tuple-element.30), channel_id=1, source_target_pairs={{0,8},{8,16},{16,24},{24,32},{32,40},{40,48},{48,56},{56,0},{1,9},... | collective-permute-start | bytes 221192 | tf_op jit(solution)/shard_map/ppermute | solution.py:403
  11.4 7.6 %collective-permute-start.3 = (bf16[288,128]{1,0:T(8,128)(2,1)S(1)}, bf16[288,128]{1,0:T(8,128)(2,1)S(1)}, u32[]{:S(2)}, u32[]{:S(2)}) collective-permute-start(bf16[288,128]{1,0:T(8,128)(2,1)S(1)} %get-tuple-element.31), channel_id=1, source_target_pairs={{0,56},{8,0},{16,8},{24,16},{32,24},{40,32},{48,40},{56,48},{1,57}... | collective-permute-start | bytes 221192 | tf_op jit(solution)/shard_map/ppermute | solution.py:403
  22.4 6.1 %copy-start.3 = (bf16[128,128]{1,0:T(8,128)(2,1)S(1)}, bf16[128,128]{1,0:T(8,128)(2,1)}, u32[]{:S(2)}) copy-start(bf16[128,128]{1,0:T(8,128)(2,1)} %get-tuple-element.24.up_ref) | copy-start | bytes 98308
  22.4 6.1 %copy-start.4 = (bf16[128,128]{1,0:T(8,128)(2,1)S(1)}, bf16[128,128]{1,0:T(8,128)(2,1)}, u32[]{:S(2)}) copy-start(bf16[128,128]{1,0:T(8,128)(2,1)} %get-tuple-element.25.down_ref) | copy-start | bytes 98308
  22.4 1.3 %collective-permute-start.4 = (bf16[24,512]{1,0:T(8,128)(2,1)S(1)}, bf16[24,512]{1,0:T(8,128)(2,1)S(1)}, u32[]{:S(2)}, u32[]{:S(2)}) collective-permute-start(bf16[24,512]{1,0:T(8,128)(2,1)S(1)} %get-tuple-element.34.a_ref), channel_id=1, source_target_pairs={{0,1},{1,0},{2,3},{3,2},{4,5},{5,4},{6,7},{7,6},{8,9},{9,8},{10,11... | collective-permute-start | bytes 73736 | tf_op jit(solution)/shard_map/ppermute | solution.py:408
  23.7 5.9 %collective-permute-start.7 = (bf16[24,512]{1,0:T(8,128)(2,1)S(1)}, bf16[24,512]{1,0:T(8,128)(2,1)S(1)}, u32[]{:S(2)}, u32[]{:S(2)}) collective-permute-start(bf16[24,512]{1,0:T(8,128)(2,1)S(1)} %shard_map.73.after_ref.a_ref), channel_id=1, source_target_pairs={{0,4},{2,6},{4,0},{6,2},{1,5},{3,7},{5,1},{7,3},{8,12},{10,14},{12... | collective-permute-start | bytes 73736 | tf_op jit(solution)/shard_map/ppermute | solution.py:408
  26.8 5.0 %collective-permute-start.6 = (bf16[24,512]{1,0:T(8,128)(2,1)S(1)}, bf16[24,512]{1,0:T(8,128)(2,1)S(1)}, u32[]{:S(2)}, u32[]{:S(2)}) collective-permute-start(bf16[24,512]{1,0:T(8,128)(2,1)S(1)} %shard_map.73.after_ref.a_ref), channel_id=1, source_target_pairs={{0,6},{2,4},{4,2},{6,0},{1,7},{3,5},{5,3},{7,1},{8,14},{10,12},{12... | collective-permute-start | bytes 73736 | tf_op jit(solution)/shard_map/ppermute | solution.py:408
  27.8 4.0 %collective-permute-start.5 = (bf16[24,512]{1,0:T(8,128)(2,1)S(1)}, bf16[24,512]{1,0:T(8,128)(2,1)S(1)}, u32[]{:S(2)}, u32[]{:S(2)}) collective-permute-start(bf16[24,512]{1,0:T(8,128)(2,1)S(1)} %shard_map.73.after_ref.a_ref), channel_id=1, source_target_pairs={{0,2},{2,0},{4,6},{6,4},{1,3},{3,1},{5,7},{7,5},{8,10},{10,8},{12,... | collective-permute-start | bytes 73736 | tf_op jit(solution)/shard_map/ppermute | solution.py:408
  31.8 5.4 %collective-permute-start.10 = (bf16[24,512]{1,0:T(8,128)(2,1)S(1)}, bf16[24,512]{1,0:T(8,128)(2,1)S(1)}, u32[]{:S(2)}, u32[]{:S(2)}) collective-permute-start(bf16[24,512]{1,0:T(8,128)(2,1)S(1)} %shard_map.76.after_ref.a_ref), channel_id=1, source_target_pairs={{0,32},{16,48},{32,0},{48,16},{1,33},{17,49},{33,1},{49,17},{2,34}... | collective-permute-start | bytes 73736 | tf_op jit(solution)/shard_map/ppermute | solution.py:408
  33.6 5.0 %collective-permute-start.9 = (bf16[24,512]{1,0:T(8,128)(2,1)S(1)}, bf16[24,512]{1,0:T(8,128)(2,1)S(1)}, u32[]{:S(2)}, u32[]{:S(2)}) collective-permute-start(bf16[24,512]{1,0:T(8,128)(2,1)S(1)} %shard_map.76.after_ref.a_ref), channel_id=1, source_target_pairs={{0,48},{16,32},{32,16},{48,0},{1,49},{17,33},{33,17},{49,1},{2,50}... | collective-permute-start | bytes 73736 | tf_op jit(solution)/shard_map/ppermute | solution.py:408
  34.7 3.9 %collective-permute-start.8 = (bf16[24,512]{1,0:T(8,128)(2,1)S(1)}, bf16[24,512]{1,0:T(8,128)(2,1)S(1)}, u32[]{:S(2)}, u32[]{:S(2)}) collective-permute-start(bf16[24,512]{1,0:T(8,128)(2,1)S(1)} %shard_map.76.after_ref.a_ref), channel_id=1, source_target_pairs={{0,16},{16,0},{32,48},{48,32},{1,17},{17,1},{33,49},{49,33},{2,18}... | collective-permute-start | bytes 73736 | tf_op jit(solution)/shard_map/ppermute | solution.py:408
  38.7 5.4 %collective-permute-start.13 = (bf16[24,512]{1,0:T(8,128)(2,1)S(1)}, bf16[24,512]{1,0:T(8,128)(2,1)S(1)}, u32[]{:S(2)}, u32[]{:S(2)}) collective-permute-start(bf16[24,512]{1,0:T(8,128)(2,1)S(1)} %shard_map.78.a_ref), channel_id=1, source_target_pairs={{0,8},{8,0},{1,9},{9,1},{2,10},{10,2},{3,11},{11,3},{4,12},{12,4},... | collective-permute-start | bytes 73736 | tf_op jit(solution)/shard_map/ppermute | solution.py:408
  41.0 5.0 %collective-permute-start.12 = (bf16[24,512]{1,0:T(8,128)(2,1)S(1)}, bf16[24,512]{1,0:T(8,128)(2,1)S(1)}, u32[]{:S(2)}, u32[]{:S(2)}) collective-permute-start(bf16[24,512]{1,0:T(8,128)(2,1)S(1)} %shard_map.78.a_ref), channel_id=1, source_target_pairs={{0,72},{8,64},{64,8},{72,0},{1,73},{9,65},{65,9},{73,1},{2,74},{10... | collective-permute-start | bytes 73736 | tf_op jit(solution)/shard_map/ppermute | solution.py:408
  43.0 3.8 %collective-permute-start.11 = (bf16[24,512]{1,0:T(8,128)(2,1)S(1)}, bf16[24,512]{1,0:T(8,128)(2,1)S(1)}, u32[]{:S(2)}, u32[]{:S(2)}) collective-permute-start(bf16[24,512]{1,0:T(8,128)(2,1)S(1)} %shard_map.78.a_ref), channel_id=1, source_target_pairs={{0,64},{64,0},{1,65},{65,1},{2,66},{66,2},{3,67},{67,3},{4,68},{68... | collective-permute-start | bytes 73736 | tf_op jit(solution)/shard_map/ppermute | solution.py:408

commit v4 on v3

--- a/solution.py
+++ b/solution.py
@@ -21,7 +21,7 @@
 OUTER = (0, 1, HX - 2, HX - 1)
 VMEM_LIMIT = 32 * 1024 * 1024
 FLOPS = 5_000_000_000
-VMEM_ALL = 60 * 1024 * 1024
+VMEM_SPARE = 55050 * 1024
 
 
 def dot_nt(lhs, rhs):
@@ -79,8 +79,20 @@
         s1[4 * t : 4 * t + 4, 0:CH] = k1_ref[t].astype(F32)
     s1[108:128, :] = jnp.zeros((20, 128), F32)
     k1t = s1[...].T[0:CH].astype(BF16)
-    rep1 = (iota((128, 27 * 128), 0) == iota((128, 27 * 128), 1) // 32).astype(BF16)
-    c1[...] = dot_nn(k1t, rep1)
+    t27, i = iota((128, 128), 0) // 4, iota((128, 128), 0) % 4
+    lane = iota((128, 128), 1)
+    spread = []
+    for kd in range(3):
+        for b in range(5):
+            tap = 2 * b + lane // 64
+            spread.append((t27 == kd * 9 + tap) & (tap <= 8) & (i == lane % 64 // 16))
+    u = lane - 64
+    for h in range(2):
+        for py in range(2):
+            kx, ky = u // 16, u % 16 // 4 - py
+            good = (u >= 0) & (kx <= 2) & (ky >= 0) & (ky <= 2) & (i == u % 4)
+            spread.append((t27 == (2 - 2 * h) * 9 + kx * 3 + ky) & good)
+    c1[...] = dot_nn(k1t, jnp.concatenate([part.astype(BF16) for part in spread], axis=1))
     groups = []
     for g in range(4):
         for j in range(8):
@@ -90,19 +102,25 @@
     rep2 = (iota((128, 2048), 0) == iota((128, 2048), 1) // 16).astype(BF16)
     cb[...] = dot_nn(jnp.concatenate(groups, axis=0).astype(BF16), rep2)
 
-    depth1 = iota((16, 128), 1) % 32
+    depth1 = iota((16, 128), 1) % 16
     depth2 = iota((16, 256), 1) % 16
+    for h in range(2):
+        for n in range(16):
+            row = (n % 2) * 128 + (n // 2) * 16
+            touches = n == 15 - 15 * h
+            for b in range(6):
+                acc = jnp.zeros((16, 128), F32)
+                if b < 5:
+                    for kd in range(3):
+                        at = (kd * 5 + b) * 128
+                        acc = jnp.where(depth1 == n + kd - 1, c1[:, at : at + 128], acc)
+                if b >= 4 and touches:
+                    at = (15 + 2 * h + b - 4) * 128
+                    acc = acc + c1[:, at : at + 128]
+                w1_ref[h, row : row + 16, b * 128 : b * 128 + 128] = acc.astype(BF16)
     for kx in range(3):
         for ky in range(3):
             ts = [kd * 9 + kx * 3 + ky for kd in range(3)]
-            at = (kx * 3 + ky) * 128
-            ones = [c1[:, t * 128 : t * 128 + 128] for t in ts]
-            for d in range(32):
-                acc = jnp.zeros((16, 128), F32)
-                for kd in range(3):
-                    acc = jnp.where(depth1 == d + kd - 1, ones[kd], acc)
-                row = (d % 2) * 256 + (d // 2) * 16
-                w1_ref[row : row + 16, at : at + 128] = acc.astype(BF16)
             at = ((2 - kx) * 3 + 2 - ky) * 256
             backs = [cb[t // 8 * 16 : t // 8 * 16 + 16, t % 8 * 256 : t % 8 * 256 + 256] for t in ts]
             for d in range(16):
@@ -130,11 +148,26 @@
         w2_ref[:, m * 256 : m * 256 + 256] = acc.reshape(256, 256).astype(BF16)
 
 
-def fine_taps(dp, taps, layers):
+def halves_matrix():
+    row, col = iota((128, 256), 0), iota((128, 256), 1)
+    place = row % 32 // 16 * 64 + row // 32 * 16 + row % 16
+    return (place == (col + col // 128 * 64) % 128).astype(BF16)
+
+
+def touch_matrix():
+    row, col = iota((512, 256), 0), iota((512, 256), 1)
+    u = col % 128 - 64
+    lane = jnp.where(col < 128, 64 + u % 4 * 16, u % 4 * 16 + 15)
+    return ((row // 128 == u % 16 // 4) & (row % 128 == lane) & (u >= 0)).astype(BF16)
+
+
+def fine_taps(dp, ds, ft, fs, vt, layers):
     for n in range(layers):
         for t in range(4):
-            rows = dp[pl.ds(n * DROW + 7 + t, HY, stride=2), :]
-            taps[n * HY : n * HY + HY, t * 128 : t * 128 + 128] = rows.astype(BF16)
+            for src, out in ((dp, ft), (ds, fs)):
+                rows = src[pl.ds(n * DROW + 7 + t, HY, stride=2), :]
+                out[n * HY : n * HY + HY, t * 128 : t * 128 + 128] = rows.astype(BF16)
+    vt[...] = dot_nn(ft[...], touch_matrix()).astype(BF16)
 
 
 def coarse_taps(padded, taps, layers):
@@ -146,18 +179,37 @@
                 taps[n * HY : n * HY + HY, lane : lane + 128] = rows.astype(BF16)
 
 
-def fine_layer(taps, rims, x, py):
-    if 0 <= x < NXT:
-        return taps[x * HY : x * HY + HY, py * 128 : py * 128 + 384]
-    n = x + 3 if x < 0 else x - NXT + 3
-    return rims[n * HY : n * HY + HY, py * 128 : py * 128 + 384]
-
-
-def fine_patch(taps, rims, cells, px, py):
-    rows = []
-    for cell in cells:
-        rows.append(jnp.concatenate([fine_layer(taps, rims, 2 * cell + px + kx - 1, py) for kx in range(3)], axis=1))
-    return jnp.concatenate(rows, axis=0)
+def pick(low, first, second):
+    return jnp.where(low, first, second)
+
+
+def patch_blocks(h, py, plain, swapped, touch, rows):
+    lane = iota((rows, 128), 1)
+    low = lane < 64
+    first, second = (plain, swapped) if h == 0 else (swapped, plain)
+    blocks = [pick(low, first(2 * b // 3, 2 * b % 3), second((2 * b + 1) // 3, (2 * b + 1) % 3)) for b in range(4)]
+    zero = jnp.zeros((rows, 128), BF16)
+    edge = pick(lane < 80, touch(0), pick(lane < 96, touch(1), touch(2)))
+    blocks.append(pick(low, first(2, 2), edge if py == 0 else zero))
+    blocks.append(edge if py == 1 else zero)
+    return blocks
+
+
+def store_patch(out, h, at, fine, rims, cell, px, py):
+    def layer(which, x, lanes):
+        if 0 <= x < NXT:
+            return fine[which][x * HY : x * HY + HY, lanes]
+        n = x + 3 if x < 0 else x - NXT + 3
+        return rims[which][n * HY : n * HY + HY, lanes]
+
+    def tap(which):
+        return lambda kx, ky: layer(which, 2 * cell + px + kx - 1, slice((py + ky) * 128, (py + ky) * 128 + 128))
+
+    def touch(kx):
+        return layer(2, 2 * cell + px + kx - 1, slice(h * 128, h * 128 + 128))
+
+    for b, block in enumerate(patch_blocks(h, py, tap(0), tap(1), touch, HY)):
+        out[h, at : at + HY, b * 128 : b * 128 + 128] = block
 
 
 def coarse_patch(taps, rims, cells):
@@ -171,59 +223,83 @@
     return jnp.concatenate(rows, axis=0)
 
 
-def pooled_sum(pre):
-    total = jnp.zeros((256, 128), F32)
-    for c in range(4):
-        part = pre[:, c * 128 : c * 128 + 128]
-        act = jnp.where(part > 0, part, LEAK * part).astype(BF16).astype(F32)
-        total = total + act[0:256] + act[256:512]
-    return total * 0.125
-
-
-def back_through(pre, back):
-    both = jnp.concatenate([back, back], axis=0)
+def pooled_sum(pres):
+    parts = []
+    for pre in pres:
+        total = jnp.zeros((128, 128), F32)
+        for c in range(4):
+            part = pre[:, c * 128 : c * 128 + 128]
+            act = jnp.where(part > 0, part, LEAK * part).astype(BF16).astype(F32)
+            total = total + act[0:128] + act[128:256]
+        parts.append(total * 0.125)
+    return jnp.concatenate(parts, axis=0)
+
+
+def back_through(h, pre, back):
+    part = back[h * 128 : h * 128 + 128]
+    both = jnp.concatenate([part, part], axis=0)
     low = LEAK * both
     return [jnp.where(pre[:, c * 128 : c * 128 + 128] > 0, both, low).astype(BF16) for c in range(4)]
 
 
-def tap_kernel(d_ref, c_ref, ft_ref, ct_ref, dp, cp):
-    for x in range(NXT):
-        dp[x * DROW + 8 : x * DROW + 8 + NYT, :] = d_ref[x].astype(F32)
+def tap_kernel(d_ref, c_ref, ft_ref, fs_ref, vt_ref, ct_ref, dp, ds, cp):
+    both = dot_nn(d_ref[...].reshape(NXT * NYT, 128), halves_matrix())
+    for n, out in enumerate((dp, ds)):
+        for x in range(NXT):
+            out[x * DROW + 8 : x * DROW + 8 + NYT, :] = both[x * NYT : x * NYT + NYT, n * 128 : n * 128 + 128]
+        for y in (7, 8 + NYT):
+            out[pl.ds(y, NXT, stride=DROW), :] = jnp.zeros((NXT, 128), F32)
     for half in range(2):
         for x in range(HX):
             at = x * CROW + 8
             cp[half, at : at + HY, :] = c_ref[x, :, half * 128 : half * 128 + 128].astype(F32)
-    fine_taps(dp, ft_ref, NXT)
+    fine_taps(dp, ds, ft_ref, fs_ref, vt_ref, NXT)
     coarse_taps(cp, ct_ref, HX)
 
 
-def set_row(ref, block, lanes, row, value):
+def set_row(ref, block, lanes, row, value, tap=None):
     old = ref[block : block + 16, lanes].astype(F32)
-    ref[block : block + 16, lanes] = jnp.where(iota((16, 128), 0) == row, value, old).astype(BF16)
-
-
-def inner_kernel(ft_in, ct_in, lo_ref, hi_ref, w1_ref, wb_ref, ft, ct, pool_ref, g1_ref, ls, hs, bpre):
+    where = iota(old.shape, 0) == row
+    if tap is not None:
+        where = where & (iota(old.shape, 1) % 16 // 4 == tap)
+    ref[block : block + 16, lanes] = jnp.where(where, value, old).astype(BF16)
+
+
+def inner_kernel(
+    ft_in, fs_in, vt_in, ct_in, lo_ref, hi_ref, w1_ref, wb_ref, ft, fs, vt, ct, pool_ref, g1_ref, ls, hs, ys, pa, bpre
+):
     ls[...] = lo_ref[...].astype(F32)
     hs[...] = hi_ref[...].astype(F32)
+    touch = touch_matrix()
+    for n, rows, t in ((0, lo_ref[64:96, :], 0), (1, hi_ref[0:32, :], 3)):
+        both = dot_nn(rows, halves_matrix())
+        ys[n, :, 0:256] = both
+        ys[n, :, 256:512] = dot_nn(both[:, 0:128].astype(BF16), touch[t * 128 : t * 128 + 128])
     for x in range(NXT):
-        set_row(ft, x * HY, slice(0, 128), 0, ls[64 + x : 65 + x, :])
-        set_row(ft, x * HY + 16, slice(384, 512), 15, hs[x : x + 1, :])
+        for n, block, row, t in ((0, x * HY, 0, 0), (1, x * HY + 16, 15, 3)):
+            lanes = slice(t * 128, t * 128 + 128)
+            set_row(ft, block, lanes, row, ys[n, x : x + 1, 0:128])
+            set_row(fs, block, lanes, row, ys[n, x : x + 1, 128:256])
+            set_row(vt, block, slice(0, 256), row, ys[n, x : x + 1, 256:512], t)
     for x in range(HX):
         for half in range(2):
             at = 96 + half * 16 + x
             set_row(ct, x * HY, slice(half * 128, half * 128 + 128), 0, ls[at : at + 1, :])
             set_row(ct, x * HY + 16, slice(512 + half * 128, 640 + half * 128), 15, hs[at : at + 1, :])
     back = dot_nt(wb_ref[...], coarse_patch(ct, None, INNER)).astype(BF16).astype(F32) * 0.125
-    patches = []
     for g in range(3):
-        cells = INNER[4 * g : 4 * g + 4]
-        group = [fine_patch(ft, None, cells, px, py) for px in range(2) for py in range(2)]
-        pre = dot_nt(w1_ref[...], jnp.concatenate(group, axis=0))
-        pool_ref[:, g * 128 : g * 128 + 128] = pooled_sum(pre).astype(BF16)
-        for c, part in enumerate(back_through(pre, back[:, g * 128 : g * 128 + 128])):
-            bpre[:, (g * 4 + c) * 128 : (g * 4 + c) * 128 + 128] = part
-        patches += group
-    g1_ref[...] = dot_nn(bpre[...], jnp.concatenate(patches, axis=0))
+        for h in range(2):
+            for c in range(4):
+                for n in range(4):
+                    at = (g * 4 + c) * 128 + n * HY
+                    store_patch(pa, h, at, (ft, fs, vt), None, INNER[4 * g + n], c // 2, c % 2)
+        pres = [dot_nt(w1_ref[h], pa[h, g * 512 : g * 512 + 512, :]) for h in range(2)]
+        pool_ref[:, g * 128 : g * 128 + 128] = pooled_sum(pres).astype(BF16)
+        for h in range(2):
+            for c, part in enumerate(back_through(h, pres[h], back[:, g * 128 : g * 128 + 128])):
+                bpre[h, :, (g * 4 + c) * 128 : (g * 4 + c) * 128 + 128] = part
+    for h in range(2):
+        g1_ref[h] = dot_nn(bpre[h], pa[h])
 
 
 def split_dot(select, values):
@@ -233,95 +309,144 @@
 
 
 def extract(g1, g2, out_ref, a1, a2):
-    depth1 = iota((16, 128), 1) % 32
+    depth1 = iota((16, 128), 1) % 16
     depth2 = iota((16, 256), 1) % 16
+    row, col = iota((256, 640), 0), iota((256, 640), 1)
+    u = row % 128 - 64
+    tap = u // 16 * 3 + u % 16 // 4 - row // 128
+    ky = u % 16 // 4 - row // 128
+    good = (u >= 0) & (u < 48) & (ky >= 0) & (ky <= 2)
+    place = (good & (col == tap // 2 * 128 + tap % 2 * 64 + u % 4 * 16)).astype(BF16)
+    touch = jnp.concatenate([g1[0, 240:256, 512:768], g1[1, 0:16, 512:768]], axis=0)
+    high = touch.astype(BF16)
+    touch = dot_nn(high, place) + dot_nn((touch - high.astype(F32)).astype(BF16), place)
+    for b in range(5):
+        lanes = slice(b * 128, b * 128 + 128)
+        total = [touch[16:32, lanes], jnp.zeros((16, 128), F32), touch[0:16, lanes]]
+        for h in range(2):
+            acc = [jnp.zeros((16, 128), F32)] * 3
+            for n in range(16):
+                row = (n % 2) * 128 + (n // 2) * 16
+                part = g1[h, row : row + 16, lanes]
+                acc = [jnp.where(depth1 == n + kd - 1, part, acc[kd]) for kd in range(3)]
+            total = [total[kd] + acc[kd] for kd in range(3)]
+        for kd in range(3):
+            a1[(b * 3 + kd) * 16 : (b * 3 + kd) * 16 + 16, :] = total[kd]
     for m in range(9):
-        acc = [jnp.zeros((16, 128), F32)] * 3
-        for d in range(32):
-            row = (d % 2) * 256 + (d // 2) * 16
-            part = g1[row : row + 16, m * 128 : m * 128 + 128]
-            acc = [jnp.where(depth1 == d + kd - 1, part, acc[kd]) for kd in range(3)]
-        for kd in range(3):
-            a1[(m * 3 + kd) * 16 : (m * 3 + kd) * 16 + 16, :] = acc[kd]
         acc = [jnp.zeros((16, 256), F32)] * 3
         for d in range(16):
             part = g2[d * 16 : d * 16 + 16, m * 256 : m * 256 + 256]
             acc = [jnp.where(depth2 == d + 1 - kd, part, acc[kd]) for kd in range(3)]
         for kd in range(3):
             a2[(m * 3 + kd) * 16 : (m * 3 + kd) * 16 + 16, :] = acc[kd]
-    a1[432:512, :] = jnp.zeros((80, 128), F32)
+    a1[240:512, :] = jnp.zeros((272, 128), F32)
     a2[432:512, :] = jnp.zeros((80, 256), F32)
     pick2 = (iota((16, 256), 1) // 16 == iota((16, 256), 0)).astype(BF16)
-    pick1 = (iota((16, 128), 1) // 32 == iota((16, 128), 0)).astype(BF16)
+    pick1 = (iota((16, 128), 1) // 16 == iota((16, 128), 0)).astype(BF16)
     two = split_dot(pick2, a2[...])
     one = split_dot(pick1, a1[...])[0:8]
     out_ref[...] = jnp.concatenate([two, one], axis=0).astype(BF16)
 
 
 def edge_kernel(
-    ft, ct, xlo_ref, xhi_ref, w1_ref, wb_ref, pool_ref, g1_ref,
-    grad_ref, outer_ref, rims, dp, cp, corner, crims, g1, g2, a1, a2,
+    ft, fs, vt, ct, xlo_ref, xhi_ref, w1_ref, wb_ref, pool_ref, g1_ref,
+    grad_ref, outer_ref, rft, rfs, rvt, dp, ds, cp, corner, swapped, crims, pa, g1, g2, a1, a2,
 ):
     for zone, src in enumerate((xlo_ref, xhi_ref)):
-        corner[zone * 32 : zone * 32 + 32, :] = src[256:288, :].astype(F32)
+        both = dot_nn(jnp.concatenate([src[0:192, :], src[256:288, :]], axis=0), halves_matrix())
         for k in range(3):
             at = (zone * 3 + k) * DROW + 8
-            dp[at : at + NYT, :] = src[k * 64 : k * 64 + 64, :].astype(F32)
+            dp[at : at + NYT, :] = both[k * 64 : k * 64 + 64, 0:128]
+            ds[at : at + NYT, :] = both[k * 64 : k * 64 + 64, 128:256]
+        swapped[0] = both[192:224, 0:128]
+        swapped[1] = both[192:224, 128:256]
+        corner[zone * 32 : zone * 32 + 32, :] = src[256:288, :].astype(F32)
         for side, y in ((0, 5), (1, 8 + NYT)):
             for ky in range(3):
                 for kx in range(3):
                     row = (zone * 3 + kx) * DROW + y + ky
-                    at = zone * 32 + side * 9 + 3 * ky + kx
-                    dp[row : row + 1, :] = corner[at : at + 1, :]
+                    at = side * 9 + 3 * ky + kx
+                    dp[row : row + 1, :] = swapped[0, at : at + 1, :]
+                    ds[row : row + 1, :] = swapped[1, at : at + 1, :]
         for half in range(2):
             at = zone * CROW + 8
             cp[half, at : at + HY, :] = src[192 + half * 32 : 224 + half * 32, :].astype(F32)
             for side, y in ((0, 7), (1, 8 + HY)):
                 at = zone * 32 + 18 + side * 2 + half
                 cp[half, zone * CROW + y : zone * CROW + y + 1, :] = corner[at : at + 1, :]
-    fine_taps(dp, rims, 6)
+    fine_taps(dp, ds, rft, rfs, rvt, 6)
     coarse_taps(cp, crims, 2)
     cpatch = coarse_patch(ct, crims, OUTER)
     back = dot_nt(wb_ref[...], cpatch).astype(BF16).astype(F32) * 0.125
-    group = [fine_patch(ft, rims, OUTER, px, py) for px in range(2) for py in range(2)]
-    group = jnp.concatenate(group, axis=0)
-    pre = dot_nt(w1_ref[...], group)
-    mean = pooled_sum(pre).astype(BF16)
+    for h in range(2):
+        for c in range(4):
+            for n, cell in enumerate(OUTER):
+                store_patch(pa, h, c * 128 + n * HY, (ft, fs, vt), (rft, rfs, rvt), cell, c // 2, c % 2)
+    pres = [dot_nt(w1_ref[h], pa[h]) for h in range(2)]
+    mean = pooled_sum(pres).astype(BF16)
     outer_ref[...] = mean
-    g1[...] = g1_ref[...] + dot_nn(jnp.concatenate(back_through(pre, back), axis=1), group)
+    for h in range(2):
+        g1[h] = g1_ref[h] + dot_nn(jnp.concatenate(back_through(h, pres[h], back), axis=1), pa[h])
     pooled = jnp.concatenate([pool_ref[...], mean], axis=1)
     g2[...] = dot_nn(pooled, jnp.concatenate([coarse_patch(ct, None, INNER), cpatch], axis=0))
     extract(g1, g2, grad_ref, a1, a2)
 
 
 def rim_kernel(
-    after_ref, up_ref, down_ref, lo_ref, hi_ref, xlo_ref, xhi_ref, ft_ref, rims_ref, w1_ref, edge_ref, col, corner, rim
+    after_ref, up_ref, down_ref, lo_ref, hi_ref, xlo_ref, xhi_ref, ft, fs, vt, rft, rfs, rvt, w1_ref,
+    edge_ref, col, raw, corner, tv, rim,
 ):
+    raw[...] = jnp.zeros(raw.shape, F32)
     for k in range(3):
-        col[k, 8:40, :] = lo_ref[k * 32 : k * 32 + 32, :].astype(F32)
-        col[5 + k, 8:40, :] = hi_ref[k * 32 : k * 32 + 32, :].astype(F32)
-    col[3, 8:40, :] = down_ref[0:32, :].astype(F32)
-    col[4, 8:40, :] = up_ref[64:96, :].astype(F32)
+        raw[k, 8:40, :] = lo_ref[k * 32 : k * 32 + 32, :].astype(F32)
+        raw[5 + k, 8:40, :] = hi_ref[k * 32 : k * 32 + 32, :].astype(F32)
+    raw[3, 8:40, :] = down_ref[0:32, :].astype(F32)
+    raw[4, 8:40, :] = up_ref[64:96, :].astype(F32)
     for src, row in ((xlo_ref, 5), (xhi_ref, 40)):
         corner[...] = src[...].astype(F32)
         for kx in range(3):
             for ky in range(3):
-                col[ky, row + kx : row + kx + 1, :] = corner[256 + 3 * ky + kx : 257 + 3 * ky + kx, :]
-                col[5 + ky, row + kx : row + kx + 1, :] = corner[265 + 3 * ky + kx : 266 + 3 * ky + kx, :]
-            col[3, row + kx : row + kx + 1, :] = corner[kx * 64 : kx * 64 + 1, :]
-            col[4, row + kx : row + kx + 1, :] = corner[kx * 64 + 63 : kx * 64 + 64, :]
-    for px in range(2):
-        for py in range(2):
-            at = (px * 2 + py) * 128
-            rim[at : at + 64, :] = fine_patch(ft_ref, rims_ref, (-1, HX), px, py)
-            for side in range(2):
-                for kx in range(3):
-                    for ky in range(3):
-                        rows = col[side * 4 + py + ky, pl.ds(5 + px + kx, 18, stride=2), :]
-                        rows = jnp.concatenate([rows, jnp.zeros((14, 128), F32)], axis=0)
-                        lane = (kx * 3 + ky) * 128
-                        rim[at + 64 + side * 32 : at + 96 + side * 32, lane : lane + 128] = rows.astype(BF16)
-    edge_ref[...] = pooled_sum(dot_nt(w1_ref[...], rim[...])).T.astype(BF16)
+                raw[ky, row + kx : row + kx + 1, :] = corner[256 + 3 * ky + kx : 257 + 3 * ky + kx, :]
+                raw[5 + ky, row + kx : row + kx + 1, :] = corner[265 + 3 * ky + kx : 266 + 3 * ky + kx, :]
+            raw[3, row + kx : row + kx + 1, :] = corner[kx * 64 : kx * 64 + 1, :]
+            raw[4, row + kx : row + kx + 1, :] = corner[kx * 64 + 63 : kx * 64 + 64, :]
+    both = dot_nn(raw[...].reshape(8 * 48, 128).astype(BF16), halves_matrix())
+    touch = touch_matrix()
+    for side in range(2):
+        parts = []
+        for t in range(4):
+            part = both[(side * 4 + t) * 48 : (side * 4 + t) * 48 + 48]
+            col[0, side * 4 + t] = part[:, 0:128]
+            col[1, side * 4 + t] = part[:, 128:256]
+            parts.append(part[:, 0:128].astype(BF16))
+        ends = dot_nn(jnp.concatenate(parts, axis=1), touch)
+        tv[side, 0] = ends[:, 0:128]
+        tv[side, 1] = ends[:, 128:256]
+    blank = jnp.zeros((14, 128), F32)
+    for h in range(2):
+        for px in range(2):
+            for py in range(2):
+                at = (px * 2 + py) * 128
+                for n, cell in enumerate((-1, HX)):
+                    store_patch(rim, h, at + n * HY, (ft, fs, vt), (rft, rfs, rvt), cell, px, py)
+                for side in range(2):
+
+                    def tap(which):
+                        def get(kx, ky):
+                            rows = col[which, side * 4 + py + ky, pl.ds(5 + px + kx, 18, stride=2), :]
+                            return jnp.concatenate([rows, blank], axis=0).astype(BF16)
+
+                        return get
+
+                    def ends_of(kx):
+                        rows = tv[side, h, pl.ds(5 + px + kx, 18, stride=2), :]
+                        return jnp.concatenate([rows, blank], axis=0).astype(BF16)
+
+                    top = at + 64 + side * 32
+                    for b, block in enumerate(patch_blocks(h, py, tap(0), tap(1), ends_of, 32)):
+                        rim[h, top : top + 32, b * 128 : b * 128 + 128] = block
+    pres = [dot_nt(w1_ref[h], rim[h]) for h in range(2)]
+    edge_ref[...] = pooled_sum(pres).T.astype(BF16)
 
 
 def feature_kernel(after_ref, edge_ref, pool_ref, outer_ref, w2_ref, feat_ref, token_ref, pp, pt):
@@ -362,9 +487,9 @@
     for kd in range(3):
         for kx in range(3):
             for ky in range(3):
-                t = kd * 9 + kx * 3 + ky
-                at = ((kx * 3 + ky) * 3 + kd) * 16
-                g1_ref[t] = total[16:20, at : at + 16]
+                t, m = kd * 9 + kx * 3 + ky, kx * 3 + ky
+                at, row = (m // 2 * 3 + kd) * 16, 16 + m % 2 * 4
+                g1_ref[t] = total[row : row + 4, at : at + 16]
                 at = (((2 - kx) * 3 + 2 - ky) * 3 + kd) * 16
                 g2_ref[t] = total[0:16, at : at + 16]
 
@@ -426,21 +551,22 @@
             buffer16(2, NXT, 16, 128), buffer16(2, HX, 16, 256),
             buffer(NXT * 16, 128), buffer(2, HX * 16, 128), pltpu.SemaphoreType.DMA((4,)),
         ),
-        limit=VMEM_ALL,
+        limit=VMEM_SPARE,
         flops=FLOPS,
     )(d, c)
     lo, hi = shift(yup, TY, 1), shift(ydown, TY, -1)
     w1, wb = call(
         weights_kernel,
         [VM] * 2,
-        (struct((512, 1152), BF16), struct((256, 2304), BF16)),
-        (buffer(128, 128), buffer(16, 27 * 128), buffer(64, 2048)),
+        (struct((2, 256, 768), BF16), struct((256, 2304), BF16)),
+        (buffer(128, 128), buffer(16, 19 * 128), buffer(64, 2048)),
     )(k1, k2)
-    ft, ct = call(
+    fine = struct((NXT * HY, 512), BF16)
+    taps = call(
         tap_kernel,
         [VM] * 2,
-        (struct((NXT * HY, 512), BF16), struct((HX * HY, 768), BF16)),
-        (buffer(NXT * DROW, 128), buffer(2, HX * CROW, 128)),
+        (fine, fine, struct((NXT * HY, 256), BF16), struct((HX * HY, 768), BF16)),
+        (buffer(NXT * DROW, 128), buffer(NXT * DROW, 128), buffer(2, HX * CROW, 128)),
     )(d, c)
     message = struct((288, 128), BF16)
     up, down = call(
@@ -448,26 +574,28 @@
         [VM] * 4 + [ANY] * 2,
         (message, message),
         (buffer(128, 128), buffer(128, 128), buffer(32, 128)),
-    )(d, c, lo, hi, w1, ct)
+    )(d, c, lo, hi, w1, taps[3])
     xlo, xhi = shift(up, TX, 1), shift(down, TX, -1)
 
-    ft, ct, pool, g1 = call(
+    *taps, pool, g1 = call(
         inner_kernel,
-        [VM] * 6,
-        (struct(ft.shape, BF16), struct(ct.shape, BF16), struct((256, 384), BF16), struct((512, 1152), F32)),
-        (buffer(128, 128), buffer(128, 128), buffer16(512, 1536)),
-        aliases={0: 0, 1: 1},
-    )(ft, ct, lo, hi, w1, wb)
+        [VM] * 8,
+        tuple(struct(tap.shape, BF16) for tap in taps) + (struct((256, 384), BF16), struct((2, 256, 768), F32)),
+        (buffer(128, 128), buffer(128, 128), buffer(2, 32, 512), buffer16(2, 1536, 768), buffer16(2, 256, 1536)),
+        aliases={0: 0, 1: 1, 2: 2, 3: 3},
+    )(*taps, lo, hi, w1, wb)
     gradient = struct((24, 512), BF16)
-    grads, outer, rims = call(
+    rim = struct((6 * HY, 512), BF16)
+    grads, outer, *rims = call(
         edge_kernel,
-        [VM] * 8,
-        (gradient, struct((256, 128), BF16), struct((6 * HY, 512), BF16)),
+        [VM] * 10,
+        (gradient, struct((256, 128), BF16), rim, rim, struct((6 * HY, 256), BF16)),
         (
-            buffer(6 * DROW, 128), buffer(2, 2 * CROW, 128), buffer(64, 128), buffer16(2 * HY, 768),
-            buffer(512, 1152), buffer(256, 2304), buffer(512, 128), buffer(512, 256),
+            buffer(6 * DROW, 128), buffer(6 * DROW, 128), buffer(2, 2 * CROW, 128), buffer(64, 128), buffer(2, 32, 128),
+            buffer16(2 * HY, 768), buffer16(2, 512, 768),
+            buffer(2, 256, 768), buffer(256, 2304), buffer(512, 128), buffer(512, 256),
         ),
-    )(ft, ct, xlo, xhi, w1, wb, pool, g1)
+    )(*taps, xlo, xhi, w1, wb, pool, g1)
 
     grads = call(add_two_kernel, [VM] * 2, gradient)(grads, partner(grads, "core", 1))
     w2 = call(
@@ -478,10 +606,12 @@
     )(k2, grads)
     edge = call(
         rim_kernel,
-        [ANY] + [VM] * 9,
+        [ANY] + [VM] * 13,
         struct((128, 256), BF16),
-        (buffer(8, 48, 128), buffer(288, 128), buffer16(512, 1152)),
-    )(grads, yup, ydown, lo, hi, xlo, xhi, ft, rims, w1)
+        (
+            buffer(2, 8, 48, 128), buffer(8, 48, 128), buffer(288, 128), buffer(2, 2, 48, 128), buffer16(2, 512, 768),
+        ),
+    )(grads, yup, ydown, lo, hi, xlo, xhi, *taps[:3], *rims, w1)
     others = [partner(grads, "z", bits) for bits in (1, 3, 2)]
     grads = call(add_four_kernel, [VM] * 4 + [ANY] * 2, gradient)(grads, *others, edge, w2)
     feat, token = call(

time: 47.8 us -> 45.9 us (0.960)
  Pallas kernels: 16.2 us -> 15.2 us
  starting transfers between devices: 21.3 us -> 20.3 us
    ppermute x10, starting transfers between devices: 12 us -> 11 us  [partner(): return lax.ppermute(value, axes, [(i, i ^ bits) for i in range(n)])]
    pallas_call x1, Pallas kernels: 1.91 us -> 1.3 us  [on_device(): call(pack_y_kernel, [ANY] * 2, (message, message), (buffer16(2, NXT, 16,...]
    ppermute x10, waiting for transfers between devices: 8.81 us -> 9.36 us  [partner(): return lax.ppermute(value, axes, [(i, i ^ bits) for i in range(n)])]
  transfers between devices with their start and end apart: 14 -> 14, of which waited for: 9 -> 7; matrix products, arithmetic and copies ran while one was open for 0% -> 0% of each run, Pallas kernels for 21% -> 22%
where the time goes in v4:
time: 45.9 us; the launch traced here: 45.7 us
  starting transfers between devices  20.3 us (44%)
  Pallas kernels  15.2 us (33%)
  waiting for transfers between devices  9.37 us (20%)
  between operations  0.8 us (2%)
    ppermute x10, starting transfers between devices, partner(): return lax.ppermute(value, axes, [(i, i ^ bits) for i in range(n)])  11 us
    ppermute x10, waiting for transfers between devices, partner(): return lax.ppermute(value, axes, [(i, i ^ bits) for i in range(n)])  9.36 us
    ppermute x4, starting transfers between devices, shift(): return lax.ppermute(value, axes, [(i, (i + step) % n) for i in range(n)])  9.3 us
    pallas_call x1, Pallas kernels, on_device(): call(inner_kernel, [VM] * 8, tuple((struct(tap.shape, BF16) for tap in ta...  4.5 us
    pallas_call x1, Pallas kernels, on_device(): call(edge_kernel, [VM] * 10, (gradient, struct((256, 128), BF16), rim, ri...  2.97 us
    pallas_call x1, Pallas kernels, on_device(): call(feature_kernel, [ANY] + [VM] * 4, (struct((HX, HY, 256), BF16), stru...  1.6 us
    pallas_call x1, Pallas kernels, on_device(): call(tap_kernel, [VM] * 2, (fine, fine, struct((NXT * HY, 256), BF16), st...  1.37 us
    pallas_call x1, Pallas kernels, on_device(): call(pack_y_kernel, [ANY] * 2, (message, message), (buffer16(2, NXT, 16,...  1.3 us
  transfers between devices with their start and end apart: 14, of which 7 were waited for; matrix products, arithmetic and copies ran while one was open for 0% of the time, Pallas kernels for 22%

profile of v4, /device:TPU:0, one launch (start us, length us, event | category | flops | bytes accessed | tf_op | source)
XLA Modules:
  0.0 45.7 jit_solution(11785073770986681473)
XLA Ops:
  0.7 1.3 %shard_map.68 = (bf16[128,128]{1,0:T(8,128)(2,1)S(1)}, bf16[128,128]{1,0:T(8,128)(2,1)S(1)}) custom-call(bf16[32,64,128]{2,1,0:T(8,128)(2,1)} %bitcast.15, bf16[16,32,256]{2,1,0:T(8,128)(2,1)} %bitcast.18), custom_call_target="tpu_custom_call" | custom-call | flops 5000000000 | bytes 1000000 | tf_op jit(solution)/shard_map/pallas_call | solution.py:546
  2.0 3.6 %collective-permute-start.1 = (bf16[128,128]{1,0:T(8,128)(2,1)S(1)}, bf16[128,128]{1,0:T(8,128)(2,1)S(1)}, u32[]{:S(2)}, u32[]{:S(2)}) collective-permute-start(bf16[128,128]{1,0:T(8,128)(2,1)S(1)} %get-tuple-element.33.down_ref), channel_id=1, source_target_pairs={{0,7},{1,0},{2,1},{3,2},{4,3},{5,4},{6,5},{7,6},{8,15},{9,8},{10,9... | collective-permute-start | bytes 98312 | tf_op jit(solution)/shard_map/ppermute | solution.py:528
  5.6 1.4 %shard_map.67 = (bf16[1024,512]{1,0:T(8,128)(2,1)S(1)}, bf16[1024,512]{1,0:T(8,128)(2,1)S(1)}, bf16[1024,256]{1,0:T(8,128)(2,1)S(1)}, bf16[512,768]{1,0:T(8,128)(2,1)S(1)}) custom-call(bf16[32,64,128]{2,1,0:T(8,128)(2,1)S(1)} %bitcast.16, bf16[16,32,256]{2,1,0:T(8,128)(2,1)S(1)} %bitcast.19), custom_call_target="tpu_custom_call" | custom-call | tf_op jit(solution)/shard_map/pallas_call | solution.py:565
  7.0 0.7 %shard_map.69 = (bf16[2,256,768]{2,1,0:T(8,128)(2,1)S(1)}, bf16[256,2304]{1,0:T(8,128)(2,1)S(1)}) custom-call(bf16[27,4,16]{2,1,0:T(4,128)(2,1)S(1)} %bitcast.23, bf16[27,16,16]{2,1,0:T(8,128)(2,1)S(1)} %bitcast.21), custom_call_target="tpu_custom_call" | custom-call | tf_op jit(solution)/shard_map/pallas_call | solution.py:558
  7.8 3.3 %collective-permute-start.2 = (bf16[288,128]{1,0:T(8,128)(2,1)S(1)}, bf16[288,128]{1,0:T(8,128)(2,1)S(1)}, u32[]{:S(2)}, u32[]{:S(2)}) collective-permute-start(bf16[288,128]{1,0:T(8,128)(2,1)S(1)} %get-tuple-element.40), channel_id=1, source_target_pairs={{0,8},{8,16},{16,24},{24,32},{32,40},{40,48},{48,56},{56,0},{1,9},... | collective-permute-start | bytes 221192 | tf_op jit(solution)/shard_map/ppermute | solution.py:528
  11.1 2.4 %collective-permute-start.3 = (bf16[288,128]{1,0:T(8,128)(2,1)S(1)}, bf16[288,128]{1,0:T(8,128)(2,1)S(1)}, u32[]{:S(2)}, u32[]{:S(2)}) collective-permute-start(bf16[288,128]{1,0:T(8,128)(2,1)S(1)} %get-tuple-element.41), channel_id=1, source_target_pairs={{0,56},{8,0},{16,8},{24,16},{32,24},{40,32},{48,40},{56,48},{1,57}... | collective-permute-start | bytes 221192 | tf_op jit(solution)/shard_map/ppermute | solution.py:528
  13.5 4.5 %shard_map.70 = (bf16[1024,512]{1,0:T(8,128)(2,1)S(1)}, bf16[1024,512]{1,0:T(8,128)(2,1)S(1)}, bf16[1024,256]{1,0:T(8,128)(2,1)S(1)}, bf16[512,768]{1,0:T(8,128)...) custom-call(bf16[1024,512]{1,0:T(8,128)(2,1)S(1)} %get-tuple-element, ...), custom_call_target="tpu_custom_call", output_to_operand_aliasing={{0}: (0, {}), {1}: (1, {}), {2}: (2, {}), {3}: (3, {})} | custom-call | tf_op jit(solution)/shard_map/pallas_call | solution.py:580
  18.0 3.0 %shard_map.72 = (bf16[24,512]{1,0:T(8,128)(2,1)S(1)}, bf16[256,128]{1,0:T(8,128)(2,1)S(1)}, bf16[192,512]{1,0:T(8,128)(2,1)S(1)}, bf16[192,512]{1,0:T(8,128)(2,1)S(1)}, bf16[192,256]{1,0:T(8,128)(2,1)S(1)}) custom-call(bf16[1024,512]{1,0:T(8,128)(2,1)S(1)} %get-tuple-element.36.ft, bf16[1024,512]{1,0:T(8,128)(2,1)S(1)} %get-tuple-element.37.fs, ...), custom_call_target="tpu_custom_call" | custom-call | tf_op jit(solution)/shard_map/pallas_call | solution.py:589
  21.1 1.2 %collective-permute-done.4.b_ref = bf16[24,512]{1,0:T(8,128)(2,1)S(1)} collective-permute-done((bf16[24,512]{1,0:T(8,128)(2,1)S(1)}, bf16[24,512]{1,0:T(8,128)(2,1)S(1)}, u32[]{:S(2)}, u32[]{:S(2)}) %collective-permute-start.4) | collective-permute-done | bytes 24608 | tf_op jit(solution)/shard_map/ppermute | solution.py:533
  22.3 2.5 %collective-permute-start.7 = (bf16[24,512]{1,0:T(8,128)(2,1)S(1)}, bf16[24,512]{1,0:T(8,128)(2,1)S(1)}, u32[]{:S(2)}, u32[]{:S(2)}) collective-permute-start(bf16[24,512]{1,0:T(8,128)(2,1)S(1)} %shard_map.73.after_ref.a_ref), channel_id=1, source_target_pairs={{0,4},{2,6},{4,0},{6,2},{1,5},{3,7},{5,1},{7,3},{8,12},{10,14},{12... | collective-permute-start | bytes 73736 | tf_op jit(solution)/shard_map/ppermute | solution.py:533
  24.8 1.0 %collective-permute-start.6 = (bf16[24,512]{1,0:T(8,128)(2,1)S(1)}, bf16[24,512]{1,0:T(8,128)(2,1)S(1)}, u32[]{:S(2)}, u32[]{:S(2)}) collective-permute-start(bf16[24,512]{1,0:T(8,128)(2,1)S(1)} %shard_map.73.after_ref.a_ref), channel_id=1, source_target_pairs={{0,6},{2,4},{4,2},{6,0},{1,7},{3,5},{5,3},{7,1},{8,14},{10,12},{12... | collective-permute-start | bytes 73736 | tf_op jit(solution)/shard_map/ppermute | solution.py:533
  25.8 0.7 %shard_map.75.also_ref.w2_ref = bf16[256,2304]{1,0:T(8,128)(2,1)S(1)} custom-call(bf16[27,16,16]{2,1,0:T(8,128)(2,1)S(1)} %bitcast.22, bf16[24,512]{1,0:T(8,128)(2,1)S(1)} %shard_map.73.after_ref.a_ref), custom_call_target="tpu_custom_call" | custom-call | tf_op jit(solution)/shard_map/pallas_call | solution.py:601
  26.6 1.1 %shard_map.74.after_ref.edge_ref = bf16[128,256]{1,0:T(8,128)(2,1)S(1)} custom-call(bf16[24,512]{1,0:T(8,128)(2,1)S(1)} %shard_map.73.after_ref.a_ref, bf16[128,128]{1,0:T(8,128)(2,1)S(1)} %get-tuple-element.32.up_ref, bf16[128,128]{1,0:T(8,128)(2,1)S(1)} %get-tuple-element.33.down_ref, bf16[128,128]{1,0:T(8,128)(2,1)S(1)} %collective-permute-done.lo_ref, ...), custom_call_target="tpu_custom_call" | custom-call | tf_op jit(solution)/shard_map/pallas_call | solution.py:607
  27.7 2.2 %collective-permute-done.6.c_ref = bf16[24,512]{1,0:T(8,128)(2,1)S(1)} collective-permute-done((bf16[24,512]{1,0:T(8,128)(2,1)S(1)}, bf16[24,512]{1,0:T(8,128)(2,1)S(1)}, u32[]{:S(2)}, u32[]{:S(2)}) %collective-permute-start.6) | collective-permute-done | bytes 24608 | tf_op jit(solution)/shard_map/ppermute | solution.py:533
  29.9 2.3 %collective-permute-start.10 = (bf16[24,512]{1,0:T(8,128)(2,1)S(1)}, bf16[24,512]{1,0:T(8,128)(2,1)S(1)}, u32[]{:S(2)}, u32[]{:S(2)}) collective-permute-start(bf16[24,512]{1,0:T(8,128)(2,1)S(1)} %shard_map.76.after_ref.a_ref), channel_id=1, source_target_pairs={{0,32},{16,48},{32,0},{48,16},{1,33},{17,49},{33,1},{49,17},{2,34}... | collective-permute-start | bytes 73736 | tf_op jit(solution)/shard_map/ppermute | solution.py:533
  32.2 1.1 %collective-permute-start.9 = (bf16[24,512]{1,0:T(8,128)(2,1)S(1)}, bf16[24,512]{1,0:T(8,128)(2,1)S(1)}, u32[]{:S(2)}, u32[]{:S(2)}) collective-permute-start(bf16[24,512]{1,0:T(8,128)(2,1)S(1)} %shard_map.76.after_ref.a_ref), channel_id=1, source_target_pairs={{0,48},{16,32},{32,16},{48,0},{1,49},{17,33},{33,17},{49,1},{2,50}... | collective-permute-start | bytes 73736 | tf_op jit(solution)/shard_map/ppermute | solution.py:533
  33.4 1.6 %shard_map.77 = (bf16[16,32,256]{2,1,0:T(8,128)(2,1)}, f32[8,128]{1,0:T(8,128)S(1)}) custom-call(bf16[24,512]{1,0:T(8,128)(2,1)S(1)} %shard_map.76.after_ref.a_ref, bf16[128,256]{1,0:T(8,128)(2,1)S(1)} %shard_map.74.after_ref.edge_ref, bf16[256,384]{1,0:T(8,128)(2,1)S(1)} %get-tuple-element.42.pool_ref, bf16[256,128]{1,0:T(8,128)(2,1)S(1)} %get-tuple-element.48.outer_ref, ...), custom_call_target="tpu_custom_call" | custom-call | tf_op jit(solution)/shard_map/pallas_call | solution.py:617
  35.3 2.0 %collective-permute-done.9.c_ref = bf16[24,512]{1,0:T(8,128)(2,1)S(1)} collective-permute-done((bf16[24,512]{1,0:T(8,128)(2,1)S(1)}, bf16[24,512]{1,0:T(8,128)(2,1)S(1)}, u32[]{:S(2)}, u32[]{:S(2)}) %collective-permute-start.9) | collective-permute-done | bytes 24608 | tf_op jit(solution)/shard_map/ppermute | solution.py:533
  37.3 2.2 %collective-permute-start.13 = (bf16[24,512]{1,0:T(8,128)(2,1)S(1)}, bf16[24,512]{1,0:T(8,128)(2,1)S(1)}, u32[]{:S(2)}, u32[]{:S(2)}) collective-permute-start(bf16[24,512]{1,0:T(8,128)(2,1)S(1)} %shard_map.78.a_ref), channel_id=1, source_target_pairs={{0,8},{8,0},{1,9},{9,1},{2,10},{10,2},{3,11},{11,3},{4,12},{12,4},... | collective-permute-start | bytes 73736 | tf_op jit(solution)/shard_map/ppermute | solution.py:533
  39.4 1.6 %collective-permute-start.12 = (bf16[24,512]{1,0:T(8,128)(2,1)S(1)}, bf16[24,512]{1,0:T(8,128)(2,1)S(1)}, u32[]{:S(2)}, u32[]{:S(2)}) collective-permute-start(bf16[24,512]{1,0:T(8,128)(2,1)S(1)} %shard_map.78.a_ref), channel_id=1, source_target_pairs={{0,72},{8,64},{64,8},{72,0},{1,73},{9,65},{65,9},{73,1},{2,74},{10... | collective-permute-start | bytes 73736 | tf_op jit(solution)/shard_map/ppermute | solution.py:533
  41.1 1.6 %collective-permute-done.13.d_ref = bf16[24,512]{1,0:T(8,128)(2,1)S(1)} collective-permute-done((bf16[24,512]{1,0:T(8,128)(2,1)S(1)}, bf16[24,512]{1,0:T(8,128)(2,1)S(1)}, u32[]{:S(2)}, u32[]{:S(2)}) %collective-permute-start.13) | collective-permute-done | bytes 24608 | tf_op jit(solution)/shard_map/ppermute | solution.py:533
  42.7 1.8 %collective-permute-done.12.c_ref = bf16[24,512]{1,0:T(8,128)(2,1)S(1)} collective-permute-done((bf16[24,512]{1,0:T(8,128)(2,1)S(1)}, bf16[24,512]{1,0:T(8,128)(2,1)S(1)}, u32[]{:S(2)}, u32[]{:S(2)}) %collective-permute-start.12) | collective-permute-done | bytes 24608 | tf_op jit(solution)/shard_map/ppermute | solution.py:533
  44.5 0.4 collective-permute-done.11.b_ref
  44.9 0.8 %shard_map.79 = (f32[27,4,16]{2,1,0:T(4,128)}, f32[27,16,16]{2,1,0:T(8,128)}) custom-call(bf16[24,512]{1,0:T(8,128)(2,1)S(1)} %shard_map.78.a_ref, bf16[24,512]{1,0:T(8,128)(2,1)S(1)} %collective-permute-done.11.b_ref, bf16[24,512]{1,0:T(8,128)(2,1)S(1)} %collective-permute-done.12.c_ref, bf16[24,512]{1,0:T(8,128)(2,1)S(1)} %collective-permute-done.13.d_ref), custom_call_target="tpu_custom_call" | custom-call | tf_op jit(solution)/shard_map/pallas_call | solution.py:628
  (25 shorter events, 0.6 us)
Async XLA Ops:
  0.6 4.9 %copy-start = (bf16[1,32,64,128]{3,2,1,0:T(8,128)(2,1)S(1)}, bf16[1,32,64,128]{3,2,1,0:T(8,128)(2,1)}, u32[]{:S(2)}) copy-start(bf16[1,32,64,128]{3,2,1,0:T(8,128)(2,1)} %param.4) | copy-start | bytes 1572868
  0.6 4.9 %copy-start.1 = (bf16[1,16,32,256]{3,2,1,0:T(8,128)(2,1)S(1)}, bf16[1,16,32,256]{3,2,1,0:T(8,128)(2,1)}, u32[]{:S(2)}) copy-start(bf16[1,16,32,256]{3,2,1,0:T(8,128)(2,1)} %param.7) | copy-start | bytes 786436
  0.7 6.3 %copy-start.2 = (bf16[16,16,3,3,3]{1,0,4,3,2:T(8,128)(2,1)S(1)}, bf16[16,16,3,3,3]{1,0,4,3,2:T(8,128)(2,1)}, u32[]{:S(2)}) copy-start(bf16[16,16,3,3,3]{1,0,4,3,2:T(8,128)(2,1)} %param.6) | copy-start | bytes 41476
  0.7 6.3 %copy-start.3 = (bf16[16,4,3,3,3]{0,1,4,3,2:T(4,128)(2,1)S(1)}, bf16[16,4,3,3,3]{0,1,4,3,2:T(4,128)(2,1)}, u32[]{:S(2)}) copy-start(bf16[16,4,3,3,3]{0,1,4,3,2:T(4,128)(2,1)} %param.5) | copy-start | bytes 10372
  2.0 5.8 %collective-permute-start = (bf16[128,128]{1,0:T(8,128)(2,1)S(1)}, bf16[128,128]{1,0:T(8,128)(2,1)S(1)}, u32[]{:S(2)}, u32[]{:S(2)}) collective-permute-start(bf16[128,128]{1,0:T(8,128)(2,1)S(1)} %get-tuple-element.32.up_ref), channel_id=1, source_target_pairs={{0,1},{1,2},{2,3},{3,4},{4,5},{5,6},{6,7},{7,0},{8,9},{9,10},{10,1... | collective-permute-start | bytes 98312 | tf_op jit(solution)/shard_map/ppermute | solution.py:528
  2.0 5.7 %collective-permute-start.1 = (bf16[128,128]{1,0:T(8,128)(2,1)S(1)}, bf16[128,128]{1,0:T(8,128)(2,1)S(1)}, u32[]{:S(2)}, u32[]{:S(2)}) collective-permute-start(bf16[128,128]{1,0:T(8,128)(2,1)S(1)} %get-tuple-element.33.down_ref), channel_id=1, source_target_pairs={{0,7},{1,0},{2,1},{3,2},{4,3},{5,4},{6,5},{7,6},{8,15},{9,8},{10,9... | collective-permute-start | bytes 98312 | tf_op jit(solution)/shard_map/ppermute | solution.py:528
  7.8 10.2 %collective-permute-start.2 = (bf16[288,128]{1,0:T(8,128)(2,1)S(1)}, bf16[288,128]{1,0:T(8,128)(2,1)S(1)}, u32[]{:S(2)}, u32[]{:S(2)}) collective-permute-start(bf16[288,128]{1,0:T(8,128)(2,1)S(1)} %get-tuple-element.40), channel_id=1, source_target_pairs={{0,8},{8,16},{16,24},{24,32},{32,40},{40,48},{48,56},{56,0},{1,9},... | collective-permute-start | bytes 221192 | tf_op jit(solution)/shard_map/ppermute | solution.py:528
  11.1 7.0 %collective-permute-start.3 = (bf16[288,128]{1,0:T(8,128)(2,1)S(1)}, bf16[288,128]{1,0:T(8,128)(2,1)S(1)}, u32[]{:S(2)}, u32[]{:S(2)}) collective-permute-start(bf16[288,128]{1,0:T(8,128)(2,1)S(1)} %get-tuple-element.41), channel_id=1, source_target_pairs={{0,56},{8,0},{16,8},{24,16},{32,24},{40,32},{48,40},{56,48},{1,57}... | collective-permute-start | bytes 221192 | tf_op jit(solution)/shard_map/ppermute | solution.py:528
  21.0 1.3 %collective-permute-start.4 = (bf16[24,512]{1,0:T(8,128)(2,1)S(1)}, bf16[24,512]{1,0:T(8,128)(2,1)S(1)}, u32[]{:S(2)}, u32[]{:S(2)}) collective-permute-start(bf16[24,512]{1,0:T(8,128)(2,1)S(1)} %get-tuple-element.44.a_ref), channel_id=1, source_target_pairs={{0,1},{1,0},{2,3},{3,2},{4,5},{5,4},{6,7},{7,6},{8,9},{9,8},{10,11... | collective-permute-start | bytes 73736 | tf_op jit(solution)/shard_map/ppermute | solution.py:533
  22.3 5.4 %collective-permute-start.7 = (bf16[24,512]{1,0:T(8,128)(2,1)S(1)}, bf16[24,512]{1,0:T(8,128)(2,1)S(1)}, u32[]{:S(2)}, u32[]{:S(2)}) collective-permute-start(bf16[24,512]{1,0:T(8,128)(2,1)S(1)} %shard_map.73.after_ref.a_ref), channel_id=1, source_target_pairs={{0,4},{2,6},{4,0},{6,2},{1,5},{3,7},{5,1},{7,3},{8,12},{10,14},{12... | collective-permute-start | bytes 73736 | tf_op jit(solution)/shard_map/ppermute | solution.py:533
  24.8 5.0 %collective-permute-start.6 = (bf16[24,512]{1,0:T(8,128)(2,1)S(1)}, bf16[24,512]{1,0:T(8,128)(2,1)S(1)}, u32[]{:S(2)}, u32[]{:S(2)}) collective-permute-start(bf16[24,512]{1,0:T(8,128)(2,1)S(1)} %shard_map.73.after_ref.a_ref), channel_id=1, source_target_pairs={{0,6},{2,4},{4,2},{6,0},{1,7},{3,5},{5,3},{7,1},{8,14},{10,12},{12... | collective-permute-start | bytes 73736 | tf_op jit(solution)/shard_map/ppermute | solution.py:533
  25.8 4.0 %collective-permute-start.5 = (bf16[24,512]{1,0:T(8,128)(2,1)S(1)}, bf16[24,512]{1,0:T(8,128)(2,1)S(1)}, u32[]{:S(2)}, u32[]{:S(2)}) collective-permute-start(bf16[24,512]{1,0:T(8,128)(2,1)S(1)} %shard_map.73.after_ref.a_ref), channel_id=1, source_target_pairs={{0,2},{2,0},{4,6},{6,4},{1,3},{3,1},{5,7},{7,5},{8,10},{10,8},{12,... | collective-permute-start | bytes 73736 | tf_op jit(solution)/shard_map/ppermute | solution.py:533
  29.9 5.4 %collective-permute-start.10 = (bf16[24,512]{1,0:T(8,128)(2,1)S(1)}, bf16[24,512]{1,0:T(8,128)(2,1)S(1)}, u32[]{:S(2)}, u32[]{:S(2)}) collective-permute-start(bf16[24,512]{1,0:T(8,128)(2,1)S(1)} %shard_map.76.after_ref.a_ref), channel_id=1, source_target_pairs={{0,32},{16,48},{32,0},{48,16},{1,33},{17,49},{33,1},{49,17},{2,34}... | collective-permute-start | bytes 73736 | tf_op jit(solution)/shard_map/ppermute | solution.py:533
  32.2 5.0 %collective-permute-start.9 = (bf16[24,512]{1,0:T(8,128)(2,1)S(1)}, bf16[24,512]{1,0:T(8,128)(2,1)S(1)}, u32[]{:S(2)}, u32[]{:S(2)}) collective-permute-start(bf16[24,512]{1,0:T(8,128)(2,1)S(1)} %shard_map.76.after_ref.a_ref), channel_id=1, source_target_pairs={{0,48},{16,32},{32,16},{48,0},{1,49},{17,33},{33,17},{49,1},{2,50}... | collective-permute-start | bytes 73736 | tf_op jit(solution)/shard_map/ppermute | solution.py:533
  33.3 3.9 %collective-permute-start.8 = (bf16[24,512]{1,0:T(8,128)(2,1)S(1)}, bf16[24,512]{1,0:T(8,128)(2,1)S(1)}, u32[]{:S(2)}, u32[]{:S(2)}) collective-permute-start(bf16[24,512]{1,0:T(8,128)(2,1)S(1)} %shard_map.76.after_ref.a_ref), channel_id=1, source_target_pairs={{0,16},{16,0},{32,48},{48,32},{1,17},{17,1},{33,49},{49,33},{2,18}... | collective-permute-start | bytes 73736 | tf_op jit(solution)/shard_map/ppermute | solution.py:533
  37.3 5.4 %collective-permute-start.13 = (bf16[24,512]{1,0:T(8,128)(2,1)S(1)}, bf16[24,512]{1,0:T(8,128)(2,1)S(1)}, u32[]{:S(2)}, u32[]{:S(2)}) collective-permute-start(bf16[24,512]{1,0:T(8,128)(2,1)S(1)} %shard_map.78.a_ref), channel_id=1, source_target_pairs={{0,8},{8,0},{1,9},{9,1},{2,10},{10,2},{3,11},{11,3},{4,12},{12,4},... | collective-permute-start | bytes 73736 | tf_op jit(solution)/shard_map/ppermute | solution.py:533
  39.4 5.0 %collective-permute-start.12 = (bf16[24,512]{1,0:T(8,128)(2,1)S(1)}, bf16[24,512]{1,0:T(8,128)(2,1)S(1)}, u32[]{:S(2)}, u32[]{:S(2)}) collective-permute-start(bf16[24,512]{1,0:T(8,128)(2,1)S(1)} %shard_map.78.a_ref), channel_id=1, source_target_pairs={{0,72},{8,64},{64,8},{72,0},{1,73},{9,65},{65,9},{73,1},{2,74},{10... | collective-permute-start | bytes 73736 | tf_op jit(solution)/shard_map/ppermute | solution.py:533
  41.1 3.8 %collective-permute-start.11 = (bf16[24,512]{1,0:T(8,128)(2,1)S(1)}, bf16[24,512]{1,0:T(8,128)(2,1)S(1)}, u32[]{:S(2)}, u32[]{:S(2)}) collective-permute-start(bf16[24,512]{1,0:T(8,128)(2,1)S(1)} %shard_map.78.a_ref), channel_id=1, source_target_pairs={{0,64},{64,0},{1,65},{65,1},{2,66},{66,2},{3,67},{67,3},{4,68},{68... | collective-permute-start | bytes 73736 | tf_op jit(solution)/shard_map/ppermute | solution.py:533

commit v5 on v4

--- a/solution.py
+++ b/solution.py
@@ -17,8 +17,9 @@
 HY = NYT // 2
 DROW = 80
 CROW = 48
-INNER = tuple(range(2, HX - 2))
-OUTER = (0, 1, HX - 2, HX - 1)
+BULK = tuple(range(2, HX - 2))
+INNER = BULK + (1, HX - 2)
+OUTER = (0, HX - 1)
 VMEM_LIMIT = 32 * 1024 * 1024
 FLOPS = 5_000_000_000
 VMEM_SPARE = 55050 * 1024
@@ -195,7 +196,7 @@
     return blocks
 
 
-def store_patch(out, h, at, fine, rims, cell, px, py):
+def cell_patch(h, fine, rims, cell, px, py):
     def layer(which, x, lanes):
         if 0 <= x < NXT:
             return fine[which][x * HY : x * HY + HY, lanes]
@@ -208,8 +209,16 @@
     def touch(kx):
         return layer(2, 2 * cell + px + kx - 1, slice(h * 128, h * 128 + 128))
 
-    for b, block in enumerate(patch_blocks(h, py, tap(0), tap(1), touch, HY)):
-        out[h, at : at + HY, b * 128 : b * 128 + 128] = block
+    return jnp.concatenate(patch_blocks(h, py, tap(0), tap(1), touch, HY), axis=1)
+
+
+def group_patch(h, fine, rims, cells):
+    rows = [cell_patch(h, fine, rims, cell, c // 2, c % 2) for c in range(4) for cell in cells]
+    return jnp.concatenate(rows, axis=0)
+
+
+def store_patch(out, h, at, fine, rims, cell, px, py):
+    out[h, at : at + HY, :] = cell_patch(h, fine, rims, cell, px, py)
 
 
 def coarse_patch(taps, rims, cells):
@@ -227,10 +236,12 @@
     parts = []
     for pre in pres:
         total = jnp.zeros((128, 128), F32)
-        for c in range(4):
-            part = pre[:, c * 128 : c * 128 + 128]
+        for at in range(0, pre.shape[1], 128):
+            part = pre[:, at : at + 128]
             act = jnp.where(part > 0, part, LEAK * part).astype(BF16).astype(F32)
             total = total + act[0:128] + act[128:256]
+        if pre.shape[1] == 256:
+            total = total + pltpu.roll(total, 64, axis=1)
         parts.append(total * 0.125)
     return jnp.concatenate(parts, axis=0)
 
@@ -239,7 +250,7 @@
     part = back[h * 128 : h * 128 + 128]
     both = jnp.concatenate([part, part], axis=0)
     low = LEAK * both
-    return [jnp.where(pre[:, c * 128 : c * 128 + 128] > 0, both, low).astype(BF16) for c in range(4)]
+    return [jnp.where(pre[:, at : at + 128] > 0, both, low).astype(BF16) for at in range(0, pre.shape[1], 128)]
 
 
 def tap_kernel(d_ref, c_ref, ft_ref, fs_ref, vt_ref, ct_ref, dp, ds, cp):
@@ -286,18 +297,19 @@
             at = 96 + half * 16 + x
             set_row(ct, x * HY, slice(half * 128, half * 128 + 128), 0, ls[at : at + 1, :])
             set_row(ct, x * HY + 16, slice(512 + half * 128, 640 + half * 128), 15, hs[at : at + 1, :])
-    back = dot_nt(wb_ref[...], coarse_patch(ct, None, INNER)).astype(BF16).astype(F32) * 0.125
-    for g in range(3):
+    back = dot_nt(wb_ref[...], coarse_patch(ct, None, INNER + INNER[12:])).astype(BF16).astype(F32) * 0.125
+    for g in range(4):
+        cells = INNER[4 * g : 4 * g + 4]
+        size = len(cells) * 128
+        pres = []
         for h in range(2):
-            for c in range(4):
-                for n in range(4):
-                    at = (g * 4 + c) * 128 + n * HY
-                    store_patch(pa, h, at, (ft, fs, vt), None, INNER[4 * g + n], c // 2, c % 2)
-        pres = [dot_nt(w1_ref[h], pa[h, g * 512 : g * 512 + 512, :]) for h in range(2)]
+            patch = group_patch(h, (ft, fs, vt), None, cells)
+            pa[h, g * 512 : g * 512 + size, :] = patch
+            pres.append(dot_nt(w1_ref[h], patch))
         pool_ref[:, g * 128 : g * 128 + 128] = pooled_sum(pres).astype(BF16)
         for h in range(2):
-            for c, part in enumerate(back_through(h, pres[h], back[:, g * 128 : g * 128 + 128])):
-                bpre[h, :, (g * 4 + c) * 128 : (g * 4 + c) * 128 + 128] = part
+            part = jnp.concatenate(back_through(h, pres[h], back[:, g * 128 : g * 128 + 128]), axis=1)
+            bpre[h, :, g * 512 : g * 512 + size] = part
     for h in range(2):
         g1_ref[h] = dot_nn(bpre[h], pa[h])
 
@@ -339,18 +351,18 @@
             acc = [jnp.where(depth2 == d + 1 - kd, part, acc[kd]) for kd in range(3)]
         for kd in range(3):
             a2[(m * 3 + kd) * 16 : (m * 3 + kd) * 16 + 16, :] = acc[kd]
-    a1[240:512, :] = jnp.zeros((272, 128), F32)
+    a1[240:256, :] = jnp.zeros((16, 128), F32)
     a2[432:512, :] = jnp.zeros((80, 256), F32)
     pick2 = (iota((16, 256), 1) // 16 == iota((16, 256), 0)).astype(BF16)
     pick1 = (iota((16, 128), 1) // 16 == iota((16, 128), 0)).astype(BF16)
     two = split_dot(pick2, a2[...])
-    one = split_dot(pick1, a1[...])[0:8]
+    one = jnp.concatenate([split_dot(pick1, a1[...])[0:8], jnp.zeros((8, 256), F32)], axis=1)
     out_ref[...] = jnp.concatenate([two, one], axis=0).astype(BF16)
 
 
 def edge_kernel(
     ft, fs, vt, ct, xlo_ref, xhi_ref, w1_ref, wb_ref, pool_ref, g1_ref,
-    grad_ref, outer_ref, rft, rfs, rvt, dp, ds, cp, corner, swapped, crims, pa, g1, g2, a1, a2,
+    grad_ref, all_ref, rft, rfs, rvt, dp, ds, cp, corner, swapped, crims, pa, g1, g2, a1, a2,
 ):
     for zone, src in enumerate((xlo_ref, xhi_ref)):
         both = dot_nn(jnp.concatenate([src[0:192, :], src[256:288, :]], axis=0), halves_matrix())
@@ -377,17 +389,18 @@
     fine_taps(dp, ds, rft, rfs, rvt, 6)
     coarse_taps(cp, crims, 2)
     cpatch = coarse_patch(ct, crims, OUTER)
-    back = dot_nt(wb_ref[...], cpatch).astype(BF16).astype(F32) * 0.125
+    back = dot_nt(wb_ref[...], jnp.concatenate([cpatch, cpatch], axis=0)).astype(BF16).astype(F32) * 0.125
+    pres = []
     for h in range(2):
-        for c in range(4):
-            for n, cell in enumerate(OUTER):
-                store_patch(pa, h, c * 128 + n * HY, (ft, fs, vt), (rft, rfs, rvt), cell, c // 2, c % 2)
-    pres = [dot_nt(w1_ref[h], pa[h]) for h in range(2)]
+        patch = group_patch(h, (ft, fs, vt), (rft, rfs, rvt), OUTER)
+        pa[h] = patch
+        pres.append(dot_nt(w1_ref[h], patch))
     mean = pooled_sum(pres).astype(BF16)
-    outer_ref[...] = mean
+    last = jnp.where(iota((256, 128), 1) < 64, pool_ref[:, 384:512], mean)
+    pooled = jnp.concatenate([pool_ref[:, 0:384], last], axis=1)
+    all_ref[...] = pooled
     for h in range(2):
         g1[h] = g1_ref[h] + dot_nn(jnp.concatenate(back_through(h, pres[h], back), axis=1), pa[h])
-    pooled = jnp.concatenate([pool_ref[...], mean], axis=1)
     g2[...] = dot_nn(pooled, jnp.concatenate([coarse_patch(ct, None, INNER), cpatch], axis=0))
     extract(g1, g2, grad_ref, a1, a2)
 
@@ -449,17 +462,15 @@
     edge_ref[...] = pooled_sum(pres).T.astype(BF16)
 
 
-def feature_kernel(after_ref, edge_ref, pool_ref, outer_ref, w2_ref, feat_ref, token_ref, pp, pt):
+def feature_kernel(after_ref, edge_ref, pool_ref, w2_ref, feat_ref, token_ref, pp, pt):
     edge = edge_ref[...].astype(F32)
     inner = pool_ref[...].astype(F32).T
-    outer = outer_ref[...].astype(F32).T
     for half in range(2):
         lanes = slice(half * 128, half * 128 + 128)
         pp[half, 8:40, :] = edge[0:32, lanes]
         pp[half, (HX + 1) * CROW + 8 : (HX + 1) * CROW + 40, :] = edge[32:64, lanes]
-        for cells, part in ((INNER, inner), (OUTER, outer)):
-            for n, x in enumerate(cells):
-                pp[half, (x + 1) * CROW + 8 : (x + 1) * CROW + 40, :] = part[n * 32 : n * 32 + 32, lanes]
+        for n, x in enumerate(INNER + OUTER):
+            pp[half, (x + 1) * CROW + 8 : (x + 1) * CROW + 40, :] = inner[n * 32 : n * 32 + 32, lanes]
         pp[half, pl.ds(7, 18, stride=CROW), :] = edge[64:82, lanes]
         pp[half, pl.ds(8 + HY, 18, stride=CROW), :] = edge[96:114, lanes]
     coarse_taps(pp, pt, HX + 2)
@@ -580,20 +591,20 @@
     *taps, pool, g1 = call(
         inner_kernel,
         [VM] * 8,
-        tuple(struct(tap.shape, BF16) for tap in taps) + (struct((256, 384), BF16), struct((2, 256, 768), F32)),
-        (buffer(128, 128), buffer(128, 128), buffer(2, 32, 512), buffer16(2, 1536, 768), buffer16(2, 256, 1536)),
+        tuple(struct(tap.shape, BF16) for tap in taps) + (struct((256, 512), BF16), struct((2, 256, 768), F32)),
+        (buffer(128, 128), buffer(128, 128), buffer(2, 32, 512), buffer16(2, 1792, 768), buffer16(2, 256, 1792)),
         aliases={0: 0, 1: 1, 2: 2, 3: 3},
     )(*taps, lo, hi, w1, wb)
     gradient = struct((24, 512), BF16)
     rim = struct((6 * HY, 512), BF16)
-    grads, outer, *rims = call(
+    grads, pool, *rims = call(
         edge_kernel,
         [VM] * 10,
-        (gradient, struct((256, 128), BF16), rim, rim, struct((6 * HY, 256), BF16)),
+        (gradient, struct((256, 512), BF16), rim, rim, struct((6 * HY, 256), BF16)),
         (
             buffer(6 * DROW, 128), buffer(6 * DROW, 128), buffer(2, 2 * CROW, 128), buffer(64, 128), buffer(2, 32, 128),
-            buffer16(2 * HY, 768), buffer16(2, 512, 768),
-            buffer(2, 256, 768), buffer(256, 2304), buffer(512, 128), buffer(512, 256),
+            buffer16(2 * HY, 768), buffer16(2, 256, 768),
+            buffer(2, 256, 768), buffer(256, 2304), buffer(256, 128), buffer(512, 256),
         ),
     )(*taps, xlo, xhi, w1, wb, pool, g1)
 
@@ -616,10 +627,10 @@
     grads = call(add_four_kernel, [VM] * 4 + [ANY] * 2, gradient)(grads, *others, edge, w2)
     feat, token = call(
         feature_kernel,
-        [ANY] + [VM] * 4,
+        [ANY] + [VM] * 3,
         (struct((HX, HY, 256), BF16), struct((8, 128), F32)),
         (buffer(2, (HX + 2) * CROW, 128), buffer16((HX + 2) * HY, 768)),
-    )(grads, edge, pool, outer, w2)
+    )(grads, edge, pool, w2)
     others = [partner(grads, "x", bits) for bits in (1, 3, 2)]
     grads = call(add_four_kernel, [VM] * 4 + [ANY] * 2, gradient)(grads, *others, token, token)
     near = partner(grads, "rep", 1)

time: 45.9 us -> 45.2 us (0.985)
  Pallas kernels: 15.2 us -> 14.5 us
    pallas_call x2, Pallas kernels: 4.58 us -> 4.07 us  [the longest x1 2.44 us: on_device(): call(edge_kernel, [VM] * 10, (gradient, struct((256, 512), BF16), rim, ri...]
where the time goes in v5:
time: 45.2 us; the launch traced here: 45.1 us
  starting transfers between devices  20.3 us (45%)
  Pallas kernels  14.5 us (32%)
  waiting for transfers between devices  9.53 us (21%)
  between operations  0.79 us (2%)
    ppermute x10, starting transfers between devices, partner(): return lax.ppermute(value, axes, [(i, i ^ bits) for i in range(n)])  11 us
    ppermute x10, waiting for transfers between devices, partner(): return lax.ppermute(value, axes, [(i, i ^ bits) for i in range(n)])  9.52 us
    ppermute x4, starting transfers between devices, shift(): return lax.ppermute(value, axes, [(i, (i + step) % n) for i in range(n)])  9.3 us
    pallas_call x1, Pallas kernels, on_device(): call(inner_kernel, [VM] * 8, tuple((struct(tap.shape, BF16) for tap in ta...  4.28 us
    pallas_call x1, Pallas kernels, on_device(): call(edge_kernel, [VM] * 10, (gradient, struct((256, 512), BF16), rim, ri...  2.44 us
    pallas_call x1, Pallas kernels, on_device(): call(feature_kernel, [ANY] + [VM] * 3, (struct((HX, HY, 256), BF16), stru...  1.62 us
    pallas_call x1, Pallas kernels, on_device(): call(tap_kernel, [VM] * 2, (fine, fine, struct((NXT * HY, 256), BF16), st...  1.37 us
    pallas_call x1, Pallas kernels, on_device(): call(pack_y_kernel, [ANY] * 2, (message, message), (buffer16(2, NXT, 16,...  1.3 us
  transfers between devices with their start and end apart: 14, of which 7 were waited for; matrix products, arithmetic and copies ran while one was open for 0% of the time, Pallas kernels for 22%

profile of v5, /device:TPU:0, one launch (start us, length us, event | category | flops | bytes accessed | tf_op | source)
XLA Modules:
  0.0 45.1 jit_solution(6302646478277179512)
XLA Ops:
  0.7 1.3 %shard_map.68 = (bf16[128,128]{1,0:T(8,128)(2,1)S(1)}, bf16[128,128]{1,0:T(8,128)(2,1)S(1)}) custom-call(bf16[32,64,128]{2,1,0:T(8,128)(2,1)} %bitcast.15, bf16[16,32,256]{2,1,0:T(8,128)(2,1)} %bitcast.18), custom_call_target="tpu_custom_call" | custom-call | flops 5000000000 | bytes 1000000 | tf_op jit(solution)/shard_map/pallas_call | solution.py:557
  2.0 3.6 %collective-permute-start.1 = (bf16[128,128]{1,0:T(8,128)(2,1)S(1)}, bf16[128,128]{1,0:T(8,128)(2,1)S(1)}, u32[]{:S(2)}, u32[]{:S(2)}) collective-permute-start(bf16[128,128]{1,0:T(8,128)(2,1)S(1)} %get-tuple-element.33.down_ref), channel_id=1, source_target_pairs={{0,7},{1,0},{2,1},{3,2},{4,3},{5,4},{6,5},{7,6},{8,15},{9,8},{10,9... | collective-permute-start | bytes 98312 | tf_op jit(solution)/shard_map/ppermute | solution.py:539
  5.6 1.4 %shard_map.67 = (bf16[1024,512]{1,0:T(8,128)(2,1)S(1)}, bf16[1024,512]{1,0:T(8,128)(2,1)S(1)}, bf16[1024,256]{1,0:T(8,128)(2,1)S(1)}, bf16[512,768]{1,0:T(8,128)(2,1)S(1)}) custom-call(bf16[32,64,128]{2,1,0:T(8,128)(2,1)S(1)} %bitcast.16, bf16[16,32,256]{2,1,0:T(8,128)(2,1)S(1)} %bitcast.19), custom_call_target="tpu_custom_call" | custom-call | tf_op jit(solution)/shard_map/pallas_call | solution.py:576
  7.0 0.7 %shard_map.69 = (bf16[2,256,768]{2,1,0:T(8,128)(2,1)S(1)}, bf16[256,2304]{1,0:T(8,128)(2,1)S(1)}) custom-call(bf16[27,4,16]{2,1,0:T(4,128)(2,1)S(1)} %bitcast.23, bf16[27,16,16]{2,1,0:T(8,128)(2,1)S(1)} %bitcast.21), custom_call_target="tpu_custom_call" | custom-call | tf_op jit(solution)/shard_map/pallas_call | solution.py:569
  7.8 3.3 %collective-permute-start.2 = (bf16[288,128]{1,0:T(8,128)(2,1)S(1)}, bf16[288,128]{1,0:T(8,128)(2,1)S(1)}, u32[]{:S(2)}, u32[]{:S(2)}) collective-permute-start(bf16[288,128]{1,0:T(8,128)(2,1)S(1)} %get-tuple-element.40), channel_id=1, source_target_pairs={{0,8},{8,16},{16,24},{24,32},{32,40},{40,48},{48,56},{56,0},{1,9},... | collective-permute-start | bytes 221192 | tf_op jit(solution)/shard_map/ppermute | solution.py:539
  11.1 2.4 %collective-permute-start.3 = (bf16[288,128]{1,0:T(8,128)(2,1)S(1)}, bf16[288,128]{1,0:T(8,128)(2,1)S(1)}, u32[]{:S(2)}, u32[]{:S(2)}) collective-permute-start(bf16[288,128]{1,0:T(8,128)(2,1)S(1)} %get-tuple-element.41), channel_id=1, source_target_pairs={{0,56},{8,0},{16,8},{24,16},{32,24},{40,32},{48,40},{56,48},{1,57}... | collective-permute-start | bytes 221192 | tf_op jit(solution)/shard_map/ppermute | solution.py:539
  13.5 4.3 %shard_map.70 = (bf16[1024,512]{1,0:T(8,128)(2,1)S(1)}, bf16[1024,512]{1,0:T(8,128)(2,1)S(1)}, bf16[1024,256]{1,0:T(8,128)(2,1)S(1)}, bf16[512,768]{1,0:T(8,128)...) custom-call(bf16[1024,512]{1,0:T(8,128)(2,1)S(1)} %get-tuple-element, ...), custom_call_target="tpu_custom_call", output_to_operand_aliasing={{0}: (0, {}), {1}: (1, {}), {2}: (2, {}), {3}: (3, {})} | custom-call | tf_op jit(solution)/shard_map/pallas_call | solution.py:591
  17.8 2.4 %shard_map.72 = (bf16[24,512]{1,0:T(8,128)(2,1)S(1)}, bf16[256,512]{1,0:T(8,128)(2,1)S(1)}, bf16[192,512]{1,0:T(8,128)(2,1)S(1)}, bf16[192,512]{1,0:T(8,128)(2,1)S(1)}, bf16[192,256]{1,0:T(8,128)(2,1)S(1)}) custom-call(bf16[1024,512]{1,0:T(8,128)(2,1)S(1)} %get-tuple-element.36.ft, bf16[1024,512]{1,0:T(8,128)(2,1)S(1)} %get-tuple-element.37.fs, ...), custom_call_target="tpu_custom_call" | custom-call | tf_op jit(solution)/shard_map/pallas_call | solution.py:600
  20.3 1.2 %collective-permute-done.4.b_ref = bf16[24,512]{1,0:T(8,128)(2,1)S(1)} collective-permute-done((bf16[24,512]{1,0:T(8,128)(2,1)S(1)}, bf16[24,512]{1,0:T(8,128)(2,1)S(1)}, u32[]{:S(2)}, u32[]{:S(2)}) %collective-permute-start.4) | collective-permute-done | bytes 24608 | tf_op jit(solution)/shard_map/ppermute | solution.py:544
  21.5 2.6 %collective-permute-start.7 = (bf16[24,512]{1,0:T(8,128)(2,1)S(1)}, bf16[24,512]{1,0:T(8,128)(2,1)S(1)}, u32[]{:S(2)}, u32[]{:S(2)}) collective-permute-start(bf16[24,512]{1,0:T(8,128)(2,1)S(1)} %shard_map.73.after_ref.a_ref), channel_id=1, source_target_pairs={{0,4},{2,6},{4,0},{6,2},{1,5},{3,7},{5,1},{7,3},{8,12},{10,14},{12... | collective-permute-start | bytes 73736 | tf_op jit(solution)/shard_map/ppermute | solution.py:544
  24.1 1.0 %collective-permute-start.6 = (bf16[24,512]{1,0:T(8,128)(2,1)S(1)}, bf16[24,512]{1,0:T(8,128)(2,1)S(1)}, u32[]{:S(2)}, u32[]{:S(2)}) collective-permute-start(bf16[24,512]{1,0:T(8,128)(2,1)S(1)} %shard_map.73.after_ref.a_ref), channel_id=1, source_target_pairs={{0,6},{2,4},{4,2},{6,0},{1,7},{3,5},{5,3},{7,1},{8,14},{10,12},{12... | collective-permute-start | bytes 73736 | tf_op jit(solution)/shard_map/ppermute | solution.py:544
  25.1 0.7 %shard_map.75.also_ref.w2_ref = bf16[256,2304]{1,0:T(8,128)(2,1)S(1)} custom-call(bf16[27,16,16]{2,1,0:T(8,128)(2,1)S(1)} %bitcast.22, bf16[24,512]{1,0:T(8,128)(2,1)S(1)} %shard_map.73.after_ref.a_ref), custom_call_target="tpu_custom_call" | custom-call | tf_op jit(solution)/shard_map/pallas_call | solution.py:612
  25.8 1.1 %shard_map.74.after_ref.edge_ref = bf16[128,256]{1,0:T(8,128)(2,1)S(1)} custom-call(bf16[24,512]{1,0:T(8,128)(2,1)S(1)} %shard_map.73.after_ref.a_ref, bf16[128,128]{1,0:T(8,128)(2,1)S(1)} %get-tuple-element.32.up_ref, bf16[128,128]{1,0:T(8,128)(2,1)S(1)} %get-tuple-element.33.down_ref, bf16[128,128]{1,0:T(8,128)(2,1)S(1)} %collective-permute-done.lo_ref, ...), custom_call_target="tpu_custom_call" | custom-call | tf_op jit(solution)/shard_map/pallas_call | solution.py:618
  26.9 2.2 %collective-permute-done.6.c_ref = bf16[24,512]{1,0:T(8,128)(2,1)S(1)} collective-permute-done((bf16[24,512]{1,0:T(8,128)(2,1)S(1)}, bf16[24,512]{1,0:T(8,128)(2,1)S(1)}, u32[]{:S(2)}, u32[]{:S(2)}) %collective-permute-start.6) | collective-permute-done | bytes 24608 | tf_op jit(solution)/shard_map/ppermute | solution.py:544
  29.2 2.5 %collective-permute-start.10 = (bf16[24,512]{1,0:T(8,128)(2,1)S(1)}, bf16[24,512]{1,0:T(8,128)(2,1)S(1)}, u32[]{:S(2)}, u32[]{:S(2)}) collective-permute-start(bf16[24,512]{1,0:T(8,128)(2,1)S(1)} %shard_map.76.after_ref.a_ref), channel_id=1, source_target_pairs={{0,32},{16,48},{32,0},{48,16},{1,33},{17,49},{33,1},{49,17},{2,34}... | collective-permute-start | bytes 73736 | tf_op jit(solution)/shard_map/ppermute | solution.py:544
  31.7 1.1 %collective-permute-start.9 = (bf16[24,512]{1,0:T(8,128)(2,1)S(1)}, bf16[24,512]{1,0:T(8,128)(2,1)S(1)}, u32[]{:S(2)}, u32[]{:S(2)}) collective-permute-start(bf16[24,512]{1,0:T(8,128)(2,1)S(1)} %shard_map.76.after_ref.a_ref), channel_id=1, source_target_pairs={{0,48},{16,32},{32,16},{48,0},{1,49},{17,33},{33,17},{49,1},{2,50}... | collective-permute-start | bytes 73736 | tf_op jit(solution)/shard_map/ppermute | solution.py:544
  32.8 1.6 %shard_map.77 = (bf16[16,32,256]{2,1,0:T(8,128)(2,1)}, f32[8,128]{1,0:T(8,128)S(1)}) custom-call(bf16[24,512]{1,0:T(8,128)(2,1)S(1)} %shard_map.76.after_ref.a_ref, bf16[128,256]{1,0:T(8,128)(2,1)S(1)} %shard_map.74.after_ref.edge_ref, bf16[256,512]{1,0:T(8,128)(2,1)S(1)} %get-tuple-element.48.pool_ref, bf16[256,2304]{1,0:T(8,128)(2,1)S(1)} %shard_map.75.also_ref.w2_ref), custom_call_target="tpu_custom_call" | custom-call | tf_op jit(solution)/shard_map/pallas_call | solution.py:628
  34.6 2.1 %collective-permute-done.9.c_ref = bf16[24,512]{1,0:T(8,128)(2,1)S(1)} collective-permute-done((bf16[24,512]{1,0:T(8,128)(2,1)S(1)}, bf16[24,512]{1,0:T(8,128)(2,1)S(1)}, u32[]{:S(2)}, u32[]{:S(2)}) %collective-permute-start.9) | collective-permute-done | bytes 24608 | tf_op jit(solution)/shard_map/ppermute | solution.py:544
  36.7 2.2 %collective-permute-start.13 = (bf16[24,512]{1,0:T(8,128)(2,1)S(1)}, bf16[24,512]{1,0:T(8,128)(2,1)S(1)}, u32[]{:S(2)}, u32[]{:S(2)}) collective-permute-start(bf16[24,512]{1,0:T(8,128)(2,1)S(1)} %shard_map.78.a_ref), channel_id=1, source_target_pairs={{0,8},{8,0},{1,9},{9,1},{2,10},{10,2},{3,11},{11,3},{4,12},{12,4},... | collective-permute-start | bytes 73736 | tf_op jit(solution)/shard_map/ppermute | solution.py:544
  38.9 1.5 %collective-permute-start.12 = (bf16[24,512]{1,0:T(8,128)(2,1)S(1)}, bf16[24,512]{1,0:T(8,128)(2,1)S(1)}, u32[]{:S(2)}, u32[]{:S(2)}) collective-permute-start(bf16[24,512]{1,0:T(8,128)(2,1)S(1)} %shard_map.78.a_ref), channel_id=1, source_target_pairs={{0,72},{8,64},{64,8},{72,0},{1,73},{9,65},{65,9},{73,1},{2,74},{10... | collective-permute-start | bytes 73736 | tf_op jit(solution)/shard_map/ppermute | solution.py:544
  40.5 1.7 %collective-permute-done.13.d_ref = bf16[24,512]{1,0:T(8,128)(2,1)S(1)} collective-permute-done((bf16[24,512]{1,0:T(8,128)(2,1)S(1)}, bf16[24,512]{1,0:T(8,128)(2,1)S(1)}, u32[]{:S(2)}, u32[]{:S(2)}) %collective-permute-start.13) | collective-permute-done | bytes 24608 | tf_op jit(solution)/shard_map/ppermute | solution.py:544
  42.1 1.8 %collective-permute-done.12.c_ref = bf16[24,512]{1,0:T(8,128)(2,1)S(1)} collective-permute-done((bf16[24,512]{1,0:T(8,128)(2,1)S(1)}, bf16[24,512]{1,0:T(8,128)(2,1)S(1)}, u32[]{:S(2)}, u32[]{:S(2)}) %collective-permute-start.12) | collective-permute-done | bytes 24608 | tf_op jit(solution)/shard_map/ppermute | solution.py:544
  43.9 0.3 collective-permute-done.11.b_ref
  44.3 0.8 %shard_map.79 = (f32[27,4,16]{2,1,0:T(4,128)}, f32[27,16,16]{2,1,0:T(8,128)}) custom-call(bf16[24,512]{1,0:T(8,128)(2,1)S(1)} %shard_map.78.a_ref, bf16[24,512]{1,0:T(8,128)(2,1)S(1)} %collective-permute-done.11.b_ref, bf16[24,512]{1,0:T(8,128)(2,1)S(1)} %collective-permute-done.12.c_ref, bf16[24,512]{1,0:T(8,128)(2,1)S(1)} %collective-permute-done.13.d_ref), custom_call_target="tpu_custom_call" | custom-call | tf_op jit(solution)/shard_map/pallas_call | solution.py:639
  (25 shorter events, 0.3 us)
Async XLA Ops:
  0.6 4.9 %copy-start = (bf16[1,32,64,128]{3,2,1,0:T(8,128)(2,1)S(1)}, bf16[1,32,64,128]{3,2,1,0:T(8,128)(2,1)}, u32[]{:S(2)}) copy-start(bf16[1,32,64,128]{3,2,1,0:T(8,128)(2,1)} %param.4) | copy-start | bytes 1572868
  0.6 4.9 %copy-start.1 = (bf16[1,16,32,256]{3,2,1,0:T(8,128)(2,1)S(1)}, bf16[1,16,32,256]{3,2,1,0:T(8,128)(2,1)}, u32[]{:S(2)}) copy-start(bf16[1,16,32,256]{3,2,1,0:T(8,128)(2,1)} %param.7) | copy-start | bytes 786436
  0.7 6.3 %copy-start.2 = (bf16[16,16,3,3,3]{1,0,4,3,2:T(8,128)(2,1)S(1)}, bf16[16,16,3,3,3]{1,0,4,3,2:T(8,128)(2,1)}, u32[]{:S(2)}) copy-start(bf16[16,16,3,3,3]{1,0,4,3,2:T(8,128)(2,1)} %param.6) | copy-start | bytes 41476
  0.7 6.3 %copy-start.3 = (bf16[16,4,3,3,3]{0,1,4,3,2:T(4,128)(2,1)S(1)}, bf16[16,4,3,3,3]{0,1,4,3,2:T(4,128)(2,1)}, u32[]{:S(2)}) copy-start(bf16[16,4,3,3,3]{0,1,4,3,2:T(4,128)(2,1)} %param.5) | copy-start | bytes 10372
  2.0 5.8 %collective-permute-start = (bf16[128,128]{1,0:T(8,128)(2,1)S(1)}, bf16[128,128]{1,0:T(8,128)(2,1)S(1)}, u32[]{:S(2)}, u32[]{:S(2)}) collective-permute-start(bf16[128,128]{1,0:T(8,128)(2,1)S(1)} %get-tuple-element.32.up_ref), channel_id=1, source_target_pairs={{0,1},{1,2},{2,3},{3,4},{4,5},{5,6},{6,7},{7,0},{8,9},{9,10},{10,1... | collective-permute-start | bytes 98312 | tf_op jit(solution)/shard_map/ppermute | solution.py:539
  2.0 5.7 %collective-permute-start.1 = (bf16[128,128]{1,0:T(8,128)(2,1)S(1)}, bf16[128,128]{1,0:T(8,128)(2,1)S(1)}, u32[]{:S(2)}, u32[]{:S(2)}) collective-permute-start(bf16[128,128]{1,0:T(8,128)(2,1)S(1)} %get-tuple-element.33.down_ref), channel_id=1, source_target_pairs={{0,7},{1,0},{2,1},{3,2},{4,3},{5,4},{6,5},{7,6},{8,15},{9,8},{10,9... | collective-permute-start | bytes 98312 | tf_op jit(solution)/shard_map/ppermute | solution.py:539
  7.8 10.0 %collective-permute-start.2 = (bf16[288,128]{1,0:T(8,128)(2,1)S(1)}, bf16[288,128]{1,0:T(8,128)(2,1)S(1)}, u32[]{:S(2)}, u32[]{:S(2)}) collective-permute-start(bf16[288,128]{1,0:T(8,128)(2,1)S(1)} %get-tuple-element.40), channel_id=1, source_target_pairs={{0,8},{8,16},{16,24},{24,32},{32,40},{40,48},{48,56},{56,0},{1,9},... | collective-permute-start | bytes 221192 | tf_op jit(solution)/shard_map/ppermute | solution.py:539
  11.1 6.7 %collective-permute-start.3 = (bf16[288,128]{1,0:T(8,128)(2,1)S(1)}, bf16[288,128]{1,0:T(8,128)(2,1)S(1)}, u32[]{:S(2)}, u32[]{:S(2)}) collective-permute-start(bf16[288,128]{1,0:T(8,128)(2,1)S(1)} %get-tuple-element.41), channel_id=1, source_target_pairs={{0,56},{8,0},{16,8},{24,16},{32,24},{40,32},{48,40},{56,48},{1,57}... | collective-permute-start | bytes 221192 | tf_op jit(solution)/shard_map/ppermute | solution.py:539
  20.3 1.2 %collective-permute-start.4 = (bf16[24,512]{1,0:T(8,128)(2,1)S(1)}, bf16[24,512]{1,0:T(8,128)(2,1)S(1)}, u32[]{:S(2)}, u32[]{:S(2)}) collective-permute-start(bf16[24,512]{1,0:T(8,128)(2,1)S(1)} %get-tuple-element.44.a_ref), channel_id=1, source_target_pairs={{0,1},{1,0},{2,3},{3,2},{4,5},{5,4},{6,7},{7,6},{8,9},{9,8},{10,11... | collective-permute-start | bytes 73736 | tf_op jit(solution)/shard_map/ppermute | solution.py:544
  21.5 5.4 %collective-permute-start.7 = (bf16[24,512]{1,0:T(8,128)(2,1)S(1)}, bf16[24,512]{1,0:T(8,128)(2,1)S(1)}, u32[]{:S(2)}, u32[]{:S(2)}) collective-permute-start(bf16[24,512]{1,0:T(8,128)(2,1)S(1)} %shard_map.73.after_ref.a_ref), channel_id=1, source_target_pairs={{0,4},{2,6},{4,0},{6,2},{1,5},{3,7},{5,1},{7,3},{8,12},{10,14},{12... | collective-permute-start | bytes 73736 | tf_op jit(solution)/shard_map/ppermute | solution.py:544
  24.1 5.0 %collective-permute-start.6 = (bf16[24,512]{1,0:T(8,128)(2,1)S(1)}, bf16[24,512]{1,0:T(8,128)(2,1)S(1)}, u32[]{:S(2)}, u32[]{:S(2)}) collective-permute-start(bf16[24,512]{1,0:T(8,128)(2,1)S(1)} %shard_map.73.after_ref.a_ref), channel_id=1, source_target_pairs={{0,6},{2,4},{4,2},{6,0},{1,7},{3,5},{5,3},{7,1},{8,14},{10,12},{12... | collective-permute-start | bytes 73736 | tf_op jit(solution)/shard_map/ppermute | solution.py:544
  25.1 4.1 %collective-permute-start.5 = (bf16[24,512]{1,0:T(8,128)(2,1)S(1)}, bf16[24,512]{1,0:T(8,128)(2,1)S(1)}, u32[]{:S(2)}, u32[]{:S(2)}) collective-permute-start(bf16[24,512]{1,0:T(8,128)(2,1)S(1)} %shard_map.73.after_ref.a_ref), channel_id=1, source_target_pairs={{0,2},{2,0},{4,6},{6,4},{1,3},{3,1},{5,7},{7,5},{8,10},{10,8},{12,... | collective-permute-start | bytes 73736 | tf_op jit(solution)/shard_map/ppermute | solution.py:544
  29.2 5.4 %collective-permute-start.10 = (bf16[24,512]{1,0:T(8,128)(2,1)S(1)}, bf16[24,512]{1,0:T(8,128)(2,1)S(1)}, u32[]{:S(2)}, u32[]{:S(2)}) collective-permute-start(bf16[24,512]{1,0:T(8,128)(2,1)S(1)} %shard_map.76.after_ref.a_ref), channel_id=1, source_target_pairs={{0,32},{16,48},{32,0},{48,16},{1,33},{17,49},{33,1},{49,17},{2,34}... | collective-permute-start | bytes 73736 | tf_op jit(solution)/shard_map/ppermute | solution.py:544
  31.7 5.0 %collective-permute-start.9 = (bf16[24,512]{1,0:T(8,128)(2,1)S(1)}, bf16[24,512]{1,0:T(8,128)(2,1)S(1)}, u32[]{:S(2)}, u32[]{:S(2)}) collective-permute-start(bf16[24,512]{1,0:T(8,128)(2,1)S(1)} %shard_map.76.after_ref.a_ref), channel_id=1, source_target_pairs={{0,48},{16,32},{32,16},{48,0},{1,49},{17,33},{33,17},{49,1},{2,50}... | collective-permute-start | bytes 73736 | tf_op jit(solution)/shard_map/ppermute | solution.py:544
  32.8 3.9 %collective-permute-start.8 = (bf16[24,512]{1,0:T(8,128)(2,1)S(1)}, bf16[24,512]{1,0:T(8,128)(2,1)S(1)}, u32[]{:S(2)}, u32[]{:S(2)}) collective-permute-start(bf16[24,512]{1,0:T(8,128)(2,1)S(1)} %shard_map.76.after_ref.a_ref), channel_id=1, source_target_pairs={{0,16},{16,0},{32,48},{48,32},{1,17},{17,1},{33,49},{49,33},{2,18}... | collective-permute-start | bytes 73736 | tf_op jit(solution)/shard_map/ppermute | solution.py:544
  36.7 5.4 %collective-permute-start.13 = (bf16[24,512]{1,0:T(8,128)(2,1)S(1)}, bf16[24,512]{1,0:T(8,128)(2,1)S(1)}, u32[]{:S(2)}, u32[]{:S(2)}) collective-permute-start(bf16[24,512]{1,0:T(8,128)(2,1)S(1)} %shard_map.78.a_ref), channel_id=1, source_target_pairs={{0,8},{8,0},{1,9},{9,1},{2,10},{10,2},{3,11},{11,3},{4,12},{12,4},... | collective-permute-start | bytes 73736 | tf_op jit(solution)/shard_map/ppermute | solution.py:544
  38.9 5.0 %collective-permute-start.12 = (bf16[24,512]{1,0:T(8,128)(2,1)S(1)}, bf16[24,512]{1,0:T(8,128)(2,1)S(1)}, u32[]{:S(2)}, u32[]{:S(2)}) collective-permute-start(bf16[24,512]{1,0:T(8,128)(2,1)S(1)} %shard_map.78.a_ref), channel_id=1, source_target_pairs={{0,72},{8,64},{64,8},{72,0},{1,73},{9,65},{65,9},{73,1},{2,74},{10... | collective-permute-start | bytes 73736 | tf_op jit(solution)/shard_map/ppermute | solution.py:544
  40.4 3.8 %collective-permute-start.11 = (bf16[24,512]{1,0:T(8,128)(2,1)S(1)}, bf16[24,512]{1,0:T(8,128)(2,1)S(1)}, u32[]{:S(2)}, u32[]{:S(2)}) collective-permute-start(bf16[24,512]{1,0:T(8,128)(2,1)S(1)} %shard_map.78.a_ref), channel_id=1, source_target_pairs={{0,64},{64,0},{1,65},{65,1},{2,66},{66,2},{3,67},{67,3},{4,68},{68... | collective-permute-start | bytes 73736 | tf_op jit(solution)/shard_map/ppermute | solution.py:544

commit v6 on v5

--- a/solution.py
+++ b/solution.py
@@ -162,13 +162,14 @@
     return ((row // 128 == u % 16 // 4) & (row % 128 == lane) & (u >= 0)).astype(BF16)
 
 
-def fine_taps(dp, ds, ft, fs, vt, layers):
-    for n in range(layers):
+def fine_taps(dp, ds, ft, fs, vt, layers, first=0):
+    for n in range(first, layers):
         for t in range(4):
             for src, out in ((dp, ft), (ds, fs)):
                 rows = src[pl.ds(n * DROW + 7 + t, HY, stride=2), :]
                 out[n * HY : n * HY + HY, t * 128 : t * 128 + 128] = rows.astype(BF16)
-    vt[...] = dot_nn(ft[...], touch_matrix()).astype(BF16)
+    rows = slice(first * HY, layers * HY)
+    vt[rows, :] = dot_nn(ft[rows, :], touch_matrix()).astype(BF16)
 
 
 def coarse_taps(padded, taps, layers):
@@ -360,33 +361,35 @@
     out_ref[...] = jnp.concatenate([two, one], axis=0).astype(BF16)
 
 
+def fill_rim(zone, src, layers, dp, ds, swapped):
+    both = dot_nn(jnp.concatenate([src[k * 64 : k * 64 + 64, :] for k in layers] + [src[256:288, :]], axis=0), halves_matrix())
+    end = len(layers) * 64
+    swapped[0] = both[end : end + 32, 0:128]
+    swapped[1] = both[end : end + 32, 128:256]
+    for n, k in enumerate(layers):
+        top = (zone * 3 + k) * DROW
+        for which, out in enumerate((dp, ds)):
+            out[top + 8 : top + 8 + NYT, :] = both[n * 64 : n * 64 + 64, which * 128 : which * 128 + 128]
+            for side, y in ((0, 5), (1, 8 + NYT)):
+                for ky in range(3):
+                    at = side * 9 + 3 * ky + k
+                    out[top + y + ky : top + y + ky + 1, :] = swapped[which, at : at + 1, :]
+
+
 def edge_kernel(
     ft, fs, vt, ct, xlo_ref, xhi_ref, w1_ref, wb_ref, pool_ref, g1_ref,
     grad_ref, all_ref, rft, rfs, rvt, dp, ds, cp, corner, swapped, crims, pa, g1, g2, a1, a2,
 ):
     for zone, src in enumerate((xlo_ref, xhi_ref)):
-        both = dot_nn(jnp.concatenate([src[0:192, :], src[256:288, :]], axis=0), halves_matrix())
-        for k in range(3):
-            at = (zone * 3 + k) * DROW + 8
-            dp[at : at + NYT, :] = both[k * 64 : k * 64 + 64, 0:128]
-            ds[at : at + NYT, :] = both[k * 64 : k * 64 + 64, 128:256]
-        swapped[0] = both[192:224, 0:128]
-        swapped[1] = both[192:224, 128:256]
         corner[zone * 32 : zone * 32 + 32, :] = src[256:288, :].astype(F32)
-        for side, y in ((0, 5), (1, 8 + NYT)):
-            for ky in range(3):
-                for kx in range(3):
-                    row = (zone * 3 + kx) * DROW + y + ky
-                    at = side * 9 + 3 * ky + kx
-                    dp[row : row + 1, :] = swapped[0, at : at + 1, :]
-                    ds[row : row + 1, :] = swapped[1, at : at + 1, :]
+        fill_rim(zone, src, (2 - 2 * zone,), dp, ds, swapped)
         for half in range(2):
             at = zone * CROW + 8
             cp[half, at : at + HY, :] = src[192 + half * 32 : 224 + half * 32, :].astype(F32)
             for side, y in ((0, 7), (1, 8 + HY)):
                 at = zone * 32 + 18 + side * 2 + half
                 cp[half, zone * CROW + y : zone * CROW + y + 1, :] = corner[at : at + 1, :]
-    fine_taps(dp, ds, rft, rfs, rvt, 6)
+    fine_taps(dp, ds, rft, rfs, rvt, 4, 2)
     coarse_taps(cp, crims, 2)
     cpatch = coarse_patch(ct, crims, OUTER)
     back = dot_nt(wb_ref[...], jnp.concatenate([cpatch, cpatch], axis=0)).astype(BF16).astype(F32) * 0.125
@@ -406,9 +409,12 @@
 
 
 def rim_kernel(
-    after_ref, up_ref, down_ref, lo_ref, hi_ref, xlo_ref, xhi_ref, ft, fs, vt, rft, rfs, rvt, w1_ref,
-    edge_ref, col, raw, corner, tv, rim,
+    after_ref, up_ref, down_ref, lo_ref, hi_ref, xlo_ref, xhi_ref, ft, fs, vt, w1_ref,
+    edge_ref, col, raw, corner, tv, rim, rft, rfs, rvt, dp, ds, swapped,
 ):
+    for zone, src in enumerate((xlo_ref, xhi_ref)):
+        fill_rim(zone, src, (0, 1, 2), dp, ds, swapped)
+    fine_taps(dp, ds, rft, rfs, rvt, 6)
     raw[...] = jnp.zeros(raw.shape, F32)
     for k in range(3):
         raw[k, 8:40, :] = lo_ref[k * 32 : k * 32 + 32, :].astype(F32)
@@ -493,7 +499,7 @@
     out_ref[...] = add_four((a_ref, b_ref, c_ref, d_ref)).astype(BF16)
 
 
-def final_kernel(a_ref, b_ref, c_ref, d_ref, g1_ref, g2_ref):
+def final_kernel(a_ref, b_ref, c_ref, d_ref, after_ref, g1_ref, g2_ref):
     total = add_four((a_ref, b_ref, c_ref, d_ref)) * 0.5
     for kd in range(3):
         for kx in range(3):
@@ -596,48 +602,50 @@
         aliases={0: 0, 1: 1, 2: 2, 3: 3},
     )(*taps, lo, hi, w1, wb)
     gradient = struct((24, 512), BF16)
-    rim = struct((6 * HY, 512), BF16)
-    grads, pool, *rims = call(
+    rims = (buffer16(6 * HY, 512), buffer16(6 * HY, 512), buffer16(6 * HY, 256))
+    padded = (buffer(6 * DROW, 128), buffer(6 * DROW, 128))
+    grads, pool = call(
         edge_kernel,
         [VM] * 10,
-        (gradient, struct((256, 512), BF16), rim, rim, struct((6 * HY, 256), BF16)),
+        (gradient, struct((256, 512), BF16)),
         (
-            buffer(6 * DROW, 128), buffer(6 * DROW, 128), buffer(2, 2 * CROW, 128), buffer(64, 128), buffer(2, 32, 128),
+            *rims, *padded, buffer(2, 2 * CROW, 128), buffer(64, 128), buffer(2, 32, 128),
             buffer16(2 * HY, 768), buffer16(2, 256, 768),
             buffer(2, 256, 768), buffer(256, 2304), buffer(256, 128), buffer(512, 256),
         ),
     )(*taps, xlo, xhi, w1, wb, pool, g1)
 
     grads = call(add_two_kernel, [VM] * 2, gradient)(grads, partner(grads, "core", 1))
+    edge = call(
+        rim_kernel,
+        [ANY] + [VM] * 10,
+        struct((128, 256), BF16),
+        (
+            buffer(2, 8, 48, 128), buffer(8, 48, 128), buffer(288, 128), buffer(2, 2, 48, 128), buffer16(2, 512, 768),
+            *rims, *padded, buffer(2, 32, 128),
+        ),
+    )(grads, yup, ydown, lo, hi, xlo, xhi, *taps[:3], w1)
+    others = [partner(grads, "z", bits) for bits in (1, 3, 2)]
+    grads = call(add_four_kernel, [VM] * 4 + [ANY] * 2, gradient)(grads, *others, edge, edge)
     w2 = call(
         feature_weights_kernel,
         [VM, ANY],
         struct((256, 2304), BF16),
         (buffer(64, 128), buffer(64, 2048)),
     )(k2, grads)
-    edge = call(
-        rim_kernel,
-        [ANY] + [VM] * 13,
-        struct((128, 256), BF16),
-        (
-            buffer(2, 8, 48, 128), buffer(8, 48, 128), buffer(288, 128), buffer(2, 2, 48, 128), buffer16(2, 512, 768),
-        ),
-    )(grads, yup, ydown, lo, hi, xlo, xhi, *taps[:3], *rims, w1)
-    others = [partner(grads, "z", bits) for bits in (1, 3, 2)]
-    grads = call(add_four_kernel, [VM] * 4 + [ANY] * 2, gradient)(grads, *others, edge, w2)
+    others = [partner(grads, "x", bits) for bits in (1, 3, 2)]
+    grads = call(add_four_kernel, [VM] * 4 + [ANY] * 2, gradient)(grads, *others, w2, w2)
     feat, token = call(
         feature_kernel,
         [ANY] + [VM] * 3,
         (struct((HX, HY, 256), BF16), struct((8, 128), F32)),
         (buffer(2, (HX + 2) * CROW, 128), buffer16((HX + 2) * HY, 768)),
     )(grads, edge, pool, w2)
-    others = [partner(grads, "x", bits) for bits in (1, 3, 2)]
-    grads = call(add_four_kernel, [VM] * 4 + [ANY] * 2, gradient)(grads, *others, token, token)
     near = partner(grads, "rep", 1)
     across = partner(grads, ("rep", "yh"), 3)
     far = partner(grads, "yh", 1)
-    g1, g2 = call(final_kernel, [VM] * 4, (struct((27, CIN, CH), F32), struct((27, CH, CH), F32)))(
-        grads, near, across, far
+    g1, g2 = call(final_kernel, [VM] * 4 + [ANY], (struct((27, CIN, CH), F32), struct((27, CH, CH), F32)))(
+        grads, near, across, far, token
     )
     g1 = jnp.transpose(g1.reshape(3, 3, 3, CIN, CH), (4, 3, 0, 1, 2))
     g2 = jnp.transpose(g2.reshape(3, 3, 3, CH, CH), (3, 4, 0, 1, 2))

time: 45.2 us -> 45.2 us (level)
  no operation moved by 1% of the time
where the time goes in v6:
time: 45.2 us; the launch traced here: 45.1 us
  starting transfers between devices  20.3 us (45%)
  Pallas kernels  14.7 us (33%)
  waiting for transfers between devices  9.34 us (21%)
  between operations  0.79 us (2%)
    ppermute x10, starting transfers between devices, partner(): return lax.ppermute(value, axes, [(i, i ^ bits) for i in range(n)])  11 us
    ppermute x10, waiting for transfers between devices, partner(): return lax.ppermute(value, axes, [(i, i ^ bits) for i in range(n)])  9.33 us
    ppermute x4, starting transfers between devices, shift(): return lax.ppermute(value, axes, [(i, (i + step) % n) for i in range(n)])  9.3 us
    pallas_call x1, Pallas kernels, on_device(): call(inner_kernel, [VM] * 8, tuple((struct(tap.shape, BF16) for tap in ta...  4.28 us
    pallas_call x1, Pallas kernels, on_device(): call(edge_kernel, [VM] * 10, (gradient, struct((256, 512), BF16)), (*rims...  2.42 us
    pallas_call x1, Pallas kernels, on_device(): call(feature_kernel, [ANY] + [VM] * 3, (struct((HX, HY, 256), BF16), stru...  1.62 us
    pallas_call x1, Pallas kernels, on_device(): call(tap_kernel, [VM] * 2, (fine, fine, struct((NXT * HY, 256), BF16), st...  1.37 us
    pallas_call x1, Pallas kernels, on_device(): call(pack_y_kernel, [ANY] * 2, (message, message), (buffer16(2, NXT, 16,...  1.3 us
  transfers between devices with their start and end apart: 14, of which 7 were waited for; matrix products, arithmetic and copies ran while one was open for 0% of the time, Pallas kernels for 22%

profile of v6, /device:TPU:0, one launch (start us, length us, event | category | flops | bytes accessed | tf_op | source)
XLA Modules:
  0.0 45.1 jit_solution(11926984702664712406)
XLA Ops:
  0.7 1.3 %shard_map.68 = (bf16[128,128]{1,0:T(8,128)(2,1)S(1)}, bf16[128,128]{1,0:T(8,128)(2,1)S(1)}) custom-call(bf16[32,64,128]{2,1,0:T(8,128)(2,1)} %bitcast.15, bf16[16,32,256]{2,1,0:T(8,128)(2,1)} %bitcast.18), custom_call_target="tpu_custom_call" | custom-call | flops 5000000000 | bytes 1000000 | tf_op jit(solution)/shard_map/pallas_call | solution.py:563
  2.0 3.6 %collective-permute-start.1 = (bf16[128,128]{1,0:T(8,128)(2,1)S(1)}, bf16[128,128]{1,0:T(8,128)(2,1)S(1)}, u32[]{:S(2)}, u32[]{:S(2)}) collective-permute-start(bf16[128,128]{1,0:T(8,128)(2,1)S(1)} %get-tuple-element.30.down_ref), channel_id=1, source_target_pairs={{0,7},{1,0},{2,1},{3,2},{4,3},{5,4},{6,5},{7,6},{8,15},{9,8},{10,9... | collective-permute-start | bytes 98312 | tf_op jit(solution)/shard_map/ppermute | solution.py:545
  5.6 1.4 %shard_map.67 = (bf16[1024,512]{1,0:T(8,128)(2,1)S(1)}, bf16[1024,512]{1,0:T(8,128)(2,1)S(1)}, bf16[1024,256]{1,0:T(8,128)(2,1)S(1)}, bf16[512,768]{1,0:T(8,128)(2,1)S(1)}) custom-call(bf16[32,64,128]{2,1,0:T(8,128)(2,1)S(1)} %bitcast.16, bf16[16,32,256]{2,1,0:T(8,128)(2,1)S(1)} %bitcast.19), custom_call_target="tpu_custom_call" | custom-call | tf_op jit(solution)/shard_map/pallas_call | solution.py:582
  7.0 0.7 %shard_map.69 = (bf16[2,256,768]{2,1,0:T(8,128)(2,1)S(1)}, bf16[256,2304]{1,0:T(8,128)(2,1)S(1)}) custom-call(bf16[27,4,16]{2,1,0:T(4,128)(2,1)S(1)} %bitcast.23, bf16[27,16,16]{2,1,0:T(8,128)(2,1)S(1)} %bitcast.21), custom_call_target="tpu_custom_call" | custom-call | tf_op jit(solution)/shard_map/pallas_call | solution.py:575
  7.8 3.3 %collective-permute-start.2 = (bf16[288,128]{1,0:T(8,128)(2,1)S(1)}, bf16[288,128]{1,0:T(8,128)(2,1)S(1)}, u32[]{:S(2)}, u32[]{:S(2)}) collective-permute-start(bf16[288,128]{1,0:T(8,128)(2,1)S(1)} %get-tuple-element.37), channel_id=1, source_target_pairs={{0,8},{8,16},{16,24},{24,32},{32,40},{40,48},{48,56},{56,0},{1,9},... | collective-permute-start | bytes 221192 | tf_op jit(solution)/shard_map/ppermute | solution.py:545
  11.1 2.4 %collective-permute-start.3 = (bf16[288,128]{1,0:T(8,128)(2,1)S(1)}, bf16[288,128]{1,0:T(8,128)(2,1)S(1)}, u32[]{:S(2)}, u32[]{:S(2)}) collective-permute-start(bf16[288,128]{1,0:T(8,128)(2,1)S(1)} %get-tuple-element.38), channel_id=1, source_target_pairs={{0,56},{8,0},{16,8},{24,16},{32,24},{40,32},{48,40},{56,48},{1,57}... | collective-permute-start | bytes 221192 | tf_op jit(solution)/shard_map/ppermute | solution.py:545
  13.5 4.3 %shard_map.70 = (bf16[1024,512]{1,0:T(8,128)(2,1)S(1)}, bf16[1024,512]{1,0:T(8,128)(2,1)S(1)}, bf16[1024,256]{1,0:T(8,128)(2,1)S(1)}, bf16[512,768]{1,0:T(8,128)...) custom-call(bf16[1024,512]{1,0:T(8,128)(2,1)S(1)} %get-tuple-element, ...), custom_call_target="tpu_custom_call", output_to_operand_aliasing={{0}: (0, {}), {1}: (1, {}), {2}: (2, {}), {3}: (3, {})} | custom-call | tf_op jit(solution)/shard_map/pallas_call | solution.py:597
  17.8 2.4 %shard_map.72 = (bf16[24,512]{1,0:T(8,128)(2,1)S(1)}, bf16[256,512]{1,0:T(8,128)(2,1)S(1)}) custom-call(bf16[1024,512]{1,0:T(8,128)(2,1)S(1)} %get-tuple-element.33.ft, bf16[1024,512]{1,0:T(8,128)(2,1)S(1)} %get-tuple-element.34.fs, bf16[1024,256]{1,0:T(8,128)(2,1)S(1)} %get-tuple-element.35.vt, bf16[512,768]{1,0:T(8,128)(2,1)S(1)} %get-tuple-element.36.ct, ...), custom_call_target="tpu_custom_call" | custom-call | tf_op jit(solution)/shard_map/pallas_call | solution.py:607
  20.2 1.2 %collective-permute-done.4.b_ref = bf16[24,512]{1,0:T(8,128)(2,1)S(1)} collective-permute-done((bf16[24,512]{1,0:T(8,128)(2,1)S(1)}, bf16[24,512]{1,0:T(8,128)(2,1)S(1)}, u32[]{:S(2)}, u32[]{:S(2)}) %collective-permute-start.4) | collective-permute-done | bytes 24608 | tf_op jit(solution)/shard_map/ppermute | solution.py:550
  21.5 2.6 %collective-permute-start.7 = (bf16[24,512]{1,0:T(8,128)(2,1)S(1)}, bf16[24,512]{1,0:T(8,128)(2,1)S(1)}, u32[]{:S(2)}, u32[]{:S(2)}) collective-permute-start(bf16[24,512]{1,0:T(8,128)(2,1)S(1)} %shard_map.73.after_ref.a_ref), channel_id=1, source_target_pairs={{0,4},{2,6},{4,0},{6,2},{1,5},{3,7},{5,1},{7,3},{8,12},{10,14},{12... | collective-permute-start | bytes 73736 | tf_op jit(solution)/shard_map/ppermute | solution.py:550
  24.1 1.0 %collective-permute-start.6 = (bf16[24,512]{1,0:T(8,128)(2,1)S(1)}, bf16[24,512]{1,0:T(8,128)(2,1)S(1)}, u32[]{:S(2)}, u32[]{:S(2)}) collective-permute-start(bf16[24,512]{1,0:T(8,128)(2,1)S(1)} %shard_map.73.after_ref.a_ref), channel_id=1, source_target_pairs={{0,6},{2,4},{4,2},{6,0},{1,7},{3,5},{5,3},{7,1},{8,14},{10,12},{12... | collective-permute-start | bytes 73736 | tf_op jit(solution)/shard_map/ppermute | solution.py:550
  25.1 1.3 %shard_map.74.after_ref.also_ref.edge_ref = bf16[128,256]{1,0:T(8,128)(2,1)S(1)} custom-call(bf16[24,512]{1,0:T(8,128)(2,1)S(1)} %shard_map.73.after_ref.a_ref, bf16[128,128]{1,0:T(8,128)(2,1)S(1)} %get-tuple-element.29.up_ref, bf16[128,128]{1,0:T(8,128)(2,1)S(1)} %get-tuple-element.30.down_ref, bf16[128,128]{1,0:T(8,128)(2,1)S(1)} %collective-permute-done.lo_ref, ...), custom_call_target="tpu_custom_call" | custom-call | tf_op jit(solution)/shard_map/pallas_call | solution.py:619
  26.3 0.5 %collective-permute-done.7.d_ref = bf16[24,512]{1,0:T(8,128)(2,1)S(1)} collective-permute-done((bf16[24,512]{1,0:T(8,128)(2,1)S(1)}, bf16[24,512]{1,0:T(8,128)(2,1)S(1)}, u32[]{:S(2)}, u32[]{:S(2)}) %collective-permute-start.7) | collective-permute-done | bytes 24608 | tf_op jit(solution)/shard_map/ppermute | solution.py:550
  26.9 2.2 %collective-permute-done.6.c_ref = bf16[24,512]{1,0:T(8,128)(2,1)S(1)} collective-permute-done((bf16[24,512]{1,0:T(8,128)(2,1)S(1)}, bf16[24,512]{1,0:T(8,128)(2,1)S(1)}, u32[]{:S(2)}, u32[]{:S(2)}) %collective-permute-start.6) | collective-permute-done | bytes 24608 | tf_op jit(solution)/shard_map/ppermute | solution.py:550
  29.1 2.5 %collective-permute-start.10 = (bf16[24,512]{1,0:T(8,128)(2,1)S(1)}, bf16[24,512]{1,0:T(8,128)(2,1)S(1)}, u32[]{:S(2)}, u32[]{:S(2)}) collective-permute-start(bf16[24,512]{1,0:T(8,128)(2,1)S(1)} %shard_map.75.after_ref.a_ref), channel_id=1, source_target_pairs={{0,32},{16,48},{32,0},{48,16},{1,33},{17,49},{33,1},{49,17},{2,34}... | collective-permute-start | bytes 73736 | tf_op jit(solution)/shard_map/ppermute | solution.py:550
  31.6 1.1 %collective-permute-start.9 = (bf16[24,512]{1,0:T(8,128)(2,1)S(1)}, bf16[24,512]{1,0:T(8,128)(2,1)S(1)}, u32[]{:S(2)}, u32[]{:S(2)}) collective-permute-start(bf16[24,512]{1,0:T(8,128)(2,1)S(1)} %shard_map.75.after_ref.a_ref), channel_id=1, source_target_pairs={{0,48},{16,32},{32,16},{48,0},{1,49},{17,33},{33,17},{49,1},{2,50}... | collective-permute-start | bytes 73736 | tf_op jit(solution)/shard_map/ppermute | solution.py:550
  32.8 0.7 %shard_map.76.after_ref.also_ref.w2_ref = bf16[256,2304]{1,0:T(8,128)(2,1)S(1)} custom-call(bf16[27,16,16]{2,1,0:T(8,128)(2,1)S(1)} %bitcast.22, bf16[24,512]{1,0:T(8,128)(2,1)S(1)} %shard_map.75.after_ref.a_ref), custom_call_target="tpu_custom_call" | custom-call | tf_op jit(solution)/shard_map/pallas_call | solution.py:630
  33.5 1.0 %collective-permute-done.10.d_ref = bf16[24,512]{1,0:T(8,128)(2,1)S(1)} collective-permute-done((bf16[24,512]{1,0:T(8,128)(2,1)S(1)}, bf16[24,512]{1,0:T(8,128)(2,1)S(1)}, u32[]{:S(2)}, u32[]{:S(2)}) %collective-permute-start.10) | collective-permute-done | bytes 24608 | tf_op jit(solution)/shard_map/ppermute | solution.py:550
  34.5 2.1 %collective-permute-done.9.c_ref = bf16[24,512]{1,0:T(8,128)(2,1)S(1)} collective-permute-done((bf16[24,512]{1,0:T(8,128)(2,1)S(1)}, bf16[24,512]{1,0:T(8,128)(2,1)S(1)}, u32[]{:S(2)}, u32[]{:S(2)}) %collective-permute-start.9) | collective-permute-done | bytes 24608 | tf_op jit(solution)/shard_map/ppermute | solution.py:550
  36.7 2.2 %collective-permute-start.13 = (bf16[24,512]{1,0:T(8,128)(2,1)S(1)}, bf16[24,512]{1,0:T(8,128)(2,1)S(1)}, u32[]{:S(2)}, u32[]{:S(2)}) collective-permute-start(bf16[24,512]{1,0:T(8,128)(2,1)S(1)} %shard_map.77.after_ref.a_ref), channel_id=1, source_target_pairs={{0,8},{8,0},{1,9},{9,1},{2,10},{10,2},{3,11},{11,3},{4,12},{12,4},... | collective-permute-start | bytes 73736 | tf_op jit(solution)/shard_map/ppermute | solution.py:550
  38.9 1.5 %collective-permute-start.12 = (bf16[24,512]{1,0:T(8,128)(2,1)S(1)}, bf16[24,512]{1,0:T(8,128)(2,1)S(1)}, u32[]{:S(2)}, u32[]{:S(2)}) collective-permute-start(bf16[24,512]{1,0:T(8,128)(2,1)S(1)} %shard_map.77.after_ref.a_ref), channel_id=1, source_target_pairs={{0,72},{8,64},{64,8},{72,0},{1,73},{9,65},{65,9},{73,1},{2,74},{10... | collective-permute-start | bytes 73736 | tf_op jit(solution)/shard_map/ppermute | solution.py:550
  40.4 1.6 %shard_map.78 = (bf16[16,32,256]{2,1,0:T(8,128)(2,1)}, f32[8,128]{1,0:T(8,128)S(1)}) custom-call(bf16[24,512]{1,0:T(8,128)(2,1)S(1)} %shard_map.77.after_ref.a_ref, bf16[128,256]{1,0:T(8,128)(2,1)S(1)} %shard_map.74.after_ref.also_ref.edge_ref, bf16[256,512]{1,0:T(8,128)(2,1)S(1)} %get-tuple-element.42.pool_ref, ...), custom_call_target="tpu_custom_call" | custom-call | tf_op jit(solution)/shard_map/pallas_call | solution.py:638
  42.1 1.8 %collective-permute-done.12.c_ref = bf16[24,512]{1,0:T(8,128)(2,1)S(1)} collective-permute-done((bf16[24,512]{1,0:T(8,128)(2,1)S(1)}, bf16[24,512]{1,0:T(8,128)(2,1)S(1)}, u32[]{:S(2)}, u32[]{:S(2)}) %collective-permute-start.12) | collective-permute-done | bytes 24608 | tf_op jit(solution)/shard_map/ppermute | solution.py:550
  44.2 0.8 %shard_map.79 = (f32[27,4,16]{2,1,0:T(4,128)}, f32[27,16,16]{2,1,0:T(8,128)}) custom-call(bf16[24,512]{1,0:T(8,128)(2,1)S(1)} %shard_map.77.after_ref.a_ref, bf16[24,512]{1,0:T(8,128)(2,1)S(1)} %collective-permute-done.11.b_ref, bf16[24,512]{1,0:T(8,128)(2,1)S(1)} %collective-permute-done.12.c_ref, bf16[24,512]{1,0:T(8,128)(2,1)S(1)} %collective-permute-done.13.d_ref, ...), custom_call_target="tpu_custom_call" | custom-call | tf_op jit(solution)/shard_map/pallas_call | solution.py:647
  (25 shorter events, 0.6 us)
Async XLA Ops:
  0.6 4.9 %copy-start = (bf16[1,32,64,128]{3,2,1,0:T(8,128)(2,1)S(1)}, bf16[1,32,64,128]{3,2,1,0:T(8,128)(2,1)}, u32[]{:S(2)}) copy-start(bf16[1,32,64,128]{3,2,1,0:T(8,128)(2,1)} %param.4) | copy-start | bytes 1572868
  0.6 4.9 %copy-start.1 = (bf16[1,16,32,256]{3,2,1,0:T(8,128)(2,1)S(1)}, bf16[1,16,32,256]{3,2,1,0:T(8,128)(2,1)}, u32[]{:S(2)}) copy-start(bf16[1,16,32,256]{3,2,1,0:T(8,128)(2,1)} %param.7) | copy-start | bytes 786436
  0.7 6.3 %copy-start.2 = (bf16[16,16,3,3,3]{1,0,4,3,2:T(8,128)(2,1)S(1)}, bf16[16,16,3,3,3]{1,0,4,3,2:T(8,128)(2,1)}, u32[]{:S(2)}) copy-start(bf16[16,16,3,3,3]{1,0,4,3,2:T(8,128)(2,1)} %param.6) | copy-start | bytes 41476
  0.7 6.3 %copy-start.3 = (bf16[16,4,3,3,3]{0,1,4,3,2:T(4,128)(2,1)S(1)}, bf16[16,4,3,3,3]{0,1,4,3,2:T(4,128)(2,1)}, u32[]{:S(2)}) copy-start(bf16[16,4,3,3,3]{0,1,4,3,2:T(4,128)(2,1)} %param.5) | copy-start | bytes 10372
  2.0 5.8 %collective-permute-start = (bf16[128,128]{1,0:T(8,128)(2,1)S(1)}, bf16[128,128]{1,0:T(8,128)(2,1)S(1)}, u32[]{:S(2)}, u32[]{:S(2)}) collective-permute-start(bf16[128,128]{1,0:T(8,128)(2,1)S(1)} %get-tuple-element.29.up_ref), channel_id=1, source_target_pairs={{0,1},{1,2},{2,3},{3,4},{4,5},{5,6},{6,7},{7,0},{8,9},{9,10},{10,1... | collective-permute-start | bytes 98312 | tf_op jit(solution)/shard_map/ppermute | solution.py:545
  2.0 5.7 %collective-permute-start.1 = (bf16[128,128]{1,0:T(8,128)(2,1)S(1)}, bf16[128,128]{1,0:T(8,128)(2,1)S(1)}, u32[]{:S(2)}, u32[]{:S(2)}) collective-permute-start(bf16[128,128]{1,0:T(8,128)(2,1)S(1)} %get-tuple-element.30.down_ref), channel_id=1, source_target_pairs={{0,7},{1,0},{2,1},{3,2},{4,3},{5,4},{6,5},{7,6},{8,15},{9,8},{10,9... | collective-permute-start | bytes 98312 | tf_op jit(solution)/shard_map/ppermute | solution.py:545
  7.8 10.0 %collective-permute-start.2 = (bf16[288,128]{1,0:T(8,128)(2,1)S(1)}, bf16[288,128]{1,0:T(8,128)(2,1)S(1)}, u32[]{:S(2)}, u32[]{:S(2)}) collective-permute-start(bf16[288,128]{1,0:T(8,128)(2,1)S(1)} %get-tuple-element.37), channel_id=1, source_target_pairs={{0,8},{8,16},{16,24},{24,32},{32,40},{40,48},{48,56},{56,0},{1,9},... | collective-permute-start | bytes 221192 | tf_op jit(solution)/shard_map/ppermute | solution.py:545
  11.1 6.7 %collective-permute-start.3 = (bf16[288,128]{1,0:T(8,128)(2,1)S(1)}, bf16[288,128]{1,0:T(8,128)(2,1)S(1)}, u32[]{:S(2)}, u32[]{:S(2)}) collective-permute-start(bf16[288,128]{1,0:T(8,128)(2,1)S(1)} %get-tuple-element.38), channel_id=1, source_target_pairs={{0,56},{8,0},{16,8},{24,16},{32,24},{40,32},{48,40},{56,48},{1,57}... | collective-permute-start | bytes 221192 | tf_op jit(solution)/shard_map/ppermute | solution.py:545
  20.2 1.2 %collective-permute-start.4 = (bf16[24,512]{1,0:T(8,128)(2,1)S(1)}, bf16[24,512]{1,0:T(8,128)(2,1)S(1)}, u32[]{:S(2)}, u32[]{:S(2)}) collective-permute-start(bf16[24,512]{1,0:T(8,128)(2,1)S(1)} %get-tuple-element.41.a_ref), channel_id=1, source_target_pairs={{0,1},{1,0},{2,3},{3,2},{4,5},{5,4},{6,7},{7,6},{8,9},{9,8},{10,11... | collective-permute-start | bytes 73736 | tf_op jit(solution)/shard_map/ppermute | solution.py:550
  21.5 5.4 %collective-permute-start.7 = (bf16[24,512]{1,0:T(8,128)(2,1)S(1)}, bf16[24,512]{1,0:T(8,128)(2,1)S(1)}, u32[]{:S(2)}, u32[]{:S(2)}) collective-permute-start(bf16[24,512]{1,0:T(8,128)(2,1)S(1)} %shard_map.73.after_ref.a_ref), channel_id=1, source_target_pairs={{0,4},{2,6},{4,0},{6,2},{1,5},{3,7},{5,1},{7,3},{8,12},{10,14},{12... | collective-permute-start | bytes 73736 | tf_op jit(solution)/shard_map/ppermute | solution.py:550
  24.1 5.0 %collective-permute-start.6 = (bf16[24,512]{1,0:T(8,128)(2,1)S(1)}, bf16[24,512]{1,0:T(8,128)(2,1)S(1)}, u32[]{:S(2)}, u32[]{:S(2)}) collective-permute-start(bf16[24,512]{1,0:T(8,128)(2,1)S(1)} %shard_map.73.after_ref.a_ref), channel_id=1, source_target_pairs={{0,6},{2,4},{4,2},{6,0},{1,7},{3,5},{5,3},{7,1},{8,14},{10,12},{12... | collective-permute-start | bytes 73736 | tf_op jit(solution)/shard_map/ppermute | solution.py:550
  25.0 4.1 %collective-permute-start.5 = (bf16[24,512]{1,0:T(8,128)(2,1)S(1)}, bf16[24,512]{1,0:T(8,128)(2,1)S(1)}, u32[]{:S(2)}, u32[]{:S(2)}) collective-permute-start(bf16[24,512]{1,0:T(8,128)(2,1)S(1)} %shard_map.73.after_ref.a_ref), channel_id=1, source_target_pairs={{0,2},{2,0},{4,6},{6,4},{1,3},{3,1},{5,7},{7,5},{8,10},{10,8},{12,... | collective-permute-start | bytes 73736 | tf_op jit(solution)/shard_map/ppermute | solution.py:550
  29.1 5.4 %collective-permute-start.10 = (bf16[24,512]{1,0:T(8,128)(2,1)S(1)}, bf16[24,512]{1,0:T(8,128)(2,1)S(1)}, u32[]{:S(2)}, u32[]{:S(2)}) collective-permute-start(bf16[24,512]{1,0:T(8,128)(2,1)S(1)} %shard_map.75.after_ref.a_ref), channel_id=1, source_target_pairs={{0,32},{16,48},{32,0},{48,16},{1,33},{17,49},{33,1},{49,17},{2,34}... | collective-permute-start | bytes 73736 | tf_op jit(solution)/shard_map/ppermute | solution.py:550
  31.6 5.0 %collective-permute-start.9 = (bf16[24,512]{1,0:T(8,128)(2,1)S(1)}, bf16[24,512]{1,0:T(8,128)(2,1)S(1)}, u32[]{:S(2)}, u32[]{:S(2)}) collective-permute-start(bf16[24,512]{1,0:T(8,128)(2,1)S(1)} %shard_map.75.after_ref.a_ref), channel_id=1, source_target_pairs={{0,48},{16,32},{32,16},{48,0},{1,49},{17,33},{33,17},{49,1},{2,50}... | collective-permute-start | bytes 73736 | tf_op jit(solution)/shard_map/ppermute | solution.py:550
  32.8 3.9 %collective-permute-start.8 = (bf16[24,512]{1,0:T(8,128)(2,1)S(1)}, bf16[24,512]{1,0:T(8,128)(2,1)S(1)}, u32[]{:S(2)}, u32[]{:S(2)}) collective-permute-start(bf16[24,512]{1,0:T(8,128)(2,1)S(1)} %shard_map.75.after_ref.a_ref), channel_id=1, source_target_pairs={{0,16},{16,0},{32,48},{48,32},{1,17},{17,1},{33,49},{49,33},{2,18}... | collective-permute-start | bytes 73736 | tf_op jit(solution)/shard_map/ppermute | solution.py:550
  36.7 5.4 %collective-permute-start.13 = (bf16[24,512]{1,0:T(8,128)(2,1)S(1)}, bf16[24,512]{1,0:T(8,128)(2,1)S(1)}, u32[]{:S(2)}, u32[]{:S(2)}) collective-permute-start(bf16[24,512]{1,0:T(8,128)(2,1)S(1)} %shard_map.77.after_ref.a_ref), channel_id=1, source_target_pairs={{0,8},{8,0},{1,9},{9,1},{2,10},{10,2},{3,11},{11,3},{4,12},{12,4},... | collective-permute-start | bytes 73736 | tf_op jit(solution)/shard_map/ppermute | solution.py:550
  38.9 5.0 %collective-permute-start.12 = (bf16[24,512]{1,0:T(8,128)(2,1)S(1)}, bf16[24,512]{1,0:T(8,128)(2,1)S(1)}, u32[]{:S(2)}, u32[]{:S(2)}) collective-permute-start(bf16[24,512]{1,0:T(8,128)(2,1)S(1)} %shard_map.77.after_ref.a_ref), channel_id=1, source_target_pairs={{0,72},{8,64},{64,8},{72,0},{1,73},{9,65},{65,9},{73,1},{2,74},{10... | collective-permute-start | bytes 73736 | tf_op jit(solution)/shard_map/ppermute | solution.py:550
  40.4 3.8 %collective-permute-start.11 = (bf16[24,512]{1,0:T(8,128)(2,1)S(1)}, bf16[24,512]{1,0:T(8,128)(2,1)S(1)}, u32[]{:S(2)}, u32[]{:S(2)}) collective-permute-start(bf16[24,512]{1,0:T(8,128)(2,1)S(1)} %shard_map.77.after_ref.a_ref), channel_id=1, source_target_pairs={{0,64},{64,0},{1,65},{65,1},{2,66},{66,2},{3,67},{67,3},{4,68},{68... | collective-permute-start | bytes 73736 | tf_op jit(solution)/shard_map/ppermute | solution.py:550
